TPU v7x, 32 devices: a whole 2x2x4 slice. The times are simulated.
32 devices in a mesh: snap: 4 (over y, core), slab: 8 (over z, x).
Axes of the slice: x: 2, y: 2, z: 4, core: 2. Of those that a mesh axis runs over, the one named last changes fastest.
Arguments:
- velocity: bfloat16 [64, 3, 64, 16, 512], P('snap', None, 'slab'), may hold values from -6 to 6
- phase_bins: int32 [64], P('snap'), may hold values from 0 to 179, as said below
Outputs:
- coefficients: float32 [3, 3, 4, 64, 16, 512], P(None, None, None, 'slab', None, 'snap')
Inputs may be any that keep to these rules, and one draw needn't show every extreme that they name: `phase_bins`: no two snapshots share a bin, and the bins of all snapshots spread over the whole revolution.
All inputs are finite; a program needn't handle non-finite values.
Results may differ from a plain program's by a relative error of at most 0.0003.
Values may be sent and summed in bfloat16 or wider, within the bound.
No kernel may reach another device: no remote copies, remote signals or barrier semaphores. Data moves between devices by JAX's collectives and lax.ppermute only.
A program may use at most 128 MiB of HBM per device.

v0:
```python
import jax
import jax.numpy as jnp
from jax import lax
from jax.sharding import PartitionSpec as P

BINS = 180


inv_spacing = 0.75


def extended(array, sides, width):
    for axis, dim in sides:
        peers, length = (lax.axis_size(axis), array.shape[dim])
        up = [(i, (i + 1) % peers) for i in range(peers - 1)]
        down = [(j, i) for i, j in up]
        last = lax.slice_in_dim(array, length - width, length, axis=dim)
        initial = lax.slice_in_dim(array, 0, width, axis=dim)
        before = lax.ppermute(last, axis, up)
        after = lax.ppermute(initial, axis, down)
        array = jnp.concatenate([before, array, after], axis=dim)
    return array


def central(padded, direction):
    extent = padded.shape[-3:]
    leading = [slice(None)] * (padded.ndim - 3)

    def shifted(offset):
        window = [slice(2, extent[0] - 2), slice(2, extent[1] - 2), slice(2, extent[2] - 2)]
        window[direction] = slice(offset, extent[direction] - 4 + offset)
        return padded[tuple(leading + window)].astype(jnp.float32)

    return (8.0 * (shifted(3) - shifted(1)) - (shifted(4) - shifted(0))) * (inv_spacing / 12.0)


def vorticity_of(comp_u, comp_v, comp_w):
    omega_x = central(comp_w, 1) - central(comp_v, 2)
    omega_y = central(comp_u, 2) - central(comp_w, 0)
    omega_z = central(comp_v, 0) - central(comp_u, 1)
    return jnp.stack([omega_x, omega_y, omega_z], axis=-4)


def basis_weights(phase_bins):
    centers = (jnp.arange(BINS, dtype=jnp.float32) + 0.5) * (2.0 * jnp.pi / BINS)
    table = jnp.stack([jnp.ones_like(centers), jnp.cos(centers), jnp.sin(centers)], axis=1)
    onehot = (phase_bins[:, None] == jnp.arange(BINS, dtype=jnp.int32)[None, :]).astype(jnp.float32)
    return jnp.dot(onehot, table, precision=lax.Precision.HIGHEST)


def invert_three(gram):
    g00, g01, g02 = (gram[0, 0], gram[0, 1], gram[0, 2])
    g10, g11, g12 = (gram[1, 0], gram[1, 1], gram[1, 2])
    g20, g21, g22 = (gram[2, 0], gram[2, 1], gram[2, 2])
    c00 = g11 * g22 - g12 * g21
    c01 = g02 * g21 - g01 * g22
    c02 = g01 * g12 - g02 * g11
    c10 = g12 * g20 - g10 * g22
    c11 = g00 * g22 - g02 * g20
    c12 = g02 * g10 - g00 * g12
    c20 = g10 * g21 - g11 * g20
    c21 = g01 * g20 - g00 * g21
    c22 = g00 * g11 - g01 * g10
    determinant = g00 * c00 + g01 * c10 + g02 * c20
    adjugate = jnp.stack(
        [jnp.stack([c00, c01, c02]), jnp.stack([c10, c11, c12]), jnp.stack([c20, c21, c22])]
    )
    return adjugate / determinant


def weighted_powers(weights, comp_u, comp_v, comp_w):

    def accumulate(total, inputs):
        weight_row, field_u, field_v, field_w = inputs
        omega = vorticity_of(field_u, field_v, field_w)
        squared = omega * omega
        powers = jnp.stack([omega, squared, squared * omega, squared * squared], axis=1)
        return (total + weight_row[:, None, None, None, None, None] * powers[None], None)

    shape_out = (
        weights.shape[1],
        3,
        4,
        comp_u.shape[1] - 4,
        comp_u.shape[2] - 4,
        comp_u.shape[3] - 4,
    )
    start = jnp.zeros(shape_out, jnp.float32)
    sums, _ = lax.scan(accumulate, start, (weights, comp_u, comp_v, comp_w))
    return sums


def local(velocity, phase_bins):
    all_bins = lax.all_gather(phase_bins, "snap", axis=0, tiled=True)
    all_weights = basis_weights(all_bins)
    gram = jnp.dot(all_weights.T, all_weights, precision=lax.Precision.HIGHEST)
    inverse = invert_three(gram)
    own_weights = basis_weights(phase_bins)
    side_planes = extended(velocity[:, 1:3], (("slab", 2),), 2)
    comp_u = jnp.pad(velocity[:, 0], ((0, 0), (2, 2), (2, 2), (2, 2)))
    comp_v = jnp.pad(side_planes[:, 0], ((0, 0), (0, 0), (2, 2), (2, 2)))
    comp_w = jnp.pad(side_planes[:, 1], ((0, 0), (0, 0), (2, 2), (2, 2)))
    partial_sums = weighted_powers(own_weights, comp_u, comp_v, comp_w)
    sums = lax.psum_scatter(partial_sums, "snap", scatter_dimension=5, tiled=True)
    return jnp.einsum("ij,j...->i...", inverse, sums, precision=lax.Precision.HIGHEST)


def solution(mesh):
    in_specs = (P("snap", None, "slab", None, None), P("snap"))
    out_specs = P(None, None, None, "slab", None, "snap")
    return jax.shard_map(local, mesh=mesh, in_specs=in_specs, out_specs=out_specs, check_vma=False)
```

profile of v0, /device:TPU:16, one launch (start us, length us, event | category | flops | bytes accessed | tf_op | source)
XLA Modules:
  0.0 441.8 jit_solution(9490213758130660406)
XLA Ops:
  19.6 7.8 %pad.13 = bf16[16,12,20,516]{3,2,1,0:T(8,128)(2,1)} pad(bf16[16,8,16,512]{3,2,1,0:T(8,128)(2,1)} %slice_bitcast_fusion.2, bf16[]{:T(256)} %constant.26.clone.1), padding=0_0x2_2x2_2x2_2 | pad | bytes 6060034 | tf_op jit(solution)/shard_map/jit(_pad)/pad | solution.py:100
  27.6 30.4 %collective-permute-done = bf16[16,2,2,16,512]{4,3,2,0,1:T(8,128)(2,1)} collective-permute-done((bf16[16,2,2,16,512]{4,3,2,0,1:T(8,128)(2,1)}, bf16[16,2,2,16,512]{4,3,2,0,1:T(8,128)(2,1)}, u32[]{:S(2)}, u32[]{:S(2)}) %collective-permute-start) | collective-permute-done | bytes 1048608 | tf_op jit(solution)/shard_map/ppermute | solution.py:19
  62.9 7.3 %pad.12 = bf16[16,12,20,516]{3,2,1,0:T(8,128)(2,1)} pad(bf16[16,12,16,512]{3,2,1,0:T(8,128)(2,1)S(1)} %get-tuple-element.78, bf16[]{:T(256)} %constant.26.clone.1), padding=0_0x0_0x2_2x2_2 | pad | bytes 7108610 | tf_op jit(solution)/shard_map/jit(_pad)/pad | solution.py:101
  70.2 7.2 %pad.11 = bf16[16,12,20,516]{3,2,1,0:T(8,128)(2,1)} pad(bf16[16,12,16,512]{3,2,1,0:T(8,128)(2,1)S(1)} %get-tuple-element.79, bf16[]{:T(256)} %constant.26.clone.1), padding=0_0x0_0x2_2x2_2 | pad | bytes 7108610 | tf_op jit(solution)/shard_map/jit(_pad)/pad | solution.py:102
  77.5 267.3 %while.11 = (s32[]{:T(128)}, f32[3,3,4,8,16,512]{5,4,3,2,1,0:T(8,128)}, f32[16,3]{1,0:T(8,128)S(1)}, bf16[16,12,20,516]{3,2,1,0:T(8,128)(2,1)}, bf16[16,12,20,51...) while((s32[]{:T(128)}, ...), condition=%wide.region_1.2_spmd.clone, body=%wide.region_0.1_spmd.clone.sunk | while | flops 14548995 | bytes 113946064 | solution.py:89
  85.5 5.0 %select_add_fusion.2 = f32[3,3,4,8,16,512]{5,4,3,2,1,0:T(8,128)S(1)} fusion(f32[3,3,4,8,16,512]{5,4,3,2,1,0:T(8,128)S(1)} %copy-done, f32[3,4,8,16,512]{4,3,2,1,0:T(8,128)} %pad_maximum_fusion.6, f32[3]{0:T(128)S(1)} %fusion.29, pred[]{:T(512)S(6)} %compare.6), kind=kLoop, calls=%fused_computation.clone.1 | loop fusion | flops 7077888 | bytes 22020108 | tf_op jit(solution)/shard_map/while/body/eval_jaxpr/add | solution.py:78
  102.2 5.0 %select_add_fusion.2 = f32[3,3,4,8,16,512]{5,4,3,2,1,0:T(8,128)S(1)} fusion(f32[3,3,4,8,16,512]{5,4,3,2,1,0:T(8,128)S(1)} %copy-done, f32[3,4,8,16,512]{4,3,2,1,0:T(8,128)} %pad_maximum_fusion.6, f32[3]{0:T(128)S(1)} %fusion.29, pred[]{:T(512)S(6)} %compare.6), kind=kLoop, calls=%fused_computation.clone.1 | loop fusion | flops 7077888 | bytes 22020108 | tf_op jit(solution)/shard_map/while/body/eval_jaxpr/add | solution.py:78
  118.9 5.0 %select_add_fusion.2 = f32[3,3,4,8,16,512]{5,4,3,2,1,0:T(8,128)S(1)} fusion(f32[3,3,4,8,16,512]{5,4,3,2,1,0:T(8,128)S(1)} %copy-done, f32[3,4,8,16,512]{4,3,2,1,0:T(8,128)} %pad_maximum_fusion.6, f32[3]{0:T(128)S(1)} %fusion.29, pred[]{:T(512)S(6)} %compare.6), kind=kLoop, calls=%fused_computation.clone.1 | loop fusion | flops 7077888 | bytes 22020108 | tf_op jit(solution)/shard_map/while/body/eval_jaxpr/add | solution.py:78
  135.6 5.0 %select_add_fusion.2 = f32[3,3,4,8,16,512]{5,4,3,2,1,0:T(8,128)S(1)} fusion(f32[3,3,4,8,16,512]{5,4,3,2,1,0:T(8,128)S(1)} %copy-done, f32[3,4,8,16,512]{4,3,2,1,0:T(8,128)} %pad_maximum_fusion.6, f32[3]{0:T(128)S(1)} %fusion.29, pred[]{:T(512)S(6)} %compare.6), kind=kLoop, calls=%fused_computation.clone.1 | loop fusion | flops 7077888 | bytes 22020108 | tf_op jit(solution)/shard_map/while/body/eval_jaxpr/add | solution.py:78
  152.3 5.0 %select_add_fusion.2 = f32[3,3,4,8,16,512]{5,4,3,2,1,0:T(8,128)S(1)} fusion(f32[3,3,4,8,16,512]{5,4,3,2,1,0:T(8,128)S(1)} %copy-done, f32[3,4,8,16,512]{4,3,2,1,0:T(8,128)} %pad_maximum_fusion.6, f32[3]{0:T(128)S(1)} %fusion.29, pred[]{:T(512)S(6)} %compare.6), kind=kLoop, calls=%fused_computation.clone.1 | loop fusion | flops 7077888 | bytes 22020108 | tf_op jit(solution)/shard_map/while/body/eval_jaxpr/add | solution.py:78
  169.1 5.0 %select_add_fusion.2 = f32[3,3,4,8,16,512]{5,4,3,2,1,0:T(8,128)S(1)} fusion(f32[3,3,4,8,16,512]{5,4,3,2,1,0:T(8,128)S(1)} %copy-done, f32[3,4,8,16,512]{4,3,2,1,0:T(8,128)} %pad_maximum_fusion.6, f32[3]{0:T(128)S(1)} %fusion.29, pred[]{:T(512)S(6)} %compare.6), kind=kLoop, calls=%fused_computation.clone.1 | loop fusion | flops 7077888 | bytes 22020108 | tf_op jit(solution)/shard_map/while/body/eval_jaxpr/add | solution.py:78
  185.8 5.0 %select_add_fusion.2 = f32[3,3,4,8,16,512]{5,4,3,2,1,0:T(8,128)S(1)} fusion(f32[3,3,4,8,16,512]{5,4,3,2,1,0:T(8,128)S(1)} %copy-done, f32[3,4,8,16,512]{4,3,2,1,0:T(8,128)} %pad_maximum_fusion.6, f32[3]{0:T(128)S(1)} %fusion.29, pred[]{:T(512)S(6)} %compare.6), kind=kLoop, calls=%fused_computation.clone.1 | loop fusion | flops 7077888 | bytes 22020108 | tf_op jit(solution)/shard_map/while/body/eval_jaxpr/add | solution.py:78
  202.5 5.0 %select_add_fusion.2 = f32[3,3,4,8,16,512]{5,4,3,2,1,0:T(8,128)S(1)} fusion(f32[3,3,4,8,16,512]{5,4,3,2,1,0:T(8,128)S(1)} %copy-done, f32[3,4,8,16,512]{4,3,2,1,0:T(8,128)} %pad_maximum_fusion.6, f32[3]{0:T(128)S(1)} %fusion.29, pred[]{:T(512)S(6)} %compare.6), kind=kLoop, calls=%fused_computation.clone.1 | loop fusion | flops 7077888 | bytes 22020108 | tf_op jit(solution)/shard_map/while/body/eval_jaxpr/add | solution.py:78
  219.2 5.0 %select_add_fusion.2 = f32[3,3,4,8,16,512]{5,4,3,2,1,0:T(8,128)S(1)} fusion(f32[3,3,4,8,16,512]{5,4,3,2,1,0:T(8,128)S(1)} %copy-done, f32[3,4,8,16,512]{4,3,2,1,0:T(8,128)} %pad_maximum_fusion.6, f32[3]{0:T(128)S(1)} %fusion.29, pred[]{:T(512)S(6)} %compare.6), kind=kLoop, calls=%fused_computation.clone.1 | loop fusion | flops 7077888 | bytes 22020108 | tf_op jit(solution)/shard_map/while/body/eval_jaxpr/add | solution.py:78
  235.9 5.0 %select_add_fusion.2 = f32[3,3,4,8,16,512]{5,4,3,2,1,0:T(8,128)S(1)} fusion(f32[3,3,4,8,16,512]{5,4,3,2,1,0:T(8,128)S(1)} %copy-done, f32[3,4,8,16,512]{4,3,2,1,0:T(8,128)} %pad_maximum_fusion.6, f32[3]{0:T(128)S(1)} %fusion.29, pred[]{:T(512)S(6)} %compare.6), kind=kLoop, calls=%fused_computation.clone.1 | loop fusion | flops 7077888 | bytes 22020108 | tf_op jit(solution)/shard_map/while/body/eval_jaxpr/add | solution.py:78
  252.6 5.0 %select_add_fusion.2 = f32[3,3,4,8,16,512]{5,4,3,2,1,0:T(8,128)S(1)} fusion(f32[3,3,4,8,16,512]{5,4,3,2,1,0:T(8,128)S(1)} %copy-done, f32[3,4,8,16,512]{4,3,2,1,0:T(8,128)} %pad_maximum_fusion.6, f32[3]{0:T(128)S(1)} %fusion.29, pred[]{:T(512)S(6)} %compare.6), kind=kLoop, calls=%fused_computation.clone.1 | loop fusion | flops 7077888 | bytes 22020108 | tf_op jit(solution)/shard_map/while/body/eval_jaxpr/add | solution.py:78
  269.3 5.0 %select_add_fusion.2 = f32[3,3,4,8,16,512]{5,4,3,2,1,0:T(8,128)S(1)} fusion(f32[3,3,4,8,16,512]{5,4,3,2,1,0:T(8,128)S(1)} %copy-done, f32[3,4,8,16,512]{4,3,2,1,0:T(8,128)} %pad_maximum_fusion.6, f32[3]{0:T(128)S(1)} %fusion.29, pred[]{:T(512)S(6)} %compare.6), kind=kLoop, calls=%fused_computation.clone.1 | loop fusion | flops 7077888 | bytes 22020108 | tf_op jit(solution)/shard_map/while/body/eval_jaxpr/add | solution.py:78
  286.0 5.0 %select_add_fusion.2 = f32[3,3,4,8,16,512]{5,4,3,2,1,0:T(8,128)S(1)} fusion(f32[3,3,4,8,16,512]{5,4,3,2,1,0:T(8,128)S(1)} %copy-done, f32[3,4,8,16,512]{4,3,2,1,0:T(8,128)} %pad_maximum_fusion.6, f32[3]{0:T(128)S(1)} %fusion.29, pred[]{:T(512)S(6)} %compare.6), kind=kLoop, calls=%fused_computation.clone.1 | loop fusion | flops 7077888 | bytes 22020108 | tf_op jit(solution)/shard_map/while/body/eval_jaxpr/add | solution.py:78
  302.7 5.0 %select_add_fusion.2 = f32[3,3,4,8,16,512]{5,4,3,2,1,0:T(8,128)S(1)} fusion(f32[3,3,4,8,16,512]{5,4,3,2,1,0:T(8,128)S(1)} %copy-done, f32[3,4,8,16,512]{4,3,2,1,0:T(8,128)} %pad_maximum_fusion.6, f32[3]{0:T(128)S(1)} %fusion.29, pred[]{:T(512)S(6)} %compare.6), kind=kLoop, calls=%fused_computation.clone.1 | loop fusion | flops 7077888 | bytes 22020108 | tf_op jit(solution)/shard_map/while/body/eval_jaxpr/add | solution.py:78
  319.4 5.0 %select_add_fusion.2 = f32[3,3,4,8,16,512]{5,4,3,2,1,0:T(8,128)S(1)} fusion(f32[3,3,4,8,16,512]{5,4,3,2,1,0:T(8,128)S(1)} %copy-done, f32[3,4,8,16,512]{4,3,2,1,0:T(8,128)} %pad_maximum_fusion.6, f32[3]{0:T(128)S(1)} %fusion.29, pred[]{:T(512)S(6)} %compare.6), kind=kLoop, calls=%fused_computation.clone.1 | loop fusion | flops 7077888 | bytes 22020108 | tf_op jit(solution)/shard_map/while/body/eval_jaxpr/add | solution.py:78
  336.1 5.0 %select_add_fusion.2 = f32[3,3,4,8,16,512]{5,4,3,2,1,0:T(8,128)S(1)} fusion(f32[3,3,4,8,16,512]{5,4,3,2,1,0:T(8,128)S(1)} %copy-done, f32[3,4,8,16,512]{4,3,2,1,0:T(8,128)} %pad_maximum_fusion.6, f32[3]{0:T(128)S(1)} %fusion.29, pred[]{:T(512)S(6)} %compare.6), kind=kLoop, calls=%fused_computation.clone.1 | loop fusion | flops 7077888 | bytes 22020108 | tf_op jit(solution)/shard_map/while/body/eval_jaxpr/add | solution.py:78
  346.9 4.9 %all-reduce.3 = s32[64]{0:T(128)S(1)} all-reduce(s32[64]{0:T(128)S(1)} %dynamic-update-slice), channel_id=1, replica_groups=mesh['snap'=4,'slab'=8] {'snap'}, use_global_device_ids=true, to_apply=%add.3 | all-reduce | flops 64 | bytes 512
  378.3 46.1 %reduce-scatter.2.cloned.1.call-done = f32[3,3,4,8,16,128]{5,4,3,2,1,0:T(8,128)} async-done(((f32[3,3,4,8,16,512]{5,4,3,2,1,0:T(8,128)}), f32[3,3,4,8,16,128]{5,4,3,2,1,0:T(8,128)}) %reduce-scatter.2.cloned.1.call-update) | async-done | bytes 2359312 | tf_op jit(solution)/shard_map/reduce_scatter | solution.py:104
  424.4 8.8 %fusion.4 = f32[3,3,4,8,16,128]{5,0,4,3,2,1:T(4,128)S(1)} fusion(f32[3,3,4,8,16,128]{5,4,3,2,1,0:T(8,128)} %reduce-scatter.2.cloned.1.call-done, f32[1,3]{1,0:T(1,128)S(1)} %maximum_bitcast_fusion.3, f32[1,3]{1,0:T(1,128)S(1)} %maximum_bitcast_fusion.2, f32[1,3]{1,0:T(1,128)S(1)} %maximum_bitcast_fusion.1, f32[]{:T(128)S(6)} %add.39), kind=kOutput, calls=%fused_computation.18 | convolution fusion | flops 21233692 | bytes 4718632 | tf_op jit(solution)/shard_map/ij,j...->i.../dot_general | solution.py:105
  (228 shorter events, 209.4 us)
Async XLA Ops:
  6.5 417.9 %reduce-scatter.2.cloned.1.call-start = ((), (), s32[]{:S(2)}) async-start(), calls=%async_computation.1 | async-start | bytes 11796480 | tf_op jit(solution)/shard_map/reduce_scatter | solution.py:104
  9.4 48.6 %collective-permute-start = (bf16[16,2,2,16,512]{4,3,2,0,1:T(8,128)(2,1)}, bf16[16,2,2,16,512]{4,3,2,0,1:T(8,128)(2,1)}, u32[]{:S(2)}, u32[]{:S(2)}) collective-permute-start(bf16[16,2,2,16,512]{4,3,2,0,1:T(8,128)(2,1)} %copy.18), channel_id=1, source_target_pairs={{0,1},{1,2},{2,3},{3,4},{4,5},{5,6},{6,7},{8,9},{9,10},{10,11},{11... | collective-permute-start | bytes 3145736 | tf_op jit(solution)/shard_map/ppermute | solution.py:19
  12.9 14.5 %copy-start.2 = (s32[16]{0:T(128)S(1)}, s32[16]{0:T(128)}, u32[]{:S(2)}) copy-start(s32[16]{0:T(128)} %param.5) | copy-start | bytes 196
  12.9 47.5 %collective-permute-start.1 = (bf16[16,2,2,16,512]{4,3,2,0,1:T(8,128)(2,1)S(1)}, bf16[16,2,2,16,512]{4,3,2,0,1:T(8,128)(2,1)}, u32[]{:S(2)}, u32[]{:S(2)}) collective-permute-start(bf16[16,2,2,16,512]{4,3,2,0,1:T(8,128)(2,1)S(1)} %copy.20), channel_id=1, source_target_pairs={{1,0},{2,1},{3,2},{4,3},{5,4},{6,5},{7,6},{9,8},{10,9},{11,10},{12... | collective-permute-start | bytes 3145736 | tf_op jit(solution)/shard_map/ppermute | solution.py:20
  16.3 43.0 %slice-start = ((s8[6291456]{0:T(1024)(128)(4,1)}), s8[2097152]{0:T(1024)(128)(4,1)S(1)}, s32[]{:S(2)}) async-start(s8[6291456]{0:T(1024)(128)(4,1)} %bitcast.85), calls=%async_computation.2 | async-start | bytes 4194304
  19.6 39.7 %slice-start.1 = ((s8[6291456]{0:T(1024)(128)(4,1)}), s8[4194304]{0:T(1024)(128)(4,1)S(1)}, s32[]{:S(2)}) async-start(s8[6291456]{0:T(1024)(128)(4,1)} %bitcast.85), calls=%async_computation.3 | async-start | bytes 8388608
  80.7 4.8 %copy-start = (f32[3,3,4,8,16,512]{5,4,3,2,1,0:T(8,128)S(1)}, f32[3,3,4,8,16,512]{5,4,3,2,1,0:T(8,128)}, u32[]{:S(2)}) copy-start(f32[3,3,4,8,16,512]{5,4,3,2,1,0:T(8,128)} %get-tuple-element.153) | copy-start | bytes 28311556 | tf_op jit(solution)/shard_map/while
  90.5 3.7 copy-start.1
  97.4 4.8 %copy-start = (f32[3,3,4,8,16,512]{5,4,3,2,1,0:T(8,128)S(1)}, f32[3,3,4,8,16,512]{5,4,3,2,1,0:T(8,128)}, u32[]{:S(2)}) copy-start(f32[3,3,4,8,16,512]{5,4,3,2,1,0:T(8,128)} %get-tuple-element.153) | copy-start | bytes 28311556 | tf_op jit(solution)/shard_map/while
  107.2 3.7 copy-start.1
  114.1 4.8 %copy-start = (f32[3,3,4,8,16,512]{5,4,3,2,1,0:T(8,128)S(1)}, f32[3,3,4,8,16,512]{5,4,3,2,1,0:T(8,128)}, u32[]{:S(2)}) copy-start(f32[3,3,4,8,16,512]{5,4,3,2,1,0:T(8,128)} %get-tuple-element.153) | copy-start | bytes 28311556 | tf_op jit(solution)/shard_map/while
  130.8 4.8 %copy-start = (f32[3,3,4,8,16,512]{5,4,3,2,1,0:T(8,128)S(1)}, f32[3,3,4,8,16,512]{5,4,3,2,1,0:T(8,128)}, u32[]{:S(2)}) copy-start(f32[3,3,4,8,16,512]{5,4,3,2,1,0:T(8,128)} %get-tuple-element.153) | copy-start | bytes 28311556 | tf_op jit(solution)/shard_map/while
  147.5 4.8 %copy-start = (f32[3,3,4,8,16,512]{5,4,3,2,1,0:T(8,128)S(1)}, f32[3,3,4,8,16,512]{5,4,3,2,1,0:T(8,128)}, u32[]{:S(2)}) copy-start(f32[3,3,4,8,16,512]{5,4,3,2,1,0:T(8,128)} %get-tuple-element.153) | copy-start | bytes 28311556 | tf_op jit(solution)/shard_map/while
  164.2 4.8 %copy-start = (f32[3,3,4,8,16,512]{5,4,3,2,1,0:T(8,128)S(1)}, f32[3,3,4,8,16,512]{5,4,3,2,1,0:T(8,128)}, u32[]{:S(2)}) copy-start(f32[3,3,4,8,16,512]{5,4,3,2,1,0:T(8,128)} %get-tuple-element.153) | copy-start | bytes 28311556 | tf_op jit(solution)/shard_map/while
  180.9 4.8 %copy-start = (f32[3,3,4,8,16,512]{5,4,3,2,1,0:T(8,128)S(1)}, f32[3,3,4,8,16,512]{5,4,3,2,1,0:T(8,128)}, u32[]{:S(2)}) copy-start(f32[3,3,4,8,16,512]{5,4,3,2,1,0:T(8,128)} %get-tuple-element.153) | copy-start | bytes 28311556 | tf_op jit(solution)/shard_map/while
  197.6 4.8 %copy-start = (f32[3,3,4,8,16,512]{5,4,3,2,1,0:T(8,128)S(1)}, f32[3,3,4,8,16,512]{5,4,3,2,1,0:T(8,128)}, u32[]{:S(2)}) copy-start(f32[3,3,4,8,16,512]{5,4,3,2,1,0:T(8,128)} %get-tuple-element.153) | copy-start | bytes 28311556 | tf_op jit(solution)/shard_map/while
  214.4 4.8 %copy-start = (f32[3,3,4,8,16,512]{5,4,3,2,1,0:T(8,128)S(1)}, f32[3,3,4,8,16,512]{5,4,3,2,1,0:T(8,128)}, u32[]{:S(2)}) copy-start(f32[3,3,4,8,16,512]{5,4,3,2,1,0:T(8,128)} %get-tuple-element.153) | copy-start | bytes 28311556 | tf_op jit(solution)/shard_map/while
  231.1 4.8 %copy-start = (f32[3,3,4,8,16,512]{5,4,3,2,1,0:T(8,128)S(1)}, f32[3,3,4,8,16,512]{5,4,3,2,1,0:T(8,128)}, u32[]{:S(2)}) copy-start(f32[3,3,4,8,16,512]{5,4,3,2,1,0:T(8,128)} %get-tuple-element.153) | copy-start | bytes 28311556 | tf_op jit(solution)/shard_map/while
  247.8 4.8 %copy-start = (f32[3,3,4,8,16,512]{5,4,3,2,1,0:T(8,128)S(1)}, f32[3,3,4,8,16,512]{5,4,3,2,1,0:T(8,128)}, u32[]{:S(2)}) copy-start(f32[3,3,4,8,16,512]{5,4,3,2,1,0:T(8,128)} %get-tuple-element.153) | copy-start | bytes 28311556 | tf_op jit(solution)/shard_map/while
  264.5 4.8 %copy-start = (f32[3,3,4,8,16,512]{5,4,3,2,1,0:T(8,128)S(1)}, f32[3,3,4,8,16,512]{5,4,3,2,1,0:T(8,128)}, u32[]{:S(2)}) copy-start(f32[3,3,4,8,16,512]{5,4,3,2,1,0:T(8,128)} %get-tuple-element.153) | copy-start | bytes 28311556 | tf_op jit(solution)/shard_map/while
  281.2 4.8 %copy-start = (f32[3,3,4,8,16,512]{5,4,3,2,1,0:T(8,128)S(1)}, f32[3,3,4,8,16,512]{5,4,3,2,1,0:T(8,128)}, u32[]{:S(2)}) copy-start(f32[3,3,4,8,16,512]{5,4,3,2,1,0:T(8,128)} %get-tuple-element.153) | copy-start | bytes 28311556 | tf_op jit(solution)/shard_map/while
  297.9 4.8 %copy-start = (f32[3,3,4,8,16,512]{5,4,3,2,1,0:T(8,128)S(1)}, f32[3,3,4,8,16,512]{5,4,3,2,1,0:T(8,128)}, u32[]{:S(2)}) copy-start(f32[3,3,4,8,16,512]{5,4,3,2,1,0:T(8,128)} %get-tuple-element.153) | copy-start | bytes 28311556 | tf_op jit(solution)/shard_map/while
  314.6 4.8 %copy-start = (f32[3,3,4,8,16,512]{5,4,3,2,1,0:T(8,128)S(1)}, f32[3,3,4,8,16,512]{5,4,3,2,1,0:T(8,128)}, u32[]{:S(2)}) copy-start(f32[3,3,4,8,16,512]{5,4,3,2,1,0:T(8,128)} %get-tuple-element.153) | copy-start | bytes 28311556 | tf_op jit(solution)/shard_map/while
  331.3 4.8 %copy-start = (f32[3,3,4,8,16,512]{5,4,3,2,1,0:T(8,128)S(1)}, f32[3,3,4,8,16,512]{5,4,3,2,1,0:T(8,128)}, u32[]{:S(2)}) copy-start(f32[3,3,4,8,16,512]{5,4,3,2,1,0:T(8,128)} %get-tuple-element.153) | copy-start | bytes 28311556 | tf_op jit(solution)/shard_map/while
  (15 other events, 51.8 us)
Sparse Core Ops, SparseCore 0:
  344.9 79.4 reduce-scatter.1
where the time goes:
time: 446 us; the launch traced here: 442 us
  local copies, waits for them, and re-layouts  159 us (36%)
  other arithmetic  145 us (33%)
  waiting for transfers between devices  76.5 us (17%)
  between operations  39.3 us (9%)
  matrix products  9.46 us (2%)
  starting transfers between devices  6.73 us (2%)
  blocking collectives  4.93 us (1%)
    while x64, local copies, waits for them, and re-layouts  87 us
    add x16, other arithmetic, accumulate(): total + weight_row[:, None, None, None, None, None] * powers[None]  79.7 us
    reduce_scatter x1, waiting for transfers between devices, local(): lax.psum_scatter(partial_sums, 'snap', scatter_dimension=5, tiled=True)  46.1 us
    squeeze x32, local copies, waits for them, and re-layouts, weighted_powers(): sums, _ = lax.scan(accumulate, start, (weights, comp_u, comp_v, comp_w))  35 us
    another operation x32, other arithmetic, accumulate(): jnp.stack([omega, squared, squared * omega, squared * squared], axis=1)  34.2 us
    ppermute x1, waiting for transfers between devices, extended(): before = lax.ppermute(last, axis, up)  30.4 us
    sub x16, other arithmetic, vorticity_of(): omega_x = central(comp_w, 1) - central(comp_v, 2)  16.7 us
    sub x16, other arithmetic, vorticity_of(): omega_z = central(comp_v, 0) - central(comp_u, 1)  9.35 us
  transfers between devices with their start and end apart: 3, of which 2 were waited for; matrix products, arithmetic and copies ran while one was open for 4% of the time, Pallas kernels for 0%

commit v1 on v0

v1 whole, which is shorter than its diff:
```python
import functools

import jax
import jax.numpy as jnp
import numpy as np
from jax import lax
from jax.experimental import pallas as pl
from jax.experimental.pallas import tpu as pltpu
from jax.sharding import PartitionSpec as P

BINS = 180
ORDERS = 4
TAPS = ((-2, 1.0), (-1, -8.0), (1, 8.0), (2, -1.0))
STEP = 0.75 / 12.0
VMEM = 48 * 2**20


def band(size):
    matrix = np.zeros((size, size), np.float32)
    for offset, factor in TAPS:
        matrix += factor * np.eye(size, k=offset, dtype=np.float32)
    return matrix


def phase_table():
    centers = (jnp.arange(BINS, dtype=jnp.float32) + 0.5) * (2.0 * jnp.pi / BINS)
    return jnp.stack([jnp.ones_like(centers), jnp.cos(centers), jnp.sin(centers)], axis=1)


def basis_weights(phase_bins):
    onehot = (phase_bins[:, None] == jnp.arange(BINS, dtype=jnp.int32)[None, :]).astype(jnp.float32)
    return jnp.dot(onehot, phase_table(), precision=lax.Precision.HIGHEST)


def invert_three(gram):
    g00, g01, g02 = (gram[0, 0], gram[0, 1], gram[0, 2])
    g10, g11, g12 = (gram[1, 0], gram[1, 1], gram[1, 2])
    g20, g21, g22 = (gram[2, 0], gram[2, 1], gram[2, 2])
    c00 = g11 * g22 - g12 * g21
    c01 = g02 * g21 - g01 * g22
    c02 = g01 * g12 - g02 * g11
    c10 = g12 * g20 - g10 * g22
    c11 = g00 * g22 - g02 * g20
    c12 = g02 * g10 - g00 * g12
    c20 = g10 * g21 - g11 * g20
    c21 = g01 * g20 - g00 * g21
    c22 = g00 * g11 - g01 * g10
    determinant = g00 * c00 + g01 * c10 + g02 * c20
    adjugate = jnp.stack(
        [jnp.stack([c00, c01, c02]), jnp.stack([c10, c11, c12]), jnp.stack([c20, c21, c22])]
    )
    return adjugate / determinant


def spread_weights(bins, table, weight):
    for s in range(weight.shape[0]):
        row = bins[s] * 2
        weight[s, 0] = jnp.full((8, 128), table[row], jnp.float32)
        weight[s, 1] = jnp.full((8, 128), table[row + 1], jnp.float32)


def sum_powers(field, weight, lane, out, cell):
    snaps = weight.shape[0]
    rows = field.shape[0] // snaps
    for half in range(rows // 8):
        total = [None] * (3 * ORDERS)
        for s in range(snaps):
            first = field[pl.ds(s * rows + half * 8, 8), pl.ds(lane, 128)]
            second = first * first
            powers = (first, second, second * first, second * second)
            for j in range(3):
                for k in range(ORDERS):
                    term = powers[k] if j == 0 else powers[k] * weight[s, j - 1]
                    at = j * ORDERS + k
                    total[at] = term if s == 0 else total[at] + term
        for j in range(3):
            for k in range(ORDERS):
                out[cell, j, k, pl.ds(half * 8, 8), :] = total[j * ORDERS + k] * STEP ** (k + 1)


def sum_blocks(field, weight, place, outs, cell):
    for block, out in enumerate(outs):
        sum_powers(field, weight, pl.multiple_of(place[block] * 128, 128), out, cell)


def flat(block):
    return block.reshape(block.shape[0] * block.shape[1], block.shape[2])


def streamwise_kernel(bins, table, place, along_y, along_z, v, w, *refs):
    outs, (weight, field) = refs[:4], refs[4:]

    @pl.when(pl.program_id(0) == 0)
    def _():
        spread_weights(bins, table, weight)

    field[...] = jnp.dot(along_y[...], flat(w[:, 0, 0]), preferred_element_type=jnp.float32) - jnp.dot(
        flat(v[:, 0, 0]), along_z[...], preferred_element_type=jnp.float32
    )
    sum_blocks(field, weight, place, outs, 0)


def difference_x(planes, q, s):
    taps = [planes(s, q + offset).astype(jnp.float32) for offset in (0, 1, 3, 4)]
    return 8.0 * (taps[2] - taps[1]) - (taps[3] - taps[0])


def cross_fields(along_y, along_z, u, planes_v, planes_w, q, field_y, field_z, snaps, rows):
    field_y[...] = jnp.dot(u, along_z[...], preferred_element_type=jnp.float32)
    field_z[...] = jnp.dot(along_y[...], u, preferred_element_type=jnp.float32)
    for s in range(snaps):
        at = pl.ds(s * rows, rows)
        field_y[at, :] = field_y[at, :] - difference_x(planes_w, q, s)
        field_z[at, :] = difference_x(planes_v, q, s) - field_z[at, :]


def inner_kernel(bins, table, place, along_y, along_z, *refs):
    u, vs, ws, outs = refs[0], refs[1:5], refs[5:9], refs[9:13]
    weight, field_y, field_z = refs[13:]

    @pl.when(pl.program_id(0) == 0)
    def _():
        spread_weights(bins, table, weight)

    slot = {0: 0, 1: 1, 3: 2, 4: 3}
    cross_fields(
        along_y, along_z, flat(u[:, 0, 0]),
        lambda s, at: vs[slot[at]][s, 0, 0],
        lambda s, at: ws[slot[at]][s, 0, 0],
        0, field_y, field_z, u.shape[0], u.shape[3],
    )
    sum_blocks(field_y, weight, place, outs, 0)
    sum_blocks(field_z, weight, place, outs, 1)


def edge_kernel(bins, table, place, side, along_y, along_z, velocity, halo, *refs):
    outs = refs[:4]
    weight, field_y, field_z, center, cross, sems = refs[4:]
    q = pl.program_id(0)
    base, own, beyond = side[0], side[1], side[2]

    @pl.when(q == 0)
    def _():
        copies = [
            pltpu.make_async_copy(
                velocity.at[:, pl.ds(0, 1), pl.ds(base, 2)], center, sems.at[0]
            ),
            pltpu.make_async_copy(
                velocity.at[:, pl.ds(1, 2), pl.ds(own, 4)], cross.at[:, :, pl.ds(2 - beyond, 4)], sems.at[1]
            ),
            pltpu.make_async_copy(halo, cross.at[:, :, pl.ds(beyond * 2, 2)], sems.at[2]),
        ]
        for copy in copies:
            copy.start()
        spread_weights(bins, table, weight)
        for copy in copies:
            copy.wait()

    cross_fields(
        along_y, along_z, flat(center[:, 0, q]),
        lambda s, at: cross[s, 0, at],
        lambda s, at: cross[s, 1, at],
        q, field_y, field_z, center.shape[0], center.shape[3],
    )
    sum_blocks(field_y, weight, place, outs, 0)
    sum_blocks(field_z, weight, place, outs, 1)


def finish_kernel(cells, of, inverse, *refs):
    keep, core, across, out = refs[0], refs[1], refs[2], refs[-1]
    for k in range(ORDERS):
        sums = [keep[0, j, k] + core[0, j, k] + across[0, j, k] for j in range(3)]
        for i in range(3):
            out[i, 0, k, 0] = inverse[3 * i] * sums[0] + inverse[3 * i + 1] * sums[1] + inverse[3 * i + 2] * sums[2]


def smem():
    return pl.BlockSpec(memory_space=pltpu.SMEM)


def local(velocity, phase_bins):
    snaps, _, planes, rows, lanes = velocity.shape
    snap, slab = lax.axis_index("snap"), lax.axis_index("slab")
    n_snap, n_slab = lax.axis_size("snap"), lax.axis_size("slab")
    width = lanes // n_snap
    odd = lax.rem(slab, 2)

    pairs = [(i, i ^ 1) for i in range(n_slab)]
    others = [(i, i + 1) for i in range(1, n_slab - 1, 2)]
    others = others + [(j, i) for i, j in others]
    far = planes - 2

    def edge_planes(start):
        return lax.dynamic_slice(velocity, (0, 1, start, 0, 0), (snaps, 2, 2, rows, lanes))

    halo_near = lax.ppermute(edge_planes(jnp.where(odd == 0, far, 0)), "slab", pairs)
    halo_far = lax.ppermute(edge_planes(jnp.where(odd == 0, 0, far)), "slab", others)

    chip, core = lax.div(snap, 2), lax.rem(snap, 2)
    there, here = (1 - chip) * 2, chip * 2
    place = jnp.stack([there + core, here + core, there + 1 - core, here + 1 - core]).astype(jnp.int32)
    core_pairs = [(i, i ^ 1) for i in range(n_snap)]
    chip_pairs = [(i, (i + 2) % n_snap) for i in range(n_snap)]

    table = phase_table()[:, 1:].reshape(-1)
    along_y = jnp.asarray(np.kron(np.eye(snaps, dtype=np.float32), band(rows)), jnp.bfloat16)
    along_z = jnp.asarray(band(lanes).T, jnp.bfloat16)
    weight = pltpu.VMEM((snaps, 2, 8, 128), jnp.float32)
    field = pltpu.VMEM((snaps * rows, lanes), jnp.float32)
    constants = [
        pl.BlockSpec((snaps * rows, snaps * rows), lambda p: (0, 0)),
        pl.BlockSpec((lanes, lanes), lambda p: (0, 0)),
    ]

    def plane(component, offset):
        return pl.BlockSpec((snaps, 1, 1, rows, lanes), lambda p: (0, component, p + offset, 0, 0))

    def sums(steps, cells):
        shape = jax.ShapeDtypeStruct((steps * cells, 3, ORDERS, rows, width), jnp.float32)
        spec = pl.BlockSpec((cells, 3, ORDERS, rows, width), lambda p: (p, 0, 0, 0, 0))
        return {"out_shape": [shape] * 4, "out_specs": [spec] * 4, "grid": (steps,)}

    def params(cells):
        flops = cells * snaps * rows * lanes * 30
        return {
            "compiler_params": pltpu.CompilerParams(vmem_limit_bytes=VMEM),
            "cost_estimate": pl.CostEstimate(flops=flops, bytes_accessed=cells * 12 * rows * lanes * 4, transcendentals=0),
        }

    with jax.named_scope("streamwise"):
        first = pl.pallas_call(
            streamwise_kernel,
            in_specs=[smem(), smem(), smem(), *constants, plane(1, 0), plane(2, 0)],
            scratch_shapes=[weight, field],
            **sums(planes, 1), **params(planes),
        )(phase_bins, table, place, along_y, along_z, velocity, velocity)

    with jax.named_scope("inner"):
        inner = pl.pallas_call(
            inner_kernel,
            in_specs=[smem(), smem(), smem(), *constants, plane(0, 2)]
            + [plane(c, offset) for c in (1, 2) for offset in (0, 1, 3, 4)],
            scratch_shapes=[weight, field, field],
            **sums(planes - 4, 2), **params(2 * planes - 8),
        )(phase_bins, table, place, along_y, along_z, *[velocity] * 9)

    def edge(halo, high):
        side = jnp.stack([high * far, high * (planes - 4), high * 2]).astype(jnp.int32)
        return pl.pallas_call(
            edge_kernel,
            in_specs=[smem(), smem(), smem(), smem(), *constants]
            + [pl.BlockSpec(memory_space=pl.ANY)] * 2,
            scratch_shapes=[
                weight, field, field,
                pltpu.VMEM((snaps, 1, 2, rows, lanes), velocity.dtype),
                pltpu.VMEM((snaps, 2, 6, rows, lanes), velocity.dtype),
                pltpu.SemaphoreType.DMA((3,)),
            ],
            **sums(2, 2), **params(4),
        )(phase_bins, table, place, side, along_y, along_z, velocity, halo)

    with jax.named_scope("edge_near"):
        near = edge(halo_near, 1 - odd)
    with jax.named_scope("edge_far"):
        outer = edge(halo_far, odd)

    all_weights = basis_weights(lax.all_gather(phase_bins, "snap", axis=0, tiled=True))
    gram = jnp.dot(all_weights.T, all_weights, precision=lax.Precision.HIGHEST)
    inverse = invert_three(gram).reshape(-1)

    def exchange(parts):
        keep_there, keep_here, send_there, send_here = parts
        core_there = lax.ppermute(send_there, "snap", core_pairs)
        core_here = lax.ppermute(send_here, "snap", core_pairs)
        across = lax.ppermute(keep_there + core_there, "snap", chip_pairs)
        return keep_here, core_here, across

    out_shape = jax.ShapeDtypeStruct((3, 3, ORDERS, planes, rows, width), jnp.float32)

    def finish(parts, out, base, where):
        cells = parts[0].shape[0]
        cell = pl.BlockSpec((1, 3, ORDERS, rows, width), lambda p, base: (p, 0, 0, 0, 0))

        def target(p, base):
            component, at = where(p, base)
            return 0, component, 0, at, 0, 0

        def body(base, inverse, *refs):
            finish_kernel(cells, where, inverse, *refs)

        ops = [inverse, *parts] + ([] if out is None else [out])
        return pl.pallas_call(
            body,
            out_shape=out_shape,
            grid_spec=pltpu.PrefetchScalarGridSpec(
                num_scalar_prefetch=1,
                grid=(cells,),
                in_specs=[smem()] + [cell] * 3 + ([] if out is None else [pl.BlockSpec(memory_space=pl.ANY)]),
                out_specs=pl.BlockSpec((3, 1, ORDERS, 1, rows, width), target),
            ),
            input_output_aliases={} if out is None else {5: 0},
            compiler_params=pltpu.CompilerParams(vmem_limit_bytes=VMEM),
        )(base, *ops)

    def pair_of(p, base):
        return 1 + lax.rem(p, 2), base[0] + lax.div(p, 2)

    def base_of(value):
        return jnp.asarray(value, jnp.int32).reshape(1)

    out = finish(exchange(first), None, base_of(0), lambda p, base: (0, p))
    out = finish(exchange(inner), out, base_of(2), pair_of)
    out = finish(exchange(near), out, base_of((1 - odd) * far), pair_of)
    return finish(exchange(outer), out, base_of(odd * far), pair_of)


def solution(mesh):
    in_specs = (P("snap", None, "slab", None, None), P("snap"))
    out_specs = P(None, None, None, "slab", None, "snap")
    return jax.shard_map(local, mesh=mesh, in_specs=in_specs, out_specs=out_specs, check_vma=False)
```

time: 446 us -> 133 us (0.30)
  local copies, waits for them, and re-layouts: 159 us -> 12.6 us
  other arithmetic: 145 us -> 8.72 us
  waiting for transfers between devices: 76.5 us -> 22.7 us
  Pallas kernels: 0 us -> 44.2 us
  between operations: 39.3 us -> 25.2 us
  matrix products: 9.46 us -> 0.31 us
    while x64 -> x0, local copies, waits for them, and re-layouts: 87 us -> none
    add x16 -> x4, other arithmetic: 79.7 us -> 8.19 us  [exchange(): across = lax.ppermute(keep_there + core_there, 'snap', chip_pairs)]
    reduce_scatter x1 -> x0, waiting for transfers between devices: 46.1 us -> none  [local(): lax.psum_scatter(partial_sums, 'snap', scatter_dimension=5, tiled=True)]
    pallas_call x0 -> x8, Pallas kernels: none -> 44.2 us  [the longest x4 15.9 us: finish(): pl.pallas_call(body, out_shape=out_shape, grid_spec=pltpu.PrefetchScalarG...]
    squeeze x34 -> x0, local copies, waits for them, and re-layouts: 39.5 us -> none  [the longest x32 35 us: weighted_powers(): sums, _ = lax.scan(accumulate, start, (weights, comp_u, comp_v, comp_w))]
    another operation x32 -> x4, other arithmetic: 34.2 us -> 0.24 us  [the longest x2 0.15 us: edge(): jnp.stack([high * far, high * (planes - 4), high * 2]).astype(jnp.int32)]
    sub x32 -> x0, other arithmetic: 26 us -> none  [the longest x16 16.7 us: vorticity_of(): omega_x = central(comp_w, 1) - central(comp_v, 2)]
    pad x3 -> x0, local copies, waits for them, and re-layouts: 22.3 us -> none  [the longest x1 7.76 us: local(): comp_u = jnp.pad(velocity[:, 0], ((0, 0), (2, 2), (2, 2), (2, 2)))]
  transfers between devices with their start and end apart: 3 -> 14, of which waited for: 2 -> 2; matrix products, arithmetic and copies ran while one was open for 4% -> 9% of each run, Pallas kernels for 0% -> 32%
where the time goes in v1:
time: 133 us; the launch traced here: 131 us
  Pallas kernels  44.2 us (33%)
  between operations  25.2 us (19%)
  waiting for transfers between devices  22.7 us (17%)
  local copies, waits for them, and re-layouts  12.6 us (9%)
  starting transfers between devices  10.4 us (8%)
  other arithmetic  8.72 us (7%)
  blocking collectives  7.23 us (5%)
    ppermute x1, waiting for transfers between devices, local(): lax.ppermute(edge_planes(jnp.where(odd == 0, far, 0)), 'slab', pairs)  19.1 us
    pallas_call x4, Pallas kernels, finish(): pl.pallas_call(body, out_shape=out_shape, grid_spec=pltpu.PrefetchScalarG...  15.9 us
    pallas_call x2, Pallas kernels, edge(): pl.pallas_call(edge_kernel, in_specs=[smem(), smem(), smem(), smem(), *co...  11.2 us
    pallas_call x1, Pallas kernels, local(): pl.pallas_call(streamwise_kernel, in_specs=[smem(), smem(), smem(), *cons...  9.1 us
    unnamed x37, local copies, waits for them, and re-layouts  8.3 us
    add x4, other arithmetic, exchange(): across = lax.ppermute(keep_there + core_there, 'snap', chip_pairs)  8.19 us
    pallas_call x1, Pallas kernels, local(): pl.pallas_call(inner_kernel, in_specs=[smem(), smem(), smem(), *constants...  7.92 us
    unnamed x1, blocking collectives  7.23 us
  transfers between devices with their start and end apart: 14, of which 2 were waited for; matrix products, arithmetic and copies ran while one was open for 9% of the time, Pallas kernels for 32%

profile of v1, /device:TPU:16, one launch (start us, length us, event | category | flops | bytes accessed | tf_op | source)
XLA Modules:
  0.0 131.3 jit_solution(1553697720728897101)
XLA Ops:
  0.0 3.3 %constant_dynamic-slice_fusion = (bf16[16,2,2,16,512]{4,3,2,1,0:T(8,128)(2,1)}, bf16[16,2,2,16,512]{4,3,2,1,0:T(8,128)(2,1)}) fusion(bf16[16,3,8,16,512]{4,3,2,1,0:T(8,128)(2,1)} %w.1, s32[]{:T(128)S(6)} %select_n.10, s32[]{:T(128)S(6)} %select_n.9), kind=kLoop, calls=%fused_computation.19 | loop fusion | bytes 4194312 | tf_op jit(solution)/shard_map/dynamic_slice | solution.py:194
  3.3 1.5 %collective-permute-start.4 = (bf16[16,2,2,16,512]{4,3,2,1,0:T(8,128)(2,1)}, bf16[16,2,2,16,512]{4,3,2,1,0:T(8,128)(2,1)S(1)}, u32[]{:S(2)}, u32[]{:S(2)}) collective-permute-start(bf16[16,2,2,16,512]{4,3,2,1,0:T(8,128)(2,1)} %get-tuple-element.37), channel_id=1, source_target_pairs={{0,1},{1,0},{2,3},{3,2},{4,5},{5,4},{6,7},{7,6},{8,9},{9,8},{10,11... | collective-permute-start | bytes 3145736 | tf_op jit(solution)/shard_map/ppermute | solution.py:196
  4.8 2.3 %collective-permute-start = (bf16[16,2,2,16,512]{4,3,2,1,0:T(8,128)(2,1)}, bf16[16,2,2,16,512]{4,3,2,1,0:T(8,128)(2,1)S(1)}, u32[]{:S(2)}, u32[]{:S(2)}) collective-permute-start(bf16[16,2,2,16,512]{4,3,2,1,0:T(8,128)(2,1)} %get-tuple-element.38), channel_id=1, source_target_pairs={{1,2},{3,4},{5,6},{2,1},{4,3},{6,5},{9,10},{11,12},{13,14},{10,9},... | collective-permute-start | bytes 3145736 | tf_op jit(solution)/shard_map/ppermute | solution.py:197
  7.8 9.1 %streamwise.1 = (f32[8,3,4,16,128]{4,3,2,1,0:T(8,128)S(1)}, f32[8,3,4,16,128]{4,3,2,1,0:T(8,128)S(1)}, f32[8,3,4,16,128]{4,3,2,1,0:T(8,128)}, f32[8,3,4,16,128]{4,3,2,1,0:T(8,128)}) custom-call(s32[16]{0:T(128)S(1)} %copy-done.11, f32[360]{0:T(512)S(1)} %reshape.32.table, s32[4]{0:T(128)S(1)} %pad_add_fusion.place, bf16[256,256]{1,0:T(8,128)(2,1)S(1)} %copy-done.1, ...), custom_call_target="tpu_custom_call" | custom-call | flops 31457280 | bytes 3145728 | tf_op jit(solution)/shard_map/streamwise/pallas_call | solution.py:231
  17.8 7.9 %inner.1 = (f32[8,3,4,16,128]{4,3,2,1,0:T(8,128)S(1)}, f32[8,3,4,16,128]{4,3,2,1,0:T(8,128)S(1)}, f32[8,3,4,16,128]{4,3,2,1,0:T(8,128)}, f32[8,3,4,16,128]{4,3,2,1,0:T(8,128)S(1)}) custom-call(s32[16]{0:T(128)S(1)} %copy-done.11, f32[360]{0:T(512)S(1)} %reshape.32.table, s32[4]{0:T(128)S(1)} %pad_add_fusion.place, bf16[256,256]{1,0:T(8,128)(2,1)S(1)} %copy-done.1, ...), custom_call_target="tpu_custom_call" | custom-call | flops 31457280 | bytes 3145728 | tf_op jit(solution)/shard_map/inner/pallas_call | solution.py:239
  26.6 0.9 copy-done.5
  27.5 0.9 copy-done.12
  29.3 2.4 %add.63 = f32[8,3,4,16,128]{4,3,2,1,0:T(8,128)} add(f32[8,3,4,16,128]{4,3,2,1,0:T(8,128)} %copy-done.4, f32[8,3,4,16,128]{4,3,2,1,0:T(8,128)} %collective-permute-done.12) | non-fusion elementwise | flops 196608 | bytes 2359296 | tf_op jit(solution)/shard_map/add | solution.py:275
  31.7 19.1 %collective-permute-done.4.halo = bf16[16,2,2,16,512]{4,3,2,1,0:T(8,128)(2,1)S(1)} collective-permute-done((bf16[16,2,2,16,512]{4,3,2,1,0:T(8,128)(2,1)}, bf16[16,2,2,16,512]{4,3,2,1,0:T(8,128)(2,1)S(1)}, u32[]{:S(2)}, u32[]{:S(2)}) %collective-permute-start.4) | collective-permute-done | bytes 1048608 | tf_op jit(solution)/shard_map/ppermute | solution.py:196
  50.9 1.5 %collective-permute-start.13 = (f32[8,3,4,16,128]{4,3,2,1,0:T(8,128)}, f32[8,3,4,16,128]{4,3,2,1,0:T(8,128)}, u32[]{:S(2)}, u32[]{:S(2)}) collective-permute-start(f32[8,3,4,16,128]{4,3,2,1,0:T(8,128)} %add.63), channel_id=1, source_target_pairs={{0,16},{8,24},{16,0},{24,8},{1,17},{9,25},{17,1},{25,9},{2,18},{10... | collective-permute-start | bytes 2359304 | tf_op jit(solution)/shard_map/ppermute | solution.py:275
  52.5 5.5 %edge_near.1 = (f32[4,3,4,16,128]{4,3,2,1,0:T(8,128)S(1)}, f32[4,3,4,16,128]{4,3,2,1,0:T(8,128)S(1)}, f32[4,3,4,16,128]{4,3,2,1,0:T(8,128)}, f32[4,3,4,16,128]{4,3,2,1,0:T(8,128)S(1)}) custom-call(s32[16]{0:T(128)S(1)} %copy-done.11, f32[360]{0:T(512)S(1)} %reshape.32.table, s32[4]{0:T(128)S(1)} %pad_add_fusion.place, s32[3]{0:T(128)S(1)} %pad_add_fusion.2.side, ...), custom_call_target="tpu_custom_call" | custom-call | flops 15728640 | bytes 1572864 | tf_op jit(solution)/shard_map/edge_near/pallas_call | solution.py:249
  60.3 1.2 dynamic-slice
  62.4 7.2 %all-reduce = s32[64]{0:T(128)S(1)} all-reduce(s32[64]{0:T(128)S(1)} %dynamic-update-slice), channel_id=1, replica_groups=mesh['snap'=4,'slab'=8] {'snap'}, use_global_device_ids=true, to_apply=%add | all-reduce | flops 64 | bytes 512
  69.7 5.7 %edge_far.1 = (f32[4,3,4,16,128]{4,3,2,1,0:T(8,128)S(1)}, f32[4,3,4,16,128]{4,3,2,1,0:T(8,128)S(1)}, f32[4,3,4,16,128]{4,3,2,1,0:T(8,128)}, f32[4,3,4,16,128]{4,3,2,1,0:T(8,128)}) custom-call(s32[16]{0:T(128)S(1)} %copy-done.11, f32[360]{0:T(512)S(1)} %reshape.32.table, s32[4]{0:T(128)S(1)} %pad_add_fusion.place, s32[3]{0:T(128)S(1)} %pad_add_fusion.1.side, ...), custom_call_target="tpu_custom_call" | custom-call | flops 15728640 | bytes 1572864 | tf_op jit(solution)/shard_map/edge_far/pallas_call | solution.py:249
  75.7 2.2 %add.62 = f32[8,3,4,16,128]{4,3,2,1,0:T(8,128)} add(f32[8,3,4,16,128]{4,3,2,1,0:T(8,128)S(1)} %copy-done.3, f32[8,3,4,16,128]{4,3,2,1,0:T(8,128)} %collective-permute-done.9) | non-fusion elementwise | flops 196608 | bytes 2359296 | tf_op jit(solution)/shard_map/add | solution.py:275
  77.9 1.5 %collective-permute-start.10 = (f32[8,3,4,16,128]{4,3,2,1,0:T(8,128)}, f32[8,3,4,16,128]{4,3,2,1,0:T(8,128)S(1)}, u32[]{:S(2)}, u32[]{:S(2)}) collective-permute-start(f32[8,3,4,16,128]{4,3,2,1,0:T(8,128)} %add.62), channel_id=1, source_target_pairs={{0,16},{8,24},{16,0},{24,8},{1,17},{9,25},{17,1},{25,9},{2,18},{10... | collective-permute-start | bytes 2359304 | tf_op jit(solution)/shard_map/ppermute | solution.py:275
  104.6 1.8 %add.61 = f32[4,3,4,16,128]{4,3,2,1,0:T(8,128)} add(f32[4,3,4,16,128]{4,3,2,1,0:T(8,128)S(1)} %copy-done.10, f32[4,3,4,16,128]{4,3,2,1,0:T(8,128)} %collective-permute-done.6) | non-fusion elementwise | flops 98304 | bytes 1179648 | tf_op jit(solution)/shard_map/add | solution.py:275
  107.3 1.8 %add.60 = f32[4,3,4,16,128]{4,3,2,1,0:T(8,128)} add(f32[4,3,4,16,128]{4,3,2,1,0:T(8,128)S(1)} %get-tuple-element.23, f32[4,3,4,16,128]{4,3,2,1,0:T(8,128)} %copy-done.14) | non-fusion elementwise | flops 98304 | bytes 1179648 | tf_op jit(solution)/shard_map/add | solution.py:275
  110.0 1.5 %collective-permute-start.3 = (f32[4,3,4,16,128]{4,3,2,1,0:T(8,128)}, f32[4,3,4,16,128]{4,3,2,1,0:T(8,128)S(1)}, u32[]{:S(2)}, u32[]{:S(2)}) collective-permute-start(f32[4,3,4,16,128]{4,3,2,1,0:T(8,128)} %add.60), channel_id=1, source_target_pairs={{0,16},{8,24},{16,0},{24,8},{1,17},{9,25},{17,1},{25,9},{2,18},{10... | collective-permute-start | bytes 1179656 | tf_op jit(solution)/shard_map/ppermute | solution.py:275
  111.8 5.5 %shard_map.46.refs_3_ = f32[3,3,4,8,16,128]{5,4,3,2,1,0:T(8,128)} custom-call(s32[1]{0:T(128)} %constant.40.clone.1.base, f32[9]{0:T(128)S(1)} %div.25.inverse, f32[8,3,4,16,128]{4,3,2,1,0:T(8,128)S(1)} %get-tuple-element.33.refs_0_, f32[8,3,4,16,128]{4,3,2,1,0:T(8,128)} %collective-permute-done.11.refs_1_, f32[8,3,4,16,128]{4,3,2,1,0:T(8,128)} %collective-permute-done.13.refs_2_), custom_call_target="tpu_custom_call" | custom-call | tf_op jit(solution)/shard_map/pallas_call | solution.py:292
  117.3 5.3 %shard_map.47.refs_3_ = f32[3,3,4,8,16,128]{5,4,3,2,1,0:T(8,128)} custom-call(s32[1]{0:T(128)} %constant.39.clone.1.base, f32[9]{0:T(128)S(1)} %div.25.inverse, f32[8,3,4,16,128]{4,3,2,1,0:T(8,128)S(1)} %copy-done.6, f32[8,3,4,16,128]{4,3,2,1,0:T(8,128)} %collective-permute-done.8.refs_1_, ...), custom_call_target="tpu_custom_call", output_to_operand_aliasing={{}: (5, {})} | custom-call | tf_op jit(solution)/shard_map/pallas_call | solution.py:292
  122.6 3.2 %shard_map.48.refs_3_ = f32[3,3,4,8,16,128]{5,4,3,2,1,0:T(8,128)} custom-call(s32[1]{0:T(128)} %bitcast.29.base, f32[9]{0:T(128)S(1)} %div.25.inverse, f32[4,3,4,16,128]{4,3,2,1,0:T(8,128)S(1)} %copy-done.8, f32[4,3,4,16,128]{4,3,2,1,0:T(8,128)S(1)} %collective-permute-done.5.refs_1_, ...), custom_call_target="tpu_custom_call", output_to_operand_aliasing={{}: (5, {})} | custom-call | tf_op jit(solution)/shard_map/pallas_call | solution.py:292
  125.8 3.5 %collective-permute-done.3.refs_2_ = f32[4,3,4,16,128]{4,3,2,1,0:T(8,128)S(1)} collective-permute-done((f32[4,3,4,16,128]{4,3,2,1,0:T(8,128)}, f32[4,3,4,16,128]{4,3,2,1,0:T(8,128)S(1)}, u32[]{:S(2)}, u32[]{:S(2)}) %collective-permute-start.3) | collective-permute-done | bytes 393248 | tf_op jit(solution)/shard_map/ppermute | solution.py:275
  129.3 2.0 %shard_map.49 = f32[3,3,4,8,16,128]{5,4,3,2,1,0:T(8,128)} custom-call(s32[1]{0:T(128)} %bitcast.base, f32[9]{0:T(128)S(1)} %div.25.inverse, f32[4,3,4,16,128]{4,3,2,1,0:T(8,128)S(1)} %get-tuple-element.21.refs_0_, f32[4,3,4,16,128]{4,3,2,1,0:T(8,128)S(1)} %collective-permute-done.1.refs_1_, ...), custom_call_target="tpu_custom_call", output_to_operand_aliasing={{}: (5, {})} | custom-call | tf_op jit(solution)/shard_map/pallas_call | solution.py:292
  (71 shorter events, 9.2 us)
Async XLA Ops:
  0.0 7.8 %copy-start.1 = (bf16[256,256]{1,0:T(8,128)(2,1)S(1)}, bf16[256,256]{1,0:T(8,128)(2,1)}, u32[]{:S(2)}) copy-start(bf16[256,256]{1,0:T(8,128)(2,1)} %constant.41.clone.along_y) | copy-start | bytes 393220
  0.0 7.8 %copy-start = (bf16[512,512]{1,0:T(8,128)(2,1)S(1)}, bf16[512,512]{1,0:T(8,128)(2,1)}, u32[]{:S(2)}) copy-start(bf16[512,512]{1,0:T(8,128)(2,1)} %constant.42.clone.along_z) | copy-start | bytes 1572868
  0.0 7.8 %copy-start.11 = (s32[16]{0:T(128)S(1)}, s32[16]{0:T(128)}, u32[]{:S(2)}) copy-start(s32[16]{0:T(128)} %bins.7) | copy-start | bytes 196
  3.3 47.6 %collective-permute-start.4 = (bf16[16,2,2,16,512]{4,3,2,1,0:T(8,128)(2,1)}, bf16[16,2,2,16,512]{4,3,2,1,0:T(8,128)(2,1)S(1)}, u32[]{:S(2)}, u32[]{:S(2)}) collective-permute-start(bf16[16,2,2,16,512]{4,3,2,1,0:T(8,128)(2,1)} %get-tuple-element.37), channel_id=1, source_target_pairs={{0,1},{1,0},{2,3},{3,2},{4,5},{5,4},{6,7},{7,6},{8,9},{9,8},{10,11... | collective-permute-start | bytes 3145736 | tf_op jit(solution)/shard_map/ppermute | solution.py:196
  4.8 54.7 %collective-permute-start = (bf16[16,2,2,16,512]{4,3,2,1,0:T(8,128)(2,1)}, bf16[16,2,2,16,512]{4,3,2,1,0:T(8,128)(2,1)S(1)}, u32[]{:S(2)}, u32[]{:S(2)}) collective-permute-start(bf16[16,2,2,16,512]{4,3,2,1,0:T(8,128)(2,1)} %get-tuple-element.38), channel_id=1, source_target_pairs={{1,2},{3,4},{5,6},{2,1},{4,3},{6,5},{9,10},{11,12},{13,14},{10,9},... | collective-permute-start | bytes 3145736 | tf_op jit(solution)/shard_map/ppermute | solution.py:197
  17.8 11.1 %collective-permute-start.12 = (f32[8,3,4,16,128]{4,3,2,1,0:T(8,128)}, f32[8,3,4,16,128]{4,3,2,1,0:T(8,128)}, u32[]{:S(2)}, u32[]{:S(2)}) collective-permute-start(f32[8,3,4,16,128]{4,3,2,1,0:T(8,128)} %get-tuple-element.36), channel_id=1, source_target_pairs={{0,8},{8,0},{16,24},{24,16},{1,9},{9,1},{17,25},{25,17},{2,10},{10... | collective-permute-start | bytes 2359304 | tf_op jit(solution)/shard_map/ppermute | solution.py:273
  26.6 0.9 copy-start.5
  27.5 0.9 copy-start.12
  28.4 47.1 %collective-permute-start.9 = (f32[8,3,4,16,128]{4,3,2,1,0:T(8,128)}, f32[8,3,4,16,128]{4,3,2,1,0:T(8,128)}, u32[]{:S(2)}, u32[]{:S(2)}) collective-permute-start(f32[8,3,4,16,128]{4,3,2,1,0:T(8,128)} %get-tuple-element.32), channel_id=1, source_target_pairs={{0,8},{8,0},{16,24},{24,16},{1,9},{9,1},{17,25},{25,17},{2,10},{10... | collective-permute-start | bytes 2359304 | tf_op jit(solution)/shard_map/ppermute | solution.py:273
  28.8 80.3 %collective-permute-start.11 = (f32[8,3,4,16,128]{4,3,2,1,0:T(8,128)}, f32[8,3,4,16,128]{4,3,2,1,0:T(8,128)}, u32[]{:S(2)}, u32[]{:S(2)}) collective-permute-start(f32[8,3,4,16,128]{4,3,2,1,0:T(8,128)} %get-tuple-element.34), channel_id=1, source_target_pairs={{0,8},{8,0},{16,24},{24,16},{1,9},{9,1},{17,25},{25,17},{2,10},{10... | collective-permute-start | bytes 2359304 | tf_op jit(solution)/shard_map/ppermute | solution.py:274
  28.9 80.6 %collective-permute-start.8 = (f32[8,3,4,16,128]{4,3,2,1,0:T(8,128)}, f32[8,3,4,16,128]{4,3,2,1,0:T(8,128)}, u32[]{:S(2)}, u32[]{:S(2)}) collective-permute-start(f32[8,3,4,16,128]{4,3,2,1,0:T(8,128)} %copy-done.12), channel_id=1, source_target_pairs={{0,8},{8,0},{16,24},{24,16},{1,9},{9,1},{17,25},{25,17},{2,10},{10... | collective-permute-start | bytes 2359304 | tf_op jit(solution)/shard_map/ppermute | solution.py:274
  50.9 59.1 %collective-permute-start.13 = (f32[8,3,4,16,128]{4,3,2,1,0:T(8,128)}, f32[8,3,4,16,128]{4,3,2,1,0:T(8,128)}, u32[]{:S(2)}, u32[]{:S(2)}) collective-permute-start(f32[8,3,4,16,128]{4,3,2,1,0:T(8,128)} %add.63), channel_id=1, source_target_pairs={{0,16},{8,24},{16,0},{24,8},{1,17},{9,25},{17,1},{25,9},{2,18},{10... | collective-permute-start | bytes 2359304 | tf_op jit(solution)/shard_map/ppermute | solution.py:275
  60.3 17.6 %collective-permute-start.6 = (f32[4,3,4,16,128]{4,3,2,1,0:T(8,128)}, f32[4,3,4,16,128]{4,3,2,1,0:T(8,128)}, u32[]{:S(2)}, u32[]{:S(2)}) collective-permute-start(f32[4,3,4,16,128]{4,3,2,1,0:T(8,128)} %get-tuple-element.28), channel_id=1, source_target_pairs={{0,8},{8,0},{16,24},{24,16},{1,9},{9,1},{17,25},{25,17},{2,10},{10... | collective-permute-start | bytes 1179656 | tf_op jit(solution)/shard_map/ppermute | solution.py:273
  69.7 5.8 %copy-start.16 = (f32[180,1]{0,1:T(1,128)S(1)}, f32[180,1]{0,1:T(1,128)}, u32[]{:S(2)}) copy-start(f32[180,1]{0,1:T(1,128)} %copy-done.15) | copy-start | bytes 2164
  69.7 6.0 %copy-start.3 = (f32[8,3,4,16,128]{4,3,2,1,0:T(8,128)S(1)}, f32[8,3,4,16,128]{4,3,2,1,0:T(8,128)}, u32[]{:S(2)}) copy-start(f32[8,3,4,16,128]{4,3,2,1,0:T(8,128)} %copy-done.2) | copy-start | bytes 2359300
  75.4 29.1 %copy-start.10 = (f32[4,3,4,16,128]{4,3,2,1,0:T(8,128)S(1)}, f32[4,3,4,16,128]{4,3,2,1,0:T(8,128)}, u32[]{:S(2)}) copy-start(f32[4,3,4,16,128]{4,3,2,1,0:T(8,128)} %copy-done.9) | copy-start | bytes 1179652
  75.4 31.0 %collective-permute-start.2 = (f32[4,3,4,16,128]{4,3,2,1,0:T(8,128)}, f32[4,3,4,16,128]{4,3,2,1,0:T(8,128)S(1)}, u32[]{:S(2)}, u32[]{:S(2)}) collective-permute-start(f32[4,3,4,16,128]{4,3,2,1,0:T(8,128)} %get-tuple-element.24), channel_id=1, source_target_pairs={{0,8},{8,0},{16,24},{24,16},{1,9},{9,1},{17,25},{25,17},{2,10},{10... | collective-permute-start | bytes 1179656 | tf_op jit(solution)/shard_map/ppermute | solution.py:273
  77.9 39.4 %collective-permute-start.10 = (f32[8,3,4,16,128]{4,3,2,1,0:T(8,128)}, f32[8,3,4,16,128]{4,3,2,1,0:T(8,128)S(1)}, u32[]{:S(2)}, u32[]{:S(2)}) collective-permute-start(f32[8,3,4,16,128]{4,3,2,1,0:T(8,128)} %add.62), channel_id=1, source_target_pairs={{0,16},{8,24},{16,0},{24,8},{1,17},{9,25},{17,1},{25,9},{2,18},{10... | collective-permute-start | bytes 2359304 | tf_op jit(solution)/shard_map/ppermute | solution.py:275
  107.1 15.5 %collective-permute-start.5 = (f32[4,3,4,16,128]{4,3,2,1,0:T(8,128)}, f32[4,3,4,16,128]{4,3,2,1,0:T(8,128)S(1)}, u32[]{:S(2)}, u32[]{:S(2)}) collective-permute-start(f32[4,3,4,16,128]{4,3,2,1,0:T(8,128)} %copy-done.13), channel_id=1, source_target_pairs={{0,8},{8,0},{16,24},{24,16},{1,9},{9,1},{17,25},{25,17},{2,10},{10... | collective-permute-start | bytes 1179656 | tf_op jit(solution)/shard_map/ppermute | solution.py:274
  109.1 16.7 %collective-permute-start.1 = (f32[4,3,4,16,128]{4,3,2,1,0:T(8,128)}, f32[4,3,4,16,128]{4,3,2,1,0:T(8,128)S(1)}, u32[]{:S(2)}, u32[]{:S(2)}) collective-permute-start(f32[4,3,4,16,128]{4,3,2,1,0:T(8,128)} %get-tuple-element.22), channel_id=1, source_target_pairs={{0,8},{8,0},{16,24},{24,16},{1,9},{9,1},{17,25},{25,17},{2,10},{10... | collective-permute-start | bytes 1179656 | tf_op jit(solution)/shard_map/ppermute | solution.py:274
  109.4 13.1 %collective-permute-start.7 = (f32[4,3,4,16,128]{4,3,2,1,0:T(8,128)}, f32[4,3,4,16,128]{4,3,2,1,0:T(8,128)}, u32[]{:S(2)}, u32[]{:S(2)}) collective-permute-start(f32[4,3,4,16,128]{4,3,2,1,0:T(8,128)} %add.61), channel_id=1, source_target_pairs={{0,16},{8,24},{16,0},{24,8},{1,17},{9,25},{17,1},{25,9},{2,18},{10... | collective-permute-start | bytes 1179656 | tf_op jit(solution)/shard_map/ppermute | solution.py:275
  110.0 19.4 %collective-permute-start.3 = (f32[4,3,4,16,128]{4,3,2,1,0:T(8,128)}, f32[4,3,4,16,128]{4,3,2,1,0:T(8,128)S(1)}, u32[]{:S(2)}, u32[]{:S(2)}) collective-permute-start(f32[4,3,4,16,128]{4,3,2,1,0:T(8,128)} %add.60), channel_id=1, source_target_pairs={{0,16},{8,24},{16,0},{24,8},{1,17},{9,25},{17,1},{25,9},{2,18},{10... | collective-permute-start | bytes 1179656 | tf_op jit(solution)/shard_map/ppermute | solution.py:275
  111.8 5.5 %copy-start.6 = (f32[8,3,4,16,128]{4,3,2,1,0:T(8,128)S(1)}, f32[8,3,4,16,128]{4,3,2,1,0:T(8,128)}, u32[]{:S(2)}) copy-start(f32[8,3,4,16,128]{4,3,2,1,0:T(8,128)} %copy-done.5) | copy-start | bytes 2359300
  117.3 5.3 %copy-start.8 = (f32[4,3,4,16,128]{4,3,2,1,0:T(8,128)S(1)}, f32[4,3,4,16,128]{4,3,2,1,0:T(8,128)}, u32[]{:S(2)}) copy-start(f32[4,3,4,16,128]{4,3,2,1,0:T(8,128)} %copy-done.7) | copy-start | bytes 1179652
  (7 other events, 5.3 us)

commit v2 on v0

v2 whole, which is shorter than its diff:
```python
import jax
import jax.numpy as jnp
import numpy as np
from jax import lax
from jax.experimental import pallas as pl
from jax.experimental.pallas import tpu as pltpu
from jax.sharding import PartitionSpec as P

BINS = 180
ORDERS = 4
TAPS = ((-2, 1.0), (-1, -8.0), (1, 8.0), (2, -1.0))
STEP = 0.75 / 12.0
PARAMS = {
    "compiler_params": pltpu.CompilerParams(vmem_limit_bytes=60 * 2**20),
    "cost_estimate": pl.CostEstimate(flops=1, bytes_accessed=1, transcendentals=0),
}
LEVELS = 32766.0
TINY = 1e-30
BLOCKS, NEAR, FAR = 0, 3, 8
EDGE, OWN, OWN_AT, HALO_AT, EDGE_AT = range(5)


def band(size):
    matrix = np.zeros((size, size), np.float32)
    for offset, factor in TAPS:
        matrix += factor * np.eye(size, k=offset, dtype=np.float32)
    return matrix


def five_planes(width):
    matrix = np.zeros((5, width, width), np.float32)
    for offset, factor in TAPS:
        matrix[2 + offset] = factor * np.eye(width, dtype=np.float32)
    return matrix.reshape(5 * width, width)


def phase_table():
    centers = (np.arange(BINS, dtype=np.float32) + np.float32(0.5)) * np.float32(2.0 * np.pi / BINS)
    return np.stack([np.cos(centers), np.sin(centers)], axis=1).astype(np.float32)


def invert_kernel(bins, table, inverse):
    g00 = jnp.float32(bins.shape[0])
    g01 = g02 = g11 = g12 = g22 = jnp.float32(0.0)
    for s in range(bins.shape[0]):
        cosine, sine = table[bins[s] * 2], table[bins[s] * 2 + 1]
        g01, g02 = g01 + cosine, g02 + sine
        g11, g12, g22 = g11 + cosine * cosine, g12 + cosine * sine, g22 + sine * sine
    g00, g01, g02, g11, g12, g22 = (jnp.full(inverse.shape[1:], g, jnp.float32) for g in (g00, g01, g02, g11, g12, g22))
    c00 = g11 * g22 - g12 * g12
    c01 = g02 * g12 - g01 * g22
    c02 = g01 * g12 - g02 * g11
    c11 = g00 * g22 - g02 * g02
    c12 = g02 * g01 - g00 * g12
    c22 = g00 * g11 - g01 * g01
    determinant = g00 * c00 + g01 * c01 + g02 * c02
    for i, entry in enumerate((c00, c01, c02, c01, c11, c12, c02, c12, c22)):
        inverse[i] = entry / determinant


def spread_weights(bins, table, weight):
    for s in range(weight.shape[0]):
        row = bins[s] * 2
        weight[s, 0] = jnp.full((8, 128), table[row], jnp.float32)
        weight[s, 1] = jnp.full((8, 128), table[row + 1], jnp.float32)


def power_sums(field, weight, lane, rows, store):
    for half in range(rows // 8):
        total = [None] * (3 * ORDERS)
        for s in range(weight.shape[0]):
            first = field[pl.ds(s * rows + half * 8, 8), pl.ds(lane, 128)]
            second = first * first
            powers = (first, second, second * first, second * second)
            for j in range(3):
                for k in range(ORDERS):
                    term = powers[k] if j == 0 else powers[k] * weight[s, j - 1]
                    at = j * ORDERS + k
                    total[at] = term if s == 0 else total[at] + term
        scaled = [[total[j * ORDERS + k] * STEP ** (k + 1) for k in range(ORDERS)] for j in range(3)]
        store(pl.ds(half * 8, 8), scaled)


def pair_sums(field, weight, rows, there, here, cell):
    for lane, target in ((0, there), (128, here)):
        def store(at, sums, target=target):
            for j in range(3):
                for k in range(ORDERS):
                    target[k, j, cell, at, :] = sums[j][k]

        power_sums(field, weight, lane, rows, store)


def encode(sums, exponents, code, groups):
    cells, rows = sums.shape[2:4]
    exponents[...] = jnp.zeros(exponents.shape, jnp.float32)
    for n in range(ORDERS * 3):
        for g, (start, stop) in enumerate(groups):
            value = sums[n // 3, n % 3, start:stop]
            top = jnp.max(jnp.max(jnp.abs(value), axis=0), axis=0, keepdims=True)
            exponent = jnp.ceil(jnp.log(jnp.maximum(top, TINY)) * np.float32(1.0 / np.log(2.0)))
            rounded = jnp.round(value * (jnp.exp2(-exponent) * LEVELS))
            code[n * cells + start : n * cells + stop] = rounded.astype(jnp.int32).astype(jnp.int16)
            exponents[pl.ds(n * len(groups) + g, 1), :] = exponent
    last = exponents[...].reshape(exponents.shape[0] // rows, rows, exponents.shape[1])
    code[ORDERS * 3 * cells :] = last.astype(jnp.int32).astype(jnp.int16)


def decode_scales(code, scales):
    exponents = code.astype(jnp.int32).astype(jnp.float32)
    scales[...] = (jnp.exp2(exponents) * (1.0 / LEVELS)).reshape(scales.shape)


def flat(block):
    return block.reshape(block.shape[0] * block.shape[1], block.shape[2])


def product(a, b):
    return jnp.dot(a, b, preferred_element_type=jnp.float32)


def lanes_from(start, size):
    return pl.ds(pl.multiple_of(start, 128), size)


def block_of(where, b):
    return lanes_from(where[BLOCKS + b] * 128, 128)


def make_copies(pairs, sems):
    return [pltpu.make_async_copy(source, target, sems.at[i]) for i, (source, target) in enumerate(pairs)]


def run_copies(pairs, sems, meanwhile=lambda: None):
    copies = make_copies(pairs, sems)
    for copy in copies:
        copy.start()
    meanwhile()
    for copy in copies:
        copy.wait()


def both_along_y(along_y, block):
    return jnp.concatenate([product(along_y[...], flat(block[g])) for g in range(block.shape[0])], axis=0)


def rows_of(block):
    return block.reshape(-1, block.shape[-1])


def fill_x(field, along_y, along_z, v, w):
    field[...] = both_along_y(along_y, w) - product(rows_of(v), along_z[...])


def fill_y(field, along_x, along_z, u, w_planes):
    field[...] = product(rows_of(u), along_z[...]) - product(rows_of(w_planes), along_x[...])


def fill_z(field, along_x, along_y, u, v_planes):
    field[...] = product(rows_of(v_planes), along_x[...]) - both_along_y(along_y, u)


def inside_kernel(bins, table, where, along_x, along_y, along_z, own, other, code, here, there, exponents, weight, *refs):
    fields, (u_full, v_full, v_half, w_half, sems) = refs[:4], refs[4:]
    step = pl.program_id(0)
    planes, rows, pair = v_full.shape[1], v_full.shape[3], fields[0].shape[1]
    steps = planes // 2

    def of_plane(p):
        pairs = []
        for g, source in enumerate((own, other)):
            pairs.append((source.at[:, 1, p], v_full.at[g, p]))
            for b in range(2):
                lane = pl.ds(p * pair + b * 128, 128)
                pairs.append((source.at[:, 1, p, :, block_of(where, b)], v_half.at[g, :, :, lane]))
                pairs.append((source.at[:, 2, p, :, block_of(where, b)], w_half.at[g, :, :, lane]))
            if 2 <= p < planes - 2:
                pairs.append((source.at[:, 0, p], u_full.at[g, p - 2]))
        return make_copies(pairs, sems.at[p])

    def streamwise(field, p):
        fill_x(field, along_y, along_z, v_full[:, p], w_half[:, :, :, lanes_from(p * pair, pair)])

    @pl.when(step == 0)
    def _():
        for p in range(planes):
            for copy in of_plane(p):
                copy.start()
        spread_weights(bins, table, weight)
        for copy in of_plane(0):
            copy.wait()
        streamwise(fields[0], 0)

    for q in range(steps):
        @pl.when(step == q)
        def _(q=q):
            for p in range(1, planes - steps + 1) if q == 0 else (planes - steps + q,):
                for copy in of_plane(p):
                    copy.wait()

    five = lanes_from(step * pair, 5 * pair)
    streamwise(fields[1], 2 * step + 1)
    pair_sums(fields[0], weight, rows, there, here, 2 * step)
    fill_y(fields[2], along_x, along_z, u_full[:, step], w_half[:, :, :, five])
    pair_sums(fields[1], weight, rows, there, here, 2 * step + 1)
    halves = jnp.concatenate([u_full[:, step, :, :, block_of(where, b)] for b in range(2)], axis=-1)
    fill_z(fields[3], along_x, along_y, halves, v_half[:, :, :, five])
    pair_sums(fields[2], weight, rows, there, here, planes + step)
    streamwise(fields[0], jnp.minimum(2 * step + 2, planes - 1))
    pair_sums(fields[3], weight, rows, there, here, planes + steps + step)

    @pl.when(step == steps - 1)
    def _():
        encode(there, exponents, code, [(g * steps, g * steps + steps) for g in range(4)])


def edge_kernel(components, side, n_halos, halo_of, bins, table, where, along_x, along_y, along_z, own, other, *refs):
    count = len(components)
    halos, refs = refs[:n_halos], refs[n_halos:]
    code, here, there, exponents, weight = refs[:5]
    fields, crosses, (u_full, sems) = refs[5:7], refs[7 : 7 + count], refs[7 + count :]
    rows, pair = u_full.shape[3], fields[0].shape[1]
    pairs = []
    for g, source in enumerate((own, other)):
        for p in range(2):
            pairs.append((source.at[:, 0, where[side + EDGE] + p], u_full.at[g, p]))
        for c, cross in zip(components, crosses):
            for p in range(4):
                for b in range(2):
                    lane = lanes_from((where[side + OWN_AT] + p) * pair + b * 128, 128)
                    plane = source.at[:, c, where[side + OWN] + p, :, block_of(where, b)]
                    pairs.append((plane, cross.at[g, :, :, lane]))
            for p in range(2):
                lane = lanes_from((where[side + HALO_AT] + p) * pair, pair)
                pairs.append((halo_of(halos, g).at[:, c - components[0], p], cross.at[g, :, :, lane]))
    run_copies(pairs, sems, lambda: spread_weights(bins, table, weight))

    def fill(n):
        i, p = n // 2, n % 2
        planes = crosses[i][:, :, :, pl.ds(p * pair, 5 * pair)]
        if components[i] == 2:
            fill_y(fields[n % 2], along_x, along_z, u_full[:, p], planes)
        else:
            halves = jnp.concatenate([u_full[:, p, :, :, block_of(where, b)] for b in range(2)], axis=-1)
            fill_z(fields[n % 2], along_x, along_y, halves, planes)

    fill(0)
    for n in range(2 * count):
        if n + 1 < 2 * count:
            fill(n + 1)
        pair_sums(fields[n % 2], weight, rows, there, here, n)
    encode(there, exponents, code, [(2 * i, 2 * i + 2) for i in range(count)])


def solve(inverse, here, code, scales, cells, group, store):
    start, stop = cells
    count, groups = here.shape[0], scales.shape[0] // 3
    depth = here.shape[1]
    sums = []
    for j in range(count):
        coded = code[j * depth + start : j * depth + stop].astype(jnp.int32).astype(jnp.float32)
        sums.append(here[j, start:stop] + coded * scales[j * groups + group : j * groups + group + 1, :])
    for i in range(3):
        store(i, inverse[3 * i] * sums[0] + inverse[3 * i + 1] * sums[1] + inverse[3 * i + 2] * sums[2])


def finish_kernel(inverse, here, code, exponents, out, scales):
    planes = out.shape[3]
    half = planes // 2

    @pl.when(pl.program_id(0) == 0)
    def _():
        decode_scales(exponents[...], scales)

    rows = scales.shape[0] // ORDERS
    own = scales.at[pl.ds(pl.program_id(0) * rows, rows)]
    for group in range(4):
        cells = group * half, group * half + half

        def store(i, value, group=group):
            if group < 2:
                out[i, 0, 0, group * half : group * half + half] = value
            else:
                out[i, group - 1, 0, 2 : planes - 2] = value

        solve(inverse, here.at[0], code, own, cells, group, store)


def finish_edges_kernel(bins, table, where, inverse, along_x, along_y, own, other, across, diagonal, halo, *refs):
    near, far_y, refs = refs[:2], refs[2:4], refs[4:]
    _, out, near_out, far_out, near_scales, far_scales, weight, *fields, u_half, v_half, sems, out_sems = refs
    parts, _, _, rows, width = u_half.shape
    pairs = []
    for g in range(parts):
        for p in range(2):
            if g < 2:
                u = (own, other)[g].at[:, 0, where[FAR + EDGE] + p, :, block_of(where, 1)]
            else:
                u = (across, diagonal)[g - 2].at[:, 4 + p]
            pairs.append((u, u_half.at[g, p]))
            lane = lanes_from((where[FAR + HALO_AT] + p) * width, width)
            pairs.append((halo.at[g, :, p], v_half.at[g, :, :, lane]))
        for p in range(4):
            if g < 2:
                v = (own, other)[g].at[:, 1, where[FAR + OWN] + p, :, block_of(where, 1)]
            else:
                v = (across, diagonal)[g - 2].at[:, p]
            lane = lanes_from((where[FAR + OWN_AT] + p) * width, width)
            pairs.append((v, v_half.at[g, :, :, lane]))
    run_copies(pairs, sems, lambda: spread_weights(bins, table, weight))

    for p in range(2):
        fill_z(fields[p], along_x, along_y, u_half[:, p], v_half[:, :, :, pl.ds(p * width, 5 * width)])
    decode_scales(near[1][ORDERS * 12 :], near_scales)
    decode_scales(far_y[1][ORDERS * 6 :], far_scales)
    for k in range(ORDERS):
        for c in range(2):
            def store_near(i, value, c=c, k=k):
                near_out[i, c, k] = value

            cells, scales = (2 - 2 * c, 4 - 2 * c), near_scales.at[pl.ds(6 * k, 6)]
            solve(inverse, near[0].at[k], near[1].at[pl.ds(12 * k, 12)], scales, cells, 1 - c, store_near)

        def store_far(i, value, k=k):
            far_out[i, 0, k] = value

        scales = far_scales.at[pl.ds(3 * k, 3)]
        solve(inverse, far_y[0].at[k], far_y[1].at[pl.ds(6 * k, 6)], scales, (0, 2), 0, store_far)
    for p in range(2):
        def store_sums(at, sums, p=p):
            for k in range(ORDERS):
                for i in range(3):
                    far_out[i, 1, k, p, at, :] = (
                        inverse[3 * i, at] * sums[0][k]
                        + inverse[3 * i + 1, at] * sums[1][k]
                        + inverse[3 * i + 2, at] * sums[2][k]
                    )

        power_sums(fields[p], weight, 0, rows, store_sums)
    run_copies(
        [
            (near_out, out.at[:, pl.ds(1, 2), :, pl.ds(where[NEAR + EDGE], 2)]),
            (far_out, out.at[:, pl.ds(1, 2), :, pl.ds(where[FAR + EDGE], 2)]),
        ],
        out_sems,
    )


def pack_near_kernel(where, own, near, sems):
    planes = pl.ds(where[NEAR + EDGE], 2)
    run_copies(
        [
            (own.at[:, pl.ds(1, 2), planes, :, block_of(where, b)], near.at[:, :, :, :, pl.ds(b * 128, 128)])
            for b in range(2)
        ],
        sems,
    )


def pack_across_kernel(where, own, across, diagonal, sems):
    pairs = []
    for target, b in ((across, 0), (diagonal, 2)):
        lane = block_of(where, b)
        pairs.append((own.at[:, 1, pl.ds(where[FAR + OWN], 4), :, lane], target.at[:, pl.ds(0, 4)]))
        pairs.append((own.at[:, 0, pl.ds(where[FAR + EDGE], 2), :, lane], target.at[:, pl.ds(4, 2)]))
    run_copies(pairs, sems)


def pack_other_kernel(where, own, other, near, far, sems):
    pairs = []
    for b in range(2):
        source, target = block_of(where, b), pl.ds(b * 128, 128)
        planes = pl.ds(where[NEAR + EDGE], 2)
        pairs.append((other.at[:, pl.ds(1, 2), planes, :, source], near.at[:, :, :, :, target]))
        planes = pl.ds(where[FAR + EDGE], 2)
        for g, array in enumerate((own, other)):
            pairs.append((array.at[:, pl.ds(2, 1), planes, :, source], far.at[g, :, :, :, :, target]))
    run_copies(pairs, sems)


def pack_far_kernel(where, own, other, across, diagonal, far, sems):
    planes = pl.ds(where[FAR + EDGE], 2)
    pairs = [(array.at[:, 1, planes, :, block_of(where, 1)], far.at[g]) for g, array in enumerate((own, other))]
    planes = pl.ds(where[FAR + EDGE_AT], 2)
    pairs += [(array.at[:, planes], far.at[2 + g]) for g, array in enumerate((across, diagonal))]
    run_copies(pairs, sems)


def smem():
    return pl.BlockSpec(memory_space=pltpu.SMEM)


def hbm():
    return pl.BlockSpec(memory_space=pl.ANY)


def vmem():
    return pl.BlockSpec(memory_space=pltpu.VMEM)


def after(value, *others):
    return lax.optimization_barrier((value, *others))[0]


def local(velocity, phase_bins):
    snaps, _, planes, rows, lanes = velocity.shape
    kind = velocity.dtype
    snap, slab = lax.axis_index("snap"), lax.axis_index("slab")
    n_snap, n_slab = lax.axis_size("snap"), lax.axis_size("slab")
    width = lanes // n_snap
    pair, size = 2 * width, snaps * rows
    odd = lax.rem(slab, 2)

    near_pairs = [(i, i ^ 1) for i in range(n_slab)]
    far_pairs = [(i, i + 1) for i in range(1, n_slab - 1, 2)]
    far_pairs = far_pairs + [(j, i) for i, j in far_pairs]
    core_pairs = [(i, i ^ 1) for i in range(n_snap)]
    chip_pairs = [(i, (i + 2) % n_snap) for i in range(n_snap)]
    diagonal_pairs = [(i, ((i + 2) % n_snap) ^ 1) for i in range(n_snap)]

    chip, core = lax.div(snap, 2), lax.rem(snap, 2)
    there, here = (1 - chip) * 2, chip * 2
    entries = [there + core, here + core, there + 1 - core]
    for high in (1 - odd, odd):
        entries += [high * (planes - 2), high * (planes - 4), 2 - high * 2, high * 4, high * 2]
    where = jnp.stack([jnp.asarray(entry, jnp.int32) for entry in entries])

    def pack(kernel, arrays, shapes, copies):
        return pl.pallas_call(
            kernel,
            in_specs=[smem()] + [hbm()] * len(arrays),
            out_specs=[vmem()] * len(shapes),
            out_shape=[jax.ShapeDtypeStruct(shape, kind) for shape in shapes],
            scratch_shapes=[pltpu.SemaphoreType.DMA((copies,))],
            **PARAMS,
        )(where, *arrays)

    near_shape, far_shape = (snaps, 2, 2, rows, pair), (2, snaps, 1, 2, rows, pair)
    table = jnp.asarray(phase_table().reshape(-1))
    along_x = jnp.asarray(five_planes(pair), jnp.bfloat16)
    along_x_half = jnp.asarray(five_planes(width), jnp.bfloat16)
    along_y = jnp.asarray(np.kron(np.eye(snaps, dtype=np.float32), band(rows)), jnp.bfloat16)
    along_z = jnp.asarray(band(lanes).T, jnp.bfloat16)
    along_z = jnp.concatenate(
        [lax.dynamic_slice_in_dim(along_z, where[b] * width, width, axis=1) for b in range(2)], axis=1
    )
    weight = pltpu.VMEM((2 * snaps, 2, 8, 128), jnp.float32)
    field = pltpu.VMEM((2 * size, pair), jnp.float32)

    def sums(cells, groups):
        shape = (ORDERS, 3, cells, rows, width)
        last = -(-ORDERS * 3 * groups // rows)
        return {
            "in_specs": [smem()] * 3 + [vmem()] * 3 + [hbm()] * 2,
            "out_shape": [
                jax.ShapeDtypeStruct((ORDERS * 3 * cells + last, rows, width), jnp.int16),
                jax.ShapeDtypeStruct(shape, jnp.float32),
            ],
            "out_specs": [vmem()] * 2,
            **PARAMS,
        }, [pltpu.VMEM(shape, jnp.float32), pltpu.VMEM((last * rows, width), jnp.float32), weight]

    def inside_sums(bins):
        steps = planes // 2
        call, scratch = sums(2 * planes, 4)
        return pl.pallas_call(
            inside_kernel,
            grid=(steps,),
            scratch_shapes=[
                *scratch, field, field, field, field,
                pltpu.VMEM((2, steps, snaps, rows, lanes), kind),
                pltpu.VMEM((2, planes, snaps, rows, lanes), kind),
                pltpu.VMEM((2, snaps, rows, planes * pair), kind),
                pltpu.VMEM((2, snaps, rows, planes * pair), kind),
                pltpu.SemaphoreType.DMA((planes, 12)),
            ],
            **call,
        )(bins, table, where, along_x, along_y, along_z, velocity, other)

    def edge_sums(bins, components, side, halos, halo_of):
        count = len(components)

        def body(*refs):
            edge_kernel(components, side, len(halos), halo_of, *refs)

        call, scratch = sums(2 * count, count)
        call["in_specs"] = call["in_specs"] + [hbm()] * len(halos)
        return pl.pallas_call(
            body,
            scratch_shapes=[
                *scratch, field, field,
                *[pltpu.VMEM((2, snaps, rows, 6 * pair), kind)] * count,
                pltpu.VMEM((2, 2, snaps, rows, lanes), kind),
                pltpu.SemaphoreType.DMA((4 + 20 * count,)),
            ],
            **call,
        )(bins, table, where, along_x, along_y, along_z, velocity, other, *halos)

    def exchange(parts):
        code, here = parts
        return here, lax.ppermute(code, "snap", chip_pairs)

    other = lax.ppermute(velocity, "snap", core_pairs)
    pair_bins = jnp.concatenate([phase_bins, lax.ppermute(phase_bins, "snap", core_pairs)])
    with jax.named_scope("pack"):
        (near_own,) = pack(pack_near_kernel, (velocity,), [near_shape], 2)
        halo_own = lax.ppermute(near_own, "slab", near_pairs)
        for_across, for_diagonal = pack(
            pack_across_kernel, (after(velocity, near_own),), [(snaps, 6, rows, width)] * 2, 4
        )
        across = lax.ppermute(for_across, "snap", chip_pairs)
        diagonal = lax.ppermute(for_diagonal, "snap", diagonal_pairs)
        near_other, far_w = pack(
            pack_other_kernel, (velocity, after(other, for_across, for_diagonal)), [near_shape, far_shape], 6
        )
        halo_other = lax.ppermute(near_other, "slab", near_pairs)

    with jax.named_scope("inside"):
        inside_parts = inside_sums(after(pair_bins, near_other, far_w))
        inside = exchange(inside_parts)

    with jax.named_scope("pack"):
        (far_v,) = pack(
            pack_far_kernel, (velocity, after(other, inside_parts[0]), across, diagonal), [(4, snaps, 2, rows, width)], 4
        )
    halo_w = lax.ppermute(after(far_w, halo_other, halo_own, inside_parts[0]), "slab", far_pairs)
    halo_v = lax.ppermute(after(far_v, halo_other, halo_own), "slab", far_pairs)

    with jax.named_scope("edge_near"):
        near = exchange(edge_sums(pair_bins, (1, 2), NEAR, (halo_own, halo_other), lambda halos, g: halos[g]))
    with jax.named_scope("edge_far"):
        ready = after(pair_bins, inside[1])
        far_y = exchange(edge_sums(ready, (2,), FAR, (halo_w,), lambda halos, g: halos[0].at[g]))

    all_bins = jnp.concatenate([pair_bins, lax.ppermute(pair_bins, "snap", chip_pairs)])
    with jax.named_scope("invert"):
        inverse = pl.pallas_call(
            invert_kernel,
            in_specs=[smem(), smem()],
            out_shape=jax.ShapeDtypeStruct((9, rows, width), jnp.float32),
            **PARAMS,
        )(all_bins, table)

    out_shape = jax.ShapeDtypeStruct((3, 3, ORDERS, planes, rows, width), jnp.float32)

    last = 3
    with jax.named_scope("finish"):
        out = pl.pallas_call(
            finish_kernel,
            out_shape=out_shape,
            grid=(ORDERS,),
            in_specs=[
                pl.BlockSpec((9, rows, width), lambda p: (0, 0, 0)),
                pl.BlockSpec((1, 3, 2 * planes, rows, width), lambda p: (p, 0, 0, 0, 0)),
                pl.BlockSpec((6 * planes, rows, width), lambda p: (p, 0, 0)),
                pl.BlockSpec((last, rows, width), lambda p: (ORDERS * 6 * planes // last, 0, 0)),
            ],
            out_specs=pl.BlockSpec((3, 3, 1, planes, rows, width), lambda p: (0, 0, p, 0, 0, 0)),
            scratch_shapes=[pltpu.VMEM((last * rows, width), jnp.float32)],
            **PARAMS,
        )(inverse, *inside, inside[1])

    with jax.named_scope("finish_edges"):
        edges = pltpu.VMEM((3, 2, ORDERS, 2, rows, width), jnp.float32)
        return pl.pallas_call(
            finish_edges_kernel,
            out_shape=out_shape,
            in_specs=[smem()] * 3 + [vmem()] * 3 + [hbm()] * 5 + [vmem()] * 4 + [hbm()],
            out_specs=hbm(),
            scratch_shapes=[
                edges, edges,
                pltpu.VMEM((2 * rows, width), jnp.float32),
                pltpu.VMEM((rows, width), jnp.float32),
                pltpu.VMEM((4 * snaps, 2, 8, 128), jnp.float32),
                pltpu.VMEM((4 * size, width), jnp.float32),
                pltpu.VMEM((4 * size, width), jnp.float32),
                pltpu.VMEM((4, 2, snaps, rows, width), kind),
                pltpu.VMEM((4, snaps, rows, 6 * width), kind),
                pltpu.SemaphoreType.DMA((32,)),
                pltpu.SemaphoreType.DMA((2,)),
            ],
            input_output_aliases={15: 0},
            **PARAMS,
        )(
            all_bins, table, where, inverse, along_x_half, along_y, velocity, other, across, diagonal,
            after(halo_v, out), *near, *far_y, out,
        )


def solution(mesh):
    in_specs = (P("snap", None, "slab", None, None), P("snap"))
    out_specs = P(None, None, None, "slab", None, "snap")
    return jax.shard_map(local, mesh=mesh, in_specs=in_specs, out_specs=out_specs, check_vma=False)
```

time: 446 us -> 79.6 us (0.18)
  local copies, waits for them, and re-layouts: 159 us -> 3.93 us
  other arithmetic: 145 us -> 1.96 us
  waiting for transfers between devices: 76.5 us -> 0.9 us
  Pallas kernels: 0 us -> 54.7 us
  between operations: 39.3 us -> 0.37 us
  starting transfers between devices: 6.73 us -> 16.4 us
  matrix products: 9.46 us -> 0 us
  blocking collectives: 4.93 us -> 0 us
    while x64 -> x0, local copies, waits for them, and re-layouts: 87 us -> none
    add x16 -> x0, other arithmetic: 79.7 us -> none  [accumulate(): total + weight_row[:, None, None, None, None, None] * powers[None]]
    pallas_call x0 -> x10, Pallas kernels: none -> 54.7 us  [the longest x1 19 us: inside_sums(): pl.pallas_call(inside_kernel, grid=(steps,), scratch_shapes=[*scratch, fi...]
    reduce_scatter x1 -> x0, waiting for transfers between devices: 46.1 us -> none  [local(): lax.psum_scatter(partial_sums, 'snap', scatter_dimension=5, tiled=True)]
    squeeze x34 -> x0, local copies, waits for them, and re-layouts: 39.5 us -> none  [the longest x32 35 us: weighted_powers(): sums, _ = lax.scan(accumulate, start, (weights, comp_u, comp_v, comp_w))]
    another operation x35 -> x0, other arithmetic: 34.4 us -> none  [the longest x32 34.2 us: accumulate(): jnp.stack([omega, squared, squared * omega, squared * squared], axis=1)]
    ppermute x2 -> x12, waiting for transfers between devices: 30.4 us -> 0.9 us  [the longest x1 0.87 us: local(): other = lax.ppermute(velocity, 'snap', core_pairs)]
    sub x32 -> x0, other arithmetic: 26 us -> none  [the longest x16 16.7 us: vorticity_of(): omega_x = central(comp_w, 1) - central(comp_v, 2)]
  transfers between devices with their start and end apart: 3 -> 12, of which waited for: 2 -> 1; matrix products, arithmetic and copies ran while one was open for 4% -> 3% of each run, Pallas kernels for 0% -> 63%
where the time goes in v2:
time: 79.6 us; the launch traced here: 78.2 us
  Pallas kernels  54.7 us (69%)
  starting transfers between devices  16.4 us (21%)
  local copies, waits for them, and re-layouts  3.93 us (5%)
  other arithmetic  1.96 us (2%)
  waiting for transfers between devices  0.9 us (1%)
    pallas_call x1, Pallas kernels, inside_sums(): pl.pallas_call(inside_kernel, grid=(steps,), scratch_shapes=[*scratch, fi...  19 us
    pallas_call x2, Pallas kernels, edge_sums(): pl.pallas_call(body, scratch_shapes=[*scratch, field, field, *[pltpu.VMEM...  13.6 us
    pallas_call x4, Pallas kernels, pack(): pl.pallas_call(kernel, in_specs=[smem()] + [hbm()] * len(arrays), out_spe...  10.9 us
    pallas_call x1, Pallas kernels, local(): pl.pallas_call(finish_edges_kernel, out_shape=out_shape, in_specs=[smem()...  5.57 us
    ppermute x1, starting transfers between devices, local(): halo_v = lax.ppermute(after(far_v, halo_other, halo_own), 'slab', far_pairs)  4.59 us
    pallas_call x1, Pallas kernels, local(): pl.pallas_call(finish_kernel, out_shape=out_shape, grid=(ORDERS,), in_spe...  4.07 us
    unnamed x24, local copies, waits for them, and re-layouts  3.25 us
    ppermute x3, starting transfers between devices, exchange(): return (here, lax.ppermute(code, 'snap', chip_pairs))  2.71 us
  transfers between devices with their start and end apart: 12, of which 1 were waited for; matrix products, arithmetic and copies ran while one was open for 3% of the time, Pallas kernels for 63%

profile of v2, /device:TPU:16, one launch (start us, length us, event | category | flops | bytes accessed | tf_op | source)
XLA Modules:
  0.0 78.2 jit_solution(9292912415612158833)
XLA Ops:
  1.2 2.6 %pack.4 = bf16[16,2,2,16,256]{4,3,2,1,0:T(8,128)(2,1)} custom-call(s32[13]{0:T(128)} %stack.49.where.refs_2_, bf16[16,3,8,16,512]{4,3,2,1,0:T(8,128)(2,1)} %own.10), custom_call_target="tpu_custom_call" | custom-call | flops 1 | bytes 1 | tf_op jit(solution)/shard_map/pack/pallas_call | solution.py:429
  3.7 1.6 %collective-permute-start.6 = (bf16[16,2,2,16,256]{4,3,2,1,0:T(8,128)(2,1)}, bf16[16,2,2,16,256]{4,3,2,1,0:T(8,128)(2,1)S(1)}, u32[]{:S(2)}, u32[]{:S(2)}) collective-permute-start(bf16[16,2,2,16,256]{4,3,2,1,0:T(8,128)(2,1)} %pack.4), channel_id=1, source_target_pairs={{0,1},{1,0},{2,3},{3,2},{4,5},{5,4},{6,7},{7,6},{8,9},{9,8},{10,11... | collective-permute-start | bytes 1572872 | tf_op jit(solution)/shard_map/pack/ppermute | solution.py:507
  5.3 2.7 %pack.5 = (bf16[16,6,16,128]{3,2,1,0:T(8,128)(2,1)}, bf16[16,6,16,128]{3,2,1,0:T(8,128)(2,1)}) custom-call(s32[13]{0:T(128)} %stack.49.where.refs_2_, bf16[16,3,8,16,512]{4,3,2,1,0:T(8,128)(2,1)} %own.10), custom_call_target="tpu_custom_call" | custom-call | flops 1 | bytes 1 | tf_op jit(solution)/shard_map/pack/pallas_call | solution.py:429
  8.0 1.6 %collective-permute-start.3 = (bf16[16,6,16,128]{3,2,1,0:T(8,128)(2,1)}, bf16[16,6,16,128]{3,2,1,0:T(8,128)(2,1)S(1)}, u32[]{:S(2)}, u32[]{:S(2)}) collective-permute-start(bf16[16,6,16,128]{3,2,1,0:T(8,128)(2,1)} %get-tuple-element.24), channel_id=1, source_target_pairs={{0,16},{8,24},{16,0},{24,8},{1,17},{9,25},{17,1},{25,9},{2,18},{10... | collective-permute-start | bytes 1179656 | tf_op jit(solution)/shard_map/pack/ppermute | solution.py:511
  9.6 0.9 %collective-permute-done.2.other.refs_7_ = bf16[16,3,8,16,512]{4,3,2,1,0:T(8,128)(2,1)} collective-permute-done((bf16[16,3,8,16,512]{4,3,2,1,0:T(8,128)(2,1)}, bf16[16,3,8,16,512]{4,3,2,1,0:T(8,128)(2,1)}, u32[]{:S(2)}, u32[]{:S(2)}) %collective-permute-start.2) | collective-permute-done | bytes 6291488 | tf_op jit(solution)/shard_map/ppermute | solution.py:503
  10.5 3.0 %pack.6 = (bf16[16,2,2,16,256]{4,3,2,1,0:T(8,128)(2,1)}, bf16[2,16,1,2,16,256]{5,4,3,2,1,0:T(8,128)(2,1)}) custom-call(s32[13]{0:T(128)} %stack.49.where.refs_2_, bf16[16,3,8,16,512]{4,3,2,1,0:T(8,128)(2,1)} %own.10, bf16[16,3,8,16,512]{4,3,2,1,0:T(8,128)(2,1)} %collective-permute-done.2.other.refs_7_), custom_call_target="tpu_custom_call" | custom-call | flops 1 | bytes 1 | tf_op jit(solution)/shard_map/pack/pallas_call | solution.py:429
  13.5 1.6 %collective-permute-start.5 = (bf16[16,2,2,16,256]{4,3,2,1,0:T(8,128)(2,1)}, bf16[16,2,2,16,256]{4,3,2,1,0:T(8,128)(2,1)S(1)}, u32[]{:S(2)}, u32[]{:S(2)}) collective-permute-start(bf16[16,2,2,16,256]{4,3,2,1,0:T(8,128)(2,1)} %get-tuple-element.27), channel_id=1, source_target_pairs={{0,1},{1,0},{2,3},{3,2},{4,5},{5,4},{6,7},{7,6},{8,9},{9,8},{10,11... | collective-permute-start | bytes 1572872 | tf_op jit(solution)/shard_map/pack/ppermute | solution.py:516
  15.1 0.7 pad_maximum_fusion.along_z.refs_5_
  16.4 19.0 %inside.1 = (s16[195,16,128]{2,1,0:T(8,128)(2,1)}, f32[4,3,16,16,128]{4,3,2,1,0:T(8,128)}) custom-call(s32[32]{0:T(128)} %pad_add_fusion.bins.refs_0_, f32[360]{0:T(512)} %constant.38.clone.table.refs_1_, s32[13]{0:T(128)} %stack.49.where.refs_2_, bf16[1280,256]{1,0:T(8,128)(2,1)} %constant.39.clone.along_x.refs_3_, ...), custom_call_target="tpu_custom_call" | custom-call | flops 1 | bytes 1 | tf_op jit(solution)/shard_map/inside/pallas_call | solution.py:466
  35.4 1.6 %collective-permute-start.8 = (s16[195,16,128]{2,1,0:T(8,128)(2,1)}, s16[195,16,128]{2,1,0:T(8,128)(2,1)S(1)}, u32[]{:S(2)}, u32[]{:S(2)}) collective-permute-start(s16[195,16,128]{2,1,0:T(8,128)(2,1)} %get-tuple-element.30), channel_id=1, source_target_pairs={{0,16},{8,24},{16,0},{24,8},{1,17},{9,25},{17,1},{25,9},{2,18},{10... | collective-permute-start | bytes 2396168 | tf_op jit(solution)/shard_map/inside/ppermute | solution.py:501
  37.0 2.3 %collective-permute-start.10 = (bf16[2,16,1,2,16,256]{5,4,3,2,1,0:T(8,128)(2,1)}, bf16[2,16,1,2,16,256]{5,4,3,2,1,0:T(8,128)(2,1)S(1)}, u32[]{:S(2)}, u32[]{:S(2)}) collective-permute-start(bf16[2,16,1,2,16,256]{5,4,3,2,1,0:T(8,128)(2,1)} %get-tuple-element.38), channel_id=1, source_target_pairs={{1,2},{3,4},{5,6},{2,1},{4,3},{6,5},{9,10},{11,12},{13,14},{10,9},... | collective-permute-start | bytes 1572872 | tf_op jit(solution)/shard_map/ppermute | solution.py:526
  39.3 0.7 copy-done.1
  40.1 0.8 copy-done.2
  40.8 2.6 %pack.7 = bf16[4,16,2,16,128]{4,3,2,1,0:T(8,128)(2,1)} custom-call(s32[13]{0:T(128)} %stack.49.where.refs_2_, bf16[16,3,8,16,512]{4,3,2,1,0:T(8,128)(2,1)} %own.10, bf16[16,3,8,16,512]{4,3,2,1,0:T(8,128)(2,1)} %collective-permute-done.2.other.refs_7_, bf16[16,6,16,128]{3,2,1,0:T(8,128)(2,1)} %copy-done.1, bf16[16,6,16,128]{3,2,1,0:T(8,128)(2,1)} %copy-done.2), custom_call_target="tpu_custom_call" | custom-call | flops 1 | bytes 1 | tf_op jit(solution)/shard_map/pack/pallas_call | solution.py:429
  43.5 4.6 %collective-permute-start.7 = (bf16[4,16,2,16,128]{4,3,2,1,0:T(8,128)(2,1)}, bf16[4,16,2,16,128]{4,3,2,1,0:T(8,128)(2,1)S(1)}, u32[]{:S(2)}, u32[]{:S(2)}) collective-permute-start(bf16[4,16,2,16,128]{4,3,2,1,0:T(8,128)(2,1)} %pack.7), channel_id=1, source_target_pairs={{1,2},{3,4},{5,6},{2,1},{4,3},{6,5},{9,10},{11,12},{13,14},{10,9},... | collective-permute-start | bytes 1572872 | tf_op jit(solution)/shard_map/ppermute | solution.py:527
  48.1 7.8 %edge_near.1 = (s16[50,16,128]{2,1,0:T(8,128)(2,1)}, f32[4,3,4,16,128]{4,3,2,1,0:T(8,128)}) custom-call(s32[32]{0:T(128)} %pad_add_fusion.bins.refs_0_, f32[360]{0:T(512)} %constant.38.clone.table.refs_1_, s32[13]{0:T(128)} %stack.49.where.refs_2_, bf16[1280,256]{1,0:T(8,128)(2,1)} %constant.39.clone.along_x.refs_3_, ...), custom_call_target="tpu_custom_call" | custom-call | flops 1 | bytes 1 | tf_op jit(solution)/shard_map/edge_near/pallas_call | solution.py:488
  56.5 1.5 %collective-permute-start.1 = (s32[32]{0:T(128)S(1)}, s32[32]{0:T(128)S(1)}, u32[]{:S(2)}, u32[]{:S(2)}) collective-permute-start(s32[32]{0:T(128)S(1)} %copy-done.10), channel_id=1, source_target_pairs={{0,16},{8,24},{16,0},{24,8},{1,17},{9,25},{17,1},{25,9},{2,18},{10... | collective-permute-start | bytes 392 | tf_op jit(solution)/shard_map/ppermute | solution.py:535
  58.0 0.8 %copy-done.6 = bf16[2,16,1,2,16,256]{5,4,3,2,1,0:T(8,128)(2,1)} copy-done((bf16[2,16,1,2,16,256]{5,4,3,2,1,0:T(8,128)(2,1)}, bf16[2,16,1,2,16,256]{5,4,3,2,1,0:T(8,128)(2,1)S(1)}, u32[]{:S(2)}) %copy-start.6) | copy-done | bytes 524312
  58.9 5.8 %edge_far.1 = (s16[25,16,128]{2,1,0:T(8,128)(2,1)}, f32[4,3,2,16,128]{4,3,2,1,0:T(8,128)}) custom-call(s32[32]{0:T(128)} %pad_add_fusion.bins.refs_0_, f32[360]{0:T(512)} %constant.38.clone.table.refs_1_, s32[13]{0:T(128)} %stack.49.where.refs_2_, bf16[1280,256]{1,0:T(8,128)(2,1)} %constant.39.clone.along_x.refs_3_, ...), custom_call_target="tpu_custom_call" | custom-call | flops 1 | bytes 1 | tf_op jit(solution)/shard_map/edge_far/pallas_call | solution.py:488
  65.2 0.7 pad_add_fusion.1.bins
  65.9 1.6 %invert.1.inverse = f32[9,16,128]{2,1,0:T(8,128)} custom-call(s32[64]{0:T(128)} %pad_add_fusion.1.bins, f32[360]{0:T(512)} %constant.38.clone.table.refs_1_), custom_call_target="tpu_custom_call" | custom-call | flops 1 | bytes 1 | tf_op jit(solution)/shard_map/invert/pallas_call | solution.py:537
  67.5 4.1 %finish.1.refs_4_ = f32[3,3,4,8,16,128]{5,4,3,2,1,0:T(8,128)} custom-call(f32[9,16,128]{2,1,0:T(8,128)} %invert.1.inverse, f32[4,3,16,16,128]{4,3,2,1,0:T(8,128)} %get-tuple-element.33.here, s16[195,16,128]{2,1,0:T(8,128)(2,1)} %copy-done, s16[195,16,128]{2,1,0:T(8,128)(2,1)} %copy-done), custom_call_target="tpu_custom_call" | custom-call | flops 1 | bytes 1 | tf_op jit(solution)/shard_map/finish/pallas_call | solution.py:548
  71.6 0.8 %copy-done.4 = bf16[4,16,2,16,128]{4,3,2,1,0:T(8,128)(2,1)} copy-done((bf16[4,16,2,16,128]{4,3,2,1,0:T(8,128)(2,1)}, bf16[4,16,2,16,128]{4,3,2,1,0:T(8,128)(2,1)S(1)}, u32[]{:S(2)}) %copy-start.4) | copy-done | bytes 524312
  72.5 5.6 %finish_edges.1 = f32[3,3,4,8,16,128]{5,4,3,2,1,0:T(8,128)} custom-call(s32[64]{0:T(128)} %pad_add_fusion.1.bins, f32[360]{0:T(512)} %constant.38.clone.table.refs_1_, s32[13]{0:T(128)} %stack.49.where.refs_2_, f32[9,16,128]{2,1,0:T(8,128)} %invert.1.inverse, bf16[640,128]{1,0:T(8,128)(2,1)} %constant.40.clone.along_x, ...), custom_call_target="tpu_custom_call", output_to_operand_aliasing={{}: (15, {})} | custom-call | flops 1 | bytes 1 | tf_op jit(solution)/shard_map/finish_edges/pallas_call | solution.py:565
  (39 shorter events, 3.1 us)
Async XLA Ops:
  0.0 10.5 %collective-permute-start.2 = (bf16[16,3,8,16,512]{4,3,2,1,0:T(8,128)(2,1)}, bf16[16,3,8,16,512]{4,3,2,1,0:T(8,128)(2,1)}, u32[]{:S(2)}, u32[]{:S(2)}) collective-permute-start(bf16[16,3,8,16,512]{4,3,2,1,0:T(8,128)(2,1)} %own.10), channel_id=1, source_target_pairs={{0,8},{8,0},{16,24},{24,16},{1,9},{9,1},{17,25},{25,17},{2,10},{10... | collective-permute-start | bytes 18874376 | tf_op jit(solution)/shard_map/ppermute | solution.py:503
  0.6 15.1 %collective-permute-start = (s32[16]{0:T(128)}, s32[16]{0:T(128)S(1)}, u32[]{:S(2)}, u32[]{:S(2)}) collective-permute-start(s32[16]{0:T(128)} %param.8), channel_id=1, source_target_pairs={{0,8},{8,0},{16,24},{24,16},{1,9},{9,1},{17,25},{25,17},{2,10},{10... | collective-permute-start | bytes 200 | tf_op jit(solution)/shard_map/ppermute | solution.py:504
  3.7 33.2 %collective-permute-start.6 = (bf16[16,2,2,16,256]{4,3,2,1,0:T(8,128)(2,1)}, bf16[16,2,2,16,256]{4,3,2,1,0:T(8,128)(2,1)S(1)}, u32[]{:S(2)}, u32[]{:S(2)}) collective-permute-start(bf16[16,2,2,16,256]{4,3,2,1,0:T(8,128)(2,1)} %pack.4), channel_id=1, source_target_pairs={{0,1},{1,0},{2,3},{3,2},{4,5},{5,4},{6,7},{7,6},{8,9},{9,8},{10,11... | collective-permute-start | bytes 1572872 | tf_op jit(solution)/shard_map/pack/ppermute | solution.py:507
  8.0 31.3 %collective-permute-start.3 = (bf16[16,6,16,128]{3,2,1,0:T(8,128)(2,1)}, bf16[16,6,16,128]{3,2,1,0:T(8,128)(2,1)S(1)}, u32[]{:S(2)}, u32[]{:S(2)}) collective-permute-start(bf16[16,6,16,128]{3,2,1,0:T(8,128)(2,1)} %get-tuple-element.24), channel_id=1, source_target_pairs={{0,16},{8,24},{16,0},{24,8},{1,17},{9,25},{17,1},{25,9},{2,18},{10... | collective-permute-start | bytes 1179656 | tf_op jit(solution)/shard_map/pack/ppermute | solution.py:511
  9.6 29.7 %collective-permute-start.4 = (bf16[16,6,16,128]{3,2,1,0:T(8,128)(2,1)}, bf16[16,6,16,128]{3,2,1,0:T(8,128)(2,1)S(1)}, u32[]{:S(2)}, u32[]{:S(2)}) collective-permute-start(bf16[16,6,16,128]{3,2,1,0:T(8,128)(2,1)} %get-tuple-element.25), channel_id=1, source_target_pairs={{0,24},{8,16},{16,8},{24,0},{1,25},{9,17},{17,9},{25,1},{2,26},{10... | collective-permute-start | bytes 1179656 | tf_op jit(solution)/shard_map/pack/ppermute | solution.py:512
  9.6 5.4 %copy-start.8 = (bf16[512,512]{1,0:T(8,128)(2,1)S(1)}, bf16[512,512]{1,0:T(8,128)(2,1)}, u32[]{:S(2)}) copy-start(bf16[512,512]{1,0:T(8,128)(2,1)} %constant.42.clone) | copy-start | bytes 1572868
  9.6 6.2 %copy-start.11 = (s32[16]{0:T(128)S(1)}, s32[16]{0:T(128)}, u32[]{:S(2)}) copy-start(s32[16]{0:T(128)} %param.8) | copy-start | bytes 196
  13.5 23.5 %collective-permute-start.5 = (bf16[16,2,2,16,256]{4,3,2,1,0:T(8,128)(2,1)}, bf16[16,2,2,16,256]{4,3,2,1,0:T(8,128)(2,1)S(1)}, u32[]{:S(2)}, u32[]{:S(2)}) collective-permute-start(bf16[16,2,2,16,256]{4,3,2,1,0:T(8,128)(2,1)} %get-tuple-element.27), channel_id=1, source_target_pairs={{0,1},{1,0},{2,3},{3,2},{4,5},{5,4},{6,7},{7,6},{8,9},{9,8},{10,11... | collective-permute-start | bytes 1572872 | tf_op jit(solution)/shard_map/pack/ppermute | solution.py:516
  35.4 22.7 %collective-permute-start.8 = (s16[195,16,128]{2,1,0:T(8,128)(2,1)}, s16[195,16,128]{2,1,0:T(8,128)(2,1)S(1)}, u32[]{:S(2)}, u32[]{:S(2)}) collective-permute-start(s16[195,16,128]{2,1,0:T(8,128)(2,1)} %get-tuple-element.30), channel_id=1, source_target_pairs={{0,16},{8,24},{16,0},{24,8},{1,17},{9,25},{17,1},{25,9},{2,18},{10... | collective-permute-start | bytes 2396168 | tf_op jit(solution)/shard_map/inside/ppermute | solution.py:501
  37.0 11.1 %copy-start.3 = (bf16[16,2,2,16,256]{4,3,2,1,0:T(8,128)(2,1)}, bf16[16,2,2,16,256]{4,3,2,1,0:T(8,128)(2,1)S(1)}, u32[]{:S(2)}) copy-start(bf16[16,2,2,16,256]{4,3,2,1,0:T(8,128)(2,1)S(1)} %collective-permute-done.6.refs_8_) | copy-start | bytes 1572868
  37.0 11.1 %copy-start.5 = (bf16[16,2,2,16,256]{4,3,2,1,0:T(8,128)(2,1)}, bf16[16,2,2,16,256]{4,3,2,1,0:T(8,128)(2,1)S(1)}, u32[]{:S(2)}) copy-start(bf16[16,2,2,16,256]{4,3,2,1,0:T(8,128)(2,1)S(1)} %collective-permute-done.5.refs_9_) | copy-start | bytes 1572868
  37.0 21.1 %collective-permute-start.10 = (bf16[2,16,1,2,16,256]{5,4,3,2,1,0:T(8,128)(2,1)}, bf16[2,16,1,2,16,256]{5,4,3,2,1,0:T(8,128)(2,1)S(1)}, u32[]{:S(2)}, u32[]{:S(2)}) collective-permute-start(bf16[2,16,1,2,16,256]{5,4,3,2,1,0:T(8,128)(2,1)} %get-tuple-element.38), channel_id=1, source_target_pairs={{1,2},{3,4},{5,6},{2,1},{4,3},{6,5},{9,10},{11,12},{13,14},{10,9},... | collective-permute-start | bytes 1572872 | tf_op jit(solution)/shard_map/ppermute | solution.py:526
  39.3 0.8 copy-start.1
  40.1 0.8 copy-start.2
  43.5 13.0 %copy-start.10 = (s32[32]{0:T(128)S(1)}, s32[32]{0:T(128)}, u32[]{:S(2)}) copy-start(s32[32]{0:T(128)} %pad_add_fusion.bins.refs_0_) | copy-start | bytes 388
  43.5 28.1 %collective-permute-start.7 = (bf16[4,16,2,16,128]{4,3,2,1,0:T(8,128)(2,1)}, bf16[4,16,2,16,128]{4,3,2,1,0:T(8,128)(2,1)S(1)}, u32[]{:S(2)}, u32[]{:S(2)}) collective-permute-start(bf16[4,16,2,16,128]{4,3,2,1,0:T(8,128)(2,1)} %pack.7), channel_id=1, source_target_pairs={{1,2},{3,4},{5,6},{2,1},{4,3},{6,5},{9,10},{11,12},{13,14},{10,9},... | collective-permute-start | bytes 1572872 | tf_op jit(solution)/shard_map/ppermute | solution.py:527
  55.9 15.6 %collective-permute-start.9 = (s16[50,16,128]{2,1,0:T(8,128)(2,1)}, s16[50,16,128]{2,1,0:T(8,128)(2,1)S(1)}, u32[]{:S(2)}, u32[]{:S(2)}) collective-permute-start(s16[50,16,128]{2,1,0:T(8,128)(2,1)} %get-tuple-element.36), channel_id=1, source_target_pairs={{0,16},{8,24},{16,0},{24,8},{1,17},{9,25},{17,1},{25,9},{2,18},{10... | collective-permute-start | bytes 614408 | tf_op jit(solution)/shard_map/edge_near/ppermute | solution.py:501
  56.5 8.7 %collective-permute-start.1 = (s32[32]{0:T(128)S(1)}, s32[32]{0:T(128)S(1)}, u32[]{:S(2)}, u32[]{:S(2)}) collective-permute-start(s32[32]{0:T(128)S(1)} %copy-done.10), channel_id=1, source_target_pairs={{0,16},{8,24},{16,0},{24,8},{1,17},{9,25},{17,1},{25,9},{2,18},{10... | collective-permute-start | bytes 392 | tf_op jit(solution)/shard_map/ppermute | solution.py:535
  58.0 6.6 %copy-start = (s16[195,16,128]{2,1,0:T(8,128)(2,1)}, s16[195,16,128]{2,1,0:T(8,128)(2,1)S(1)}, u32[]{:S(2)}) copy-start(s16[195,16,128]{2,1,0:T(8,128)(2,1)S(1)} %collective-permute-done.8.code.exponents) | copy-start | bytes 2396164
  58.0 0.8 %copy-start.6 = (bf16[2,16,1,2,16,256]{5,4,3,2,1,0:T(8,128)(2,1)}, bf16[2,16,1,2,16,256]{5,4,3,2,1,0:T(8,128)(2,1)S(1)}, u32[]{:S(2)}) copy-start(bf16[2,16,1,2,16,256]{5,4,3,2,1,0:T(8,128)(2,1)S(1)} %collective-permute-done.10.refs_8_) | copy-start | bytes 1572868
  64.7 6.9 %collective-permute-start.11 = (s16[25,16,128]{2,1,0:T(8,128)(2,1)}, s16[25,16,128]{2,1,0:T(8,128)(2,1)S(1)}, u32[]{:S(2)}, u32[]{:S(2)}) collective-permute-start(s16[25,16,128]{2,1,0:T(8,128)(2,1)} %get-tuple-element.40), channel_id=1, source_target_pairs={{0,16},{8,24},{16,0},{24,8},{1,17},{9,25},{17,1},{25,9},{2,18},{10... | collective-permute-start | bytes 307208 | tf_op jit(solution)/shard_map/edge_far/ppermute | solution.py:501
  71.5 0.8 %copy-start.4 = (bf16[4,16,2,16,128]{4,3,2,1,0:T(8,128)(2,1)}, bf16[4,16,2,16,128]{4,3,2,1,0:T(8,128)(2,1)S(1)}, u32[]{:S(2)}) copy-start(bf16[4,16,2,16,128]{4,3,2,1,0:T(8,128)(2,1)S(1)} %collective-permute-done.7.halo) | copy-start | bytes 1572868
  71.5 0.9 %copy-start.7 = (s16[50,16,128]{2,1,0:T(8,128)(2,1)}, s16[50,16,128]{2,1,0:T(8,128)(2,1)S(1)}, u32[]{:S(2)}) copy-start(s16[50,16,128]{2,1,0:T(8,128)(2,1)S(1)} %collective-permute-done.9.refs_1_) | copy-start | bytes 614404
  71.6 0.9 %copy-start.9 = (s16[25,16,128]{2,1,0:T(8,128)(2,1)}, s16[25,16,128]{2,1,0:T(8,128)(2,1)S(1)}, u32[]{:S(2)}) copy-start(s16[25,16,128]{2,1,0:T(8,128)(2,1)S(1)} %collective-permute-done.11.refs_3_) | copy-start | bytes 307204

commit v3 on v2

v3 whole, which is shorter than its diff:
```python
import jax
import jax.numpy as jnp
import numpy as np
from jax import lax
from jax.experimental import pallas as pl
from jax.experimental.pallas import tpu as pltpu
from jax.sharding import PartitionSpec as P

BINS = 180
ORDERS = 4
TAPS = ((-2, 1.0), (-1, -8.0), (1, 8.0), (2, -1.0))
STEP = 0.75 / 12.0
LEVELS = 32766.0
TINY = 1e-30


def band(size):
    matrix = np.zeros((size, size), np.float32)
    for offset, factor in TAPS:
        matrix += factor * np.eye(size, k=offset, dtype=np.float32)
    return matrix


def four_planes(width):
    return np.concatenate([factor * np.eye(width, dtype=np.float32) for _, factor in TAPS])


def phase_table():
    centers = (np.arange(BINS, dtype=np.float32) + np.float32(0.5)) * np.float32(2.0 * np.pi / BINS)
    return np.stack([np.cos(centers), np.sin(centers)], axis=1).astype(np.float32)


def weights_kernel(bins, table, weight):
    for s in range(bins.shape[0]):
        weight[s, 0] = jnp.full(weight.shape[2:], table[bins[s] * 2], jnp.float32)
        weight[s, 1] = jnp.full(weight.shape[2:], table[bins[s] * 2 + 1], jnp.float32)


def invert_kernel(weight, inverse):
    g01 = g02 = g11 = g12 = g22 = jnp.zeros(weight.shape[2:], jnp.float32)
    for s in range(weight.shape[0]):
        cosine, sine = weight[s, 0], weight[s, 1]
        g01, g02 = g01 + cosine, g02 + sine
        g11, g12, g22 = g11 + cosine * cosine, g12 + cosine * sine, g22 + sine * sine
    g00 = jnp.full(weight.shape[2:], weight.shape[0], jnp.float32)
    c00 = g11 * g22 - g12 * g12
    c01 = g02 * g12 - g01 * g22
    c02 = g01 * g12 - g02 * g11
    c11 = g00 * g22 - g02 * g02
    c12 = g02 * g01 - g00 * g12
    c22 = g00 * g11 - g01 * g01
    determinant = g00 * c00 + g01 * c01 + g02 * c02
    for i, entry in enumerate((c00, c01, c02, c01, c11, c12, c02, c12, c22)):
        for half in range(inverse.shape[1] // 8):
            inverse[i, pl.ds(half * 8, 8)] = entry / determinant


class Spot:
    def __init__(self, planes):
        snap, odd = lax.axis_index("snap"), lax.rem(lax.axis_index("slab"), 2)
        chip, core = lax.div(snap, 2), lax.rem(snap, 2)
        there, here = (1 - chip) * 2, chip * 2
        self.there, self.here, self.diagonal = there + core, here + core, there + 1 - core
        self.near, self.far = Side(planes, 1 - odd), Side(planes, odd)

    def lanes(self, block):
        return lanes_from(block * 128, 128)

    def pair(self):
        return self.lanes(self.there), self.lanes(self.here)


class Side:
    def __init__(self, planes, high):
        self.high = high == 1
        self.edge, self.own, self.own_at = high * (planes - 2), high * (planes - 4), 2 - high * 2
        self.halo_at, self.edge_at = high * 4, high * 2

    def around(self, p, own, halo):
        planes = []
        for offset, _ in TAPS:
            at = p + 2 + offset
            if at < 2:
                planes.append(jnp.where(self.high, own(at), halo(at)))
            elif at < 4:
                planes.append(own(at - self.own_at))
            else:
                planes.append(jnp.where(self.high, halo(at - 4), own(at - 2)))
        return jnp.concatenate(planes, axis=1)


def lanes_from(start, size):
    return pl.ds(pl.multiple_of(start, 128), size)


def power_sums(field, weight, lane, half, rows, store):
    total = [None] * (3 * ORDERS)
    for s in range(weight.shape[0]):
        first = field[pl.ds(s * rows + half * 8, 8), pl.ds(lane, 128)]
        second = first * first
        powers = (first, second, second * first, second * second)
        for j in range(3):
            for k in range(ORDERS):
                term = powers[k] if j == 0 else powers[k] * weight[s, j - 1]
                at = j * ORDERS + k
                total[at] = term if s == 0 else total[at] + term
    store(pl.ds(half * 8, 8), [[total[j * ORDERS + k] * STEP ** (k + 1) for k in range(ORDERS)] for j in range(3)])


def pair_sums(field, weight, rows, there, here, cell):
    def piece(half, lane, target):
        def store(at, sums):
            for j in range(3):
                for k in range(ORDERS):
                    target[k, j, cell, at, :] = sums[j][k]

        power_sums(field, weight, lane, half, rows, store)

    return [
        lambda half=half, lane=lane, target=target: piece(half, lane, target)
        for lane, target in ((0, there), (128, here))
        for half in range(rows // 8)
    ]


def weave(pieces, chunks):
    done = 0
    for i, piece in enumerate(pieces):
        piece()
        while done * len(pieces) < (i + 1) * len(chunks):
            chunks[done]()
            done += 1


def encode(sums, exponents, code, groups):
    cells, rows = sums.shape[2:4]
    exponents[...] = jnp.zeros(exponents.shape, jnp.float32)
    for n in range(ORDERS * 3):
        for g, (start, stop) in enumerate(groups):
            value = sums[n // 3, n % 3, start:stop]
            top = jnp.max(jnp.max(jnp.abs(value), axis=0), axis=0, keepdims=True)
            exponent = jnp.ceil(jnp.log(jnp.maximum(top, TINY)) * np.float32(1.0 / np.log(2.0)))
            rounded = jnp.round(value * (jnp.exp2(-exponent) * LEVELS))
            code[n * cells + start : n * cells + stop] = rounded.astype(jnp.int32).astype(jnp.int16)
            exponents[pl.ds(n * len(groups) + g, 1), :] = exponent
    last = exponents[...].reshape(exponents.shape[0] // rows, rows, exponents.shape[1])
    code[ORDERS * 3 * cells :] = last.astype(jnp.int32).astype(jnp.int16)


def decode_scales(code, scales):
    exponents = code.astype(jnp.int32).astype(jnp.float32)
    scales[...] = (jnp.exp2(exponents) * (1.0 / LEVELS)).reshape(scales.shape)


def flat(block):
    return block.reshape(block.shape[0] * block.shape[1], block.shape[2])


def product(a, b):
    return jnp.dot(a, b, preferred_element_type=jnp.float32)


def make_copies(pairs, sems):
    return [pltpu.make_async_copy(source, target, sems.at[i]) for i, (source, target) in enumerate(pairs)]


def run_copies(pairs, sems):
    copies = make_copies(pairs, sems)
    for copy in copies:
        copy.start()
    for copy in copies:
        copy.wait()


def fill_x(field, along_y, along_z, v, w):
    size = along_y.shape[0]

    def chunk(g):
        field[pl.ds(g * size, size), :] = product(along_y[...], w(g)) - product(v(g), along_z())

    return [lambda g=g: chunk(g) for g in range(field.shape[0] // size)]


def fill_y(field, along_x, along_y, along_z, u, planes):
    size = along_y.shape[0]

    def chunk(g):
        field[pl.ds(g * size, size), :] = product(u(g), along_z()) - product(planes(g), along_x[...])

    return [lambda g=g: chunk(g) for g in range(field.shape[0] // size)]


def fill_z(field, along_x, along_y, u, planes):
    size = along_y.shape[0]

    def chunk(g):
        field[pl.ds(g * size, size), :] = product(planes(g), along_x[...]) - product(along_y[...], u(g))

    return [lambda g=g: chunk(g) for g in range(field.shape[0] // size)]


def run(chunks):
    for chunk in chunks:
        chunk()


def halves(spot, load):
    return jnp.concatenate([flat(load(block)) for block in spot.pair()], axis=1)


def inside_kernel(weight, along_x, along_y, all_z, own, other, code, here, there, exponents, *fields):
    planes, rows = own.shape[2:4]
    steps = planes // 2
    spot = Spot(planes)
    sources = (own, other)

    def half(c, g, p):
        return halves(spot, lambda block: sources[g][:, c, p, :, block])

    def along_z():
        return jnp.concatenate([all_z[:, block] for block in spot.pair()], axis=1)

    def streamwise(field, p):
        return fill_x(field, along_y, along_z, lambda g: flat(sources[g][:, 1, p]), lambda g: half(2, g, p))

    def around(c, g, p):
        return jnp.concatenate([half(c, g, p + offset) for offset, _ in TAPS], axis=1)

    def summed(i, cell):
        return pair_sums(fields[i], weight, rows, there, here, cell)

    run(streamwise(fields[0], 0))

    @pl.loop(0, steps)
    def _(step):
        p = step + 2
        weave(summed(0, 2 * step), streamwise(fields[1], 2 * step + 1))
        weave(
            summed(1, 2 * step + 1),
            fill_z(fields[3], along_x, along_y, lambda g: half(0, g, p), lambda g: around(1, g, p)),
        )
        weave(
            summed(3, planes + steps + step),
            fill_y(
                fields[2], along_x, along_y, along_z,
                lambda g: flat(sources[g][:, 0, p]), lambda g: around(2, g, p),
            ),
        )
        weave(summed(2, planes + step), streamwise(fields[0], jnp.minimum(2 * step + 2, planes - 1)))

    encode(there, exponents, code, [(g * steps, g * steps + steps) for g in range(4)])


def edge_kernel(components, near, n_halos, halo_of, weight, along_x, along_y, all_z, own, other, *refs):
    count = len(components)
    halos, (code, here, there, exponents, *fields) = refs[:n_halos], refs[n_halos:]
    rows = own.shape[3]
    spot = Spot(own.shape[2])
    side = spot.near if near else spot.far
    sources = (own, other)

    def along_z():
        return jnp.concatenate([all_z[:, block] for block in spot.pair()], axis=1)

    def fill(n):
        c, p = components[n // 2], n % 2

        def around(g):
            return side.around(
                p,
                lambda i: halves(spot, lambda block: sources[g][:, c, side.own + i, :, block]),
                lambda i: flat(halo_of(halos, g)[:, c - components[0], i]),
            )

        if c == 2:
            return fill_y(
                fields[n % 2], along_x, along_y, along_z, lambda g: flat(sources[g][:, 0, side.edge + p]), around
            )
        return fill_z(
            fields[n % 2], along_x, along_y,
            lambda g: halves(spot, lambda block: sources[g][:, 0, side.edge + p, :, block]), around,
        )

    run(fill(0))
    for n in range(2 * count):
        weave(
            pair_sums(fields[n % 2], weight, rows, there, here, n),
            fill(n + 1) if n + 1 < 2 * count else [],
        )
    encode(there, exponents, code, [(2 * i, 2 * i + 2) for i in range(count)])


def solve(inverse, here, code, scales, cells, group, store):
    start, stop = cells
    count, groups = here.shape[0], scales.shape[0] // 3
    depth = here.shape[1]
    sums = []
    for j in range(count):
        coded = code[j * depth + start : j * depth + stop].astype(jnp.int32).astype(jnp.float32)
        sums.append(here[j, start:stop] + coded * scales[j * groups + group : j * groups + group + 1, :])
    for i in range(3):
        store(i, inverse[3 * i] * sums[0] + inverse[3 * i + 1] * sums[1] + inverse[3 * i + 2] * sums[2])


def finish_kernel(inverse, here, code, exponents, out, scales):
    planes = out.shape[3]
    half = planes // 2

    @pl.when(pl.program_id(0) == 0)
    def _():
        decode_scales(exponents[...], scales)

    rows = scales.shape[0] // ORDERS
    own = scales.at[pl.ds(pl.program_id(0) * rows, rows)]
    for group in range(4):
        cells = group * half, group * half + half

        def store(i, value, group=group):
            if group < 2:
                out[i, 0, 0, group * half : group * half + half] = value
            else:
                out[i, group - 1, 0, 2 : planes - 2] = value

        solve(inverse, here.at[0], code, own, cells, group, store)


def finish_edges_kernel(weight, inverse, along_x, along_y, own, other, across, diagonal, halo, *refs):
    near_here, near_code, far_here, far_code, _, out, near_out, far_out = refs[:8]
    near_scales, far_scales, *fields, out_sems = refs[8:]
    rows = own.shape[3]
    spot = Spot(own.shape[2])
    side, lane_here = spot.far, spot.lanes(spot.here)
    sources = (own, other, across, diagonal)

    def fill(p):
        def u(g):
            return flat(sources[g][:, 0, side.edge + p, :, lane_here] if g < 2 else sources[g][:, 4 + p])

        def own_plane(g, i):
            return flat(sources[g][:, 1, side.own + i, :, lane_here] if g < 2 else sources[g][:, i])

        def around(g):
            return side.around(p, lambda i: own_plane(g, i), lambda i: flat(halo[g, :, i]))

        return fill_z(fields[p], along_x, along_y, u, around)

    def solve_order(k):
        for c in range(2):
            def store_near(i, value, c=c):
                near_out[i, c, k] = value

            cells, scales = (2 - 2 * c, 4 - 2 * c), near_scales.at[pl.ds(6 * k, 6)]
            solve(inverse, near_here.at[k], near_code.at[pl.ds(12 * k, 12)], scales, cells, 1 - c, store_near)

        def store_far(i, value):
            far_out[i, 0, k] = value

        scales = far_scales.at[pl.ds(3 * k, 3)]
        solve(inverse, far_here.at[k], far_code.at[pl.ds(6 * k, 6)], scales, (0, 2), 0, store_far)

    def sum_half(p, half):
        def store(at, sums):
            for k in range(ORDERS):
                for i in range(3):
                    far_out[i, 1, k, p, at, :] = (
                        inverse[3 * i, at] * sums[0][k]
                        + inverse[3 * i + 1, at] * sums[1][k]
                        + inverse[3 * i + 2, at] * sums[2][k]
                    )

        power_sums(fields[p], weight, 0, half, rows, store)

    decode_scales(near_code[ORDERS * 12 :], near_scales)
    decode_scales(far_code[ORDERS * 6 :], far_scales)
    weave([lambda k=k: solve_order(k) for k in range(ORDERS)], fill(0))
    near_copy, far_copy = make_copies(
        [
            (near_out, out.at[:, pl.ds(1, 2), :, pl.ds(spot.near.edge, 2)]),
            (far_out, out.at[:, pl.ds(1, 2), :, pl.ds(spot.far.edge, 2)]),
        ],
        out_sems,
    )
    near_copy.start()
    weave([lambda half=half: sum_half(0, half) for half in range(rows // 8)], fill(1))
    for half in range(rows // 8):
        sum_half(1, half)
    far_copy.start()
    near_copy.wait()
    far_copy.wait()


def pack_near_kernel(own, near, sems):
    spot = Spot(own.shape[2])
    planes = pl.ds(spot.near.edge, 2)
    run_copies(
        [
            (own.at[:, pl.ds(1, 2), planes, :, block], near.at[:, :, :, :, pl.ds(b * 128, 128)])
            for b, block in enumerate(spot.pair())
        ],
        sems,
    )


def pack_across_kernel(own, across, diagonal, sems):
    spot = Spot(own.shape[2])
    pairs = []
    for target, block in ((across, spot.there), (diagonal, spot.diagonal)):
        lane = spot.lanes(block)
        pairs.append((own.at[:, 1, pl.ds(spot.far.own, 4), :, lane], target.at[:, pl.ds(0, 4)]))
        pairs.append((own.at[:, 0, pl.ds(spot.far.edge, 2), :, lane], target.at[:, pl.ds(4, 2)]))
    run_copies(pairs, sems)


def pack_other_kernel(own, other, near, far, sems):
    spot = Spot(own.shape[2])
    pairs = []
    for b, source in enumerate(spot.pair()):
        target = pl.ds(b * 128, 128)
        planes = pl.ds(spot.near.edge, 2)
        pairs.append((other.at[:, pl.ds(1, 2), planes, :, source], near.at[:, :, :, :, target]))
        planes = pl.ds(spot.far.edge, 2)
        for g, array in enumerate((own, other)):
            pairs.append((array.at[:, pl.ds(2, 1), planes, :, source], far.at[g, :, :, :, :, target]))
    run_copies(pairs, sems)


def pack_far_kernel(own, other, across, diagonal, far, sems):
    spot = Spot(own.shape[2])
    planes, lane = pl.ds(spot.far.edge, 2), spot.lanes(spot.here)
    pairs = [(array.at[:, 1, planes, :, lane], far.at[g]) for g, array in enumerate((own, other))]
    planes = pl.ds(spot.far.edge_at, 2)
    pairs += [(array.at[:, planes], far.at[2 + g]) for g, array in enumerate((across, diagonal))]
    run_copies(pairs, sems)


def params(megabytes):
    return {
        "compiler_params": pltpu.CompilerParams(vmem_limit_bytes=megabytes * 2**20),
        "cost_estimate": pl.CostEstimate(flops=1, bytes_accessed=1, transcendentals=0),
    }


def smem():
    return pl.BlockSpec(memory_space=pltpu.SMEM)


def hbm():
    return pl.BlockSpec(memory_space=pl.ANY)


def vmem():
    return pl.BlockSpec(memory_space=pltpu.VMEM)


def after(value, *others):
    return lax.optimization_barrier((value, *others))[0]


def local(velocity, phase_bins):
    snaps, _, planes, rows, lanes = velocity.shape
    kind = velocity.dtype
    n_snap, n_slab = lax.axis_size("snap"), lax.axis_size("slab")
    width = lanes // n_snap
    pair, size = 2 * width, snaps * rows

    near_pairs = [(i, i ^ 1) for i in range(n_slab)]
    far_pairs = [(i, i + 1) for i in range(1, n_slab - 1, 2)]
    far_pairs = far_pairs + [(j, i) for i, j in far_pairs]
    core_pairs = [(i, i ^ 1) for i in range(n_snap)]
    chip_pairs = [(i, (i + 2) % n_snap) for i in range(n_snap)]
    diagonal_pairs = [(i, ((i + 2) % n_snap) ^ 1) for i in range(n_snap)]

    def pack(kernel, arrays, shapes, copies):
        return pl.pallas_call(
            kernel,
            in_specs=[hbm()] * len(arrays),
            out_specs=[vmem()] * len(shapes),
            out_shape=[jax.ShapeDtypeStruct(shape, kind) for shape in shapes],
            scratch_shapes=[pltpu.SemaphoreType.DMA((copies,))],
            **params(8),
        )(*arrays)

    near_shape, far_shape = (snaps, 2, 2, rows, pair), (2, snaps, 1, 2, rows, pair)
    table = jnp.asarray(phase_table().reshape(-1))
    along_x = jnp.asarray(four_planes(pair), jnp.bfloat16)
    along_x_half = jnp.asarray(four_planes(width), jnp.bfloat16)
    along_y = jnp.asarray(np.kron(np.eye(snaps, dtype=np.float32), band(rows)), jnp.bfloat16)
    along_z = jnp.asarray(band(lanes).T, jnp.bfloat16)
    field = pltpu.VMEM((2 * size, pair), jnp.float32)

    def sums(cells, groups):
        shape = (ORDERS, 3, cells, rows, width)
        last = -(-ORDERS * 3 * groups // rows)
        return {
            "out_shape": [
                jax.ShapeDtypeStruct((ORDERS * 3 * cells + last, rows, width), jnp.int16),
                jax.ShapeDtypeStruct(shape, jnp.float32),
            ],
        }, [pltpu.VMEM(shape, jnp.float32), pltpu.VMEM((last * rows, width), jnp.float32)]

    def inside_sums(weights):
        call, scratch = sums(2 * planes, 4)
        return pl.pallas_call(
            inside_kernel, scratch_shapes=[*scratch, field, field, field, field], **call, **params(26)
        )(weights, along_x, along_y, along_z, velocity, other)

    def edge_sums(weights, components, near, halos, halo_of):
        count = len(components)

        def body(*refs):
            edge_kernel(components, near, len(halos), halo_of, *refs)

        call, scratch = sums(2 * count, count)
        return pl.pallas_call(body, scratch_shapes=[*scratch, field, field], **call, **params(26))(
            weights, along_x, along_y, along_z, velocity, other, *halos
        )

    def exchange(parts):
        code, here = parts
        return here, lax.ppermute(code, "snap", chip_pairs)

    other = lax.ppermute(velocity, "snap", core_pairs)
    with jax.named_scope("pack"):
        (near_own,) = pack(pack_near_kernel, (velocity,), [near_shape], 2)
        halo_own = lax.ppermute(near_own, "slab", near_pairs)
    pair_bins = jnp.concatenate([phase_bins, lax.ppermute(phase_bins, "snap", core_pairs)])
    chip_bins = [lax.ppermute(phase_bins, "snap", pairs) for pairs in (chip_pairs, diagonal_pairs)]
    all_bins = jnp.concatenate([pair_bins, *chip_bins])

    def spread(bins):
        return pl.pallas_call(
            weights_kernel,
            in_specs=[smem(), smem()],
            out_shape=jax.ShapeDtypeStruct((bins.shape[0], 2, 8, 128), jnp.float32),
            **params(8),
        )(bins, table)

    with jax.named_scope("weights"):
        pair_weights = spread(pair_bins)
    with jax.named_scope("pack"):
        for_across, for_diagonal = pack(
            pack_across_kernel, (after(velocity, near_own),), [(snaps, 6, rows, width)] * 2, 4
        )
        across = lax.ppermute(for_across, "snap", chip_pairs)
        diagonal = lax.ppermute(for_diagonal, "snap", diagonal_pairs)
        near_other, far_w = pack(
            pack_other_kernel, (velocity, after(other, for_across, for_diagonal)), [near_shape, far_shape], 6
        )
        halo_other = lax.ppermute(near_other, "slab", near_pairs)

    with jax.named_scope("inside"):
        inside_parts = inside_sums(after(pair_weights, near_other, far_w))

    with jax.named_scope("pack"):
        (far_v,) = pack(
            pack_far_kernel, (velocity, after(other, inside_parts[0]), across, diagonal), [(4, snaps, 2, rows, width)], 4
        )
    inside = exchange((after(inside_parts[0], far_v), inside_parts[1]))
    halo_w = lax.ppermute(after(far_w, halo_other, halo_own, inside_parts[0]), "slab", far_pairs)
    halo_v = lax.ppermute(far_v, "slab", far_pairs)

    with jax.named_scope("edge_near"):
        near = exchange(edge_sums(pair_weights, (1, 2), True, (halo_own, halo_other), lambda halos, g: halos[g]))
    with jax.named_scope("edge_far"):
        ready = after(pair_weights, inside[1])
        far_y = exchange(edge_sums(ready, (2,), False, (halo_w,), lambda halos, g: halos[0].at[g]))

    with jax.named_scope("invert"):
        weights = spread(after(all_bins, inside_parts[0]))
        inverse = pl.pallas_call(
            invert_kernel, out_shape=jax.ShapeDtypeStruct((9, rows, width), jnp.float32), **params(8)
        )(weights)

    out_shape = jax.ShapeDtypeStruct((3, 3, ORDERS, planes, rows, width), jnp.float32)

    last = 3
    with jax.named_scope("finish"):
        out = pl.pallas_call(
            finish_kernel,
            out_shape=out_shape,
            grid=(ORDERS,),
            in_specs=[
                pl.BlockSpec((9, rows, width), lambda p: (0, 0, 0)),
                pl.BlockSpec((1, 3, 2 * planes, rows, width), lambda p: (p, 0, 0, 0, 0)),
                pl.BlockSpec((6 * planes, rows, width), lambda p: (p, 0, 0)),
                pl.BlockSpec((last, rows, width), lambda p: (ORDERS * 6 * planes // last, 0, 0)),
            ],
            out_specs=pl.BlockSpec((3, 3, 1, planes, rows, width), lambda p: (0, 0, p, 0, 0, 0)),
            scratch_shapes=[pltpu.VMEM((last * rows, width), jnp.float32)],
            **params(16),
        )(inverse, *inside, inside[1])

    with jax.named_scope("finish_edges"):
        edges = pltpu.VMEM((3, 2, ORDERS, 2, rows, width), jnp.float32)
        return pl.pallas_call(
            finish_edges_kernel,
            out_shape=out_shape,
            in_specs=[vmem()] * 13 + [hbm()],
            out_specs=hbm(),
            scratch_shapes=[
                edges, edges,
                pltpu.VMEM((2 * rows, width), jnp.float32),
                pltpu.VMEM((rows, width), jnp.float32),
                pltpu.VMEM((4 * size, width), jnp.float32),
                pltpu.VMEM((4 * size, width), jnp.float32),
                pltpu.SemaphoreType.DMA((2,)),
            ],
            input_output_aliases={13: 0},
            **params(26),
        )(
            weights, inverse, along_x_half, along_y, velocity, other, across, diagonal,
            after(halo_v, out), *near, *far_y, out,
        )


def solution(mesh):
    in_specs = (P("snap", None, "slab", None, None), P("snap"))
    out_specs = P(None, None, None, "slab", None, "snap")
    return jax.shard_map(local, mesh=mesh, in_specs=in_specs, out_specs=out_specs, check_vma=False)
```

time: 79.6 us -> 60.8 us (0.76); the launches traced: 78.2 us -> 60.6 us
  Pallas kernels: 54.7 us -> 22.7 us
  waiting for transfers between devices: 0.9 us -> 16.4 us
  other arithmetic: 1.96 us -> 0.15 us
  starting transfers between devices: 16.4 us -> 18.2 us
  local copies, waits for them, and re-layouts: 3.93 us -> 2.83 us
    pallas_call x9 -> x11, Pallas kernels: 50.6 us -> 20.6 us  [the longest x1 10.8 us: inside_sums(): pl.pallas_call(inside_kernel, scratch_shapes=[*scratch, field, field, fie...]
    ppermute x1, waiting for transfers between devices: 0.01 us -> 3.93 us  [local(): halo_other = lax.ppermute(near_other, 'slab', near_pairs)]
    ppermute x3, waiting for transfers between devices: 0.01 us -> 3.38 us  [exchange(): return (here, lax.ppermute(code, 'snap', chip_pairs))]
    ppermute x2 -> x3, waiting for transfers between devices: 0.01 us -> 3.24 us  [the longest x1 3.24 us: local(): halo_v = lax.ppermute(far_v, 'slab', far_pairs)]
    ppermute x1, waiting for transfers between devices: 0.87 us -> 3.72 us  [local(): other = lax.ppermute(velocity, 'snap', core_pairs)]
    ppermute x3, starting transfers between devices: 2.71 us -> 4.75 us  [exchange(): return (here, lax.ppermute(code, 'snap', chip_pairs))]
    pallas_call x1, Pallas kernels: 4.07 us -> 2.11 us  [local(): pl.pallas_call(finish_kernel, out_shape=out_shape, grid=(ORDERS,), in_spe...]
    concatenate x2 -> x1, other arithmetic: 1.37 us -> 0.08 us  [local(): all_bins = jnp.concatenate([pair_bins, *chip_bins])]
  transfers between devices with their start and end apart: 12 -> 13, of which waited for: 1 -> 6; matrix products, arithmetic and copies ran while one was open for 3% -> 0% of each run, Pallas kernels for 63% -> 33%
where the time goes in v3:
time: 60.8 us; the launch traced here: 60.6 us
  Pallas kernels  22.7 us (37%)
  starting transfers between devices  18.2 us (30%)
  waiting for transfers between devices  16.4 us (27%)
  local copies, waits for them, and re-layouts  2.83 us (5%)
    pallas_call x1, Pallas kernels, inside_sums(): pl.pallas_call(inside_kernel, scratch_shapes=[*scratch, field, field, fie...  10.8 us
    pallas_call x2, Pallas kernels, edge_sums(): pl.pallas_call(body, scratch_shapes=[*scratch, field, field], **call, **p...  5.14 us
    ppermute x3, starting transfers between devices, exchange(): return (here, lax.ppermute(code, 'snap', chip_pairs))  4.75 us
    ppermute x1, waiting for transfers between devices, local(): halo_other = lax.ppermute(near_other, 'slab', near_pairs)  3.93 us
    ppermute x1, waiting for transfers between devices, local(): other = lax.ppermute(velocity, 'snap', core_pairs)  3.72 us
    ppermute x1, starting transfers between devices, local(): halo_v = lax.ppermute(far_v, 'slab', far_pairs)  3.64 us
    ppermute x3, waiting for transfers between devices, exchange(): return (here, lax.ppermute(code, 'snap', chip_pairs))  3.38 us
    ppermute x1, starting transfers between devices, local(): lax.ppermute(after(far_w, halo_other, halo_own, inside_parts[0]), 'slab',...  3.27 us
  transfers between devices with their start and end apart: 13, of which 6 were waited for; matrix products, arithmetic and copies ran while one was open for 0% of the time, Pallas kernels for 33%

profile of v3, /device:TPU:16, one launch (start us, length us, event | category | flops | bytes accessed | tf_op | source)
XLA Modules:
  0.0 60.6 jit_solution(13916455540498271590)
XLA Ops:
  0.0 2.8 %copy-done = bf16[16,3,8,16,512]{4,3,2,1,0:T(8,128)(2,1)S(1)} copy-done((bf16[16,3,8,16,512]{4,3,2,1,0:T(8,128)(2,1)S(1)}, bf16[16,3,8,16,512]{4,3,2,1,0:T(8,128)(2,1)}, u32[]{:S(2)}) %copy-start) | copy-done | bytes 6291480
  3.1 1.6 %collective-permute-start.4 = (bf16[16,6,16,128]{3,2,1,0:T(8,128)(2,1)S(1)}, bf16[16,6,16,128]{3,2,1,0:T(8,128)(2,1)S(1)}, u32[]{:S(2)}, u32[]{:S(2)}) collective-permute-start(bf16[16,6,16,128]{3,2,1,0:T(8,128)(2,1)S(1)} %get-tuple-element.25), channel_id=1, source_target_pairs={{0,16},{8,24},{16,0},{24,8},{1,17},{9,25},{17,1},{25,9},{2,18},{10... | collective-permute-start | bytes 1179656 | tf_op jit(solution)/shard_map/pack/ppermute | solution.py:544
  4.8 0.4 collective-permute-start.5
  5.2 1.5 %collective-permute-start.8 = (bf16[16,2,2,16,256]{4,3,2,1,0:T(8,128)(2,1)S(1)}, bf16[16,2,2,16,256]{4,3,2,1,0:T(8,128)(2,1)S(1)}, u32[]{:S(2)}, u32[]{:S(2)}) collective-permute-start(bf16[16,2,2,16,256]{4,3,2,1,0:T(8,128)(2,1)S(1)} %pack.4), channel_id=1, source_target_pairs={{0,1},{1,0},{2,3},{3,2},{4,5},{5,4},{6,7},{7,6},{8,9},{9,8},{10,11... | collective-permute-start | bytes 1572872 | tf_op jit(solution)/shard_map/pack/ppermute | solution.py:525
  6.7 3.7 %collective-permute-done.3.other.refs_5_ = bf16[16,3,8,16,512]{4,3,2,1,0:T(8,128)(2,1)S(1)} collective-permute-done((bf16[16,3,8,16,512]{4,3,2,1,0:T(8,128)(2,1)}, bf16[16,3,8,16,512]{4,3,2,1,0:T(8,128)(2,1)S(1)}, u32[]{:S(2)}, u32[]{:S(2)}) %collective-permute-start.3) | collective-permute-done | bytes 6291488 | tf_op jit(solution)/shard_map/ppermute | solution.py:522
  10.6 1.6 %collective-permute-start.9 = (bf16[16,2,2,16,256]{4,3,2,1,0:T(8,128)(2,1)S(1)}, bf16[16,2,2,16,256]{4,3,2,1,0:T(8,128)(2,1)S(1)}, u32[]{:S(2)}, u32[]{:S(2)}) collective-permute-start(bf16[16,2,2,16,256]{4,3,2,1,0:T(8,128)(2,1)S(1)} %get-tuple-element.28), channel_id=1, source_target_pairs={{0,1},{1,0},{2,3},{3,2},{4,5},{5,4},{6,7},{7,6},{8,9},{9,8},{10,11... | collective-permute-start | bytes 1572872 | tf_op jit(solution)/shard_map/pack/ppermute | solution.py:549
  12.2 1.1 %collective-permute-done = s32[16]{0:T(128)S(1)} collective-permute-done((s32[16]{0:T(128)S(1)}, s32[16]{0:T(128)S(1)}, u32[]{:S(2)}, u32[]{:S(2)}) %collective-permute-start) | collective-permute-done | bytes 96 | tf_op jit(solution)/shard_map/ppermute | solution.py:526
  13.4 0.6 %weights.1.weight.refs_0_ = f32[32,2,8,128]{3,2,1,0:T(8,128)S(1)} custom-call(s32[32]{0:T(128)S(1)} %pad_add_fusion.1.bins, f32[360]{0:T(512)S(1)} %copy-done.5), custom_call_target="tpu_custom_call" | custom-call | flops 1 | bytes 1 | tf_op jit(solution)/shard_map/weights/pallas_call | solution.py:531
  14.1 10.8 %inside.1 = (s16[195,16,128]{2,1,0:T(8,128)(2,1)S(1)}, f32[4,3,16,16,128]{4,3,2,1,0:T(8,128)S(1)}) custom-call(f32[32,2,8,128]{3,2,1,0:T(8,128)S(1)} %weights.1.weight.refs_0_, bf16[1024,256]{1,0:T(8,128)(2,1)S(1)} %copy-done.2, bf16[256,256]{1,0:T(8,128)(2,1)S(1)} %copy-done.3, bf16[512,512]{1,0:T(8,128)(2,1)S(1)} %copy-done.1, ...), custom_call_target="tpu_custom_call" | custom-call | flops 1 | bytes 1 | tf_op jit(solution)/shard_map/inside/pallas_call | solution.py:503
  25.0 1.6 %collective-permute-start.7 = (s16[195,16,128]{2,1,0:T(8,128)(2,1)S(1)}, s16[195,16,128]{2,1,0:T(8,128)(2,1)S(1)}, u32[]{:S(2)}, u32[]{:S(2)}) collective-permute-start(s16[195,16,128]{2,1,0:T(8,128)(2,1)S(1)} %get-tuple-element.35), channel_id=1, source_target_pairs={{0,16},{8,24},{16,0},{24,8},{1,17},{9,25},{17,1},{25,9},{2,18},{10... | collective-permute-start | bytes 2396168 | tf_op jit(solution)/shard_map/ppermute | solution.py:520
  26.6 3.9 %collective-permute-done.9.refs_7_ = bf16[16,2,2,16,256]{4,3,2,1,0:T(8,128)(2,1)S(1)} collective-permute-done((bf16[16,2,2,16,256]{4,3,2,1,0:T(8,128)(2,1)S(1)}, bf16[16,2,2,16,256]{4,3,2,1,0:T(8,128)(2,1)S(1)}, u32[]{:S(2)}, u32[]{:S(2)}) %collective-permute-start.9) | collective-permute-done | bytes 524320 | tf_op jit(solution)/shard_map/pack/ppermute | solution.py:549
  30.5 3.3 %collective-permute-start.11 = (bf16[2,16,1,2,16,256]{5,4,3,2,1,0:T(8,128)(2,1)S(1)}, bf16[2,16,1,2,16,256]{5,4,3,2,1,0:T(8,128)(2,1)S(1)}, u32[]{:S(2)}, u32[]{:S(2)}) collective-permute-start(bf16[2,16,1,2,16,256]{5,4,3,2,1,0:T(8,128)(2,1)S(1)} %get-tuple-element.40), channel_id=1, source_target_pairs={{1,2},{3,4},{5,6},{2,1},{4,3},{6,5},{9,10},{11,12},{13,14},{10,9},... | collective-permute-start | bytes 1572872 | tf_op jit(solution)/shard_map/ppermute | solution.py:559
  33.8 3.6 %collective-permute-start.6 = (bf16[4,16,2,16,128]{4,3,2,1,0:T(8,128)(2,1)S(1)}, bf16[4,16,2,16,128]{4,3,2,1,0:T(8,128)(2,1)S(1)}, u32[]{:S(2)}, u32[]{:S(2)}) collective-permute-start(bf16[4,16,2,16,128]{4,3,2,1,0:T(8,128)(2,1)S(1)} %pack.7), channel_id=1, source_target_pairs={{1,2},{3,4},{5,6},{2,1},{4,3},{6,5},{9,10},{11,12},{13,14},{10,9},... | collective-permute-start | bytes 1572872 | tf_op jit(solution)/shard_map/ppermute | solution.py:560
  37.4 3.3 %edge_near.1 = (s16[50,16,128]{2,1,0:T(8,128)(2,1)S(1)}, f32[4,3,4,16,128]{4,3,2,1,0:T(8,128)S(1)}) custom-call(f32[32,2,8,128]{3,2,1,0:T(8,128)S(1)} %weights.1.weight.refs_0_, bf16[1024,256]{1,0:T(8,128)(2,1)S(1)} %copy-done.2, bf16[256,256]{1,0:T(8,128)(2,1)S(1)} %copy-done.3, bf16[512,512]{1,0:T(8,128)(2,1)S(1)} %copy-done.1, ...), custom_call_target="tpu_custom_call" | custom-call | flops 1 | bytes 1 | tf_op jit(solution)/shard_map/edge_near/pallas_call | solution.py:514
  40.7 1.6 %collective-permute-start.10 = (s16[50,16,128]{2,1,0:T(8,128)(2,1)S(1)}, s16[50,16,128]{2,1,0:T(8,128)(2,1)S(1)}, u32[]{:S(2)}, u32[]{:S(2)}) collective-permute-start(s16[50,16,128]{2,1,0:T(8,128)(2,1)S(1)} %get-tuple-element.38), channel_id=1, source_target_pairs={{0,16},{8,24},{16,0},{24,8},{1,17},{9,25},{17,1},{25,9},{2,18},{10... | collective-permute-start | bytes 614408 | tf_op jit(solution)/shard_map/edge_near/ppermute | solution.py:520
  42.3 3.4 %collective-permute-done.7.code.exponents = s16[195,16,128]{2,1,0:T(8,128)(2,1)S(1)} collective-permute-done((s16[195,16,128]{2,1,0:T(8,128)(2,1)S(1)}, s16[195,16,128]{2,1,0:T(8,128)(2,1)S(1)}, u32[]{:S(2)}, u32[]{:S(2)}) %collective-permute-start.7) | collective-permute-done | bytes 798752 | tf_op jit(solution)/shard_map/ppermute | solution.py:520
  45.7 1.5 %collective-permute-start.1 = (s32[16]{0:T(128)S(1)}, s32[16]{0:T(128)S(1)}, u32[]{:S(2)}, u32[]{:S(2)}) collective-permute-start(s32[16]{0:T(128)S(1)} %copy-done.6), channel_id=1, source_target_pairs={{0,16},{8,24},{16,0},{24,8},{1,17},{9,25},{17,1},{25,9},{2,18},{10... | collective-permute-start | bytes 200 | tf_op jit(solution)/shard_map/ppermute | solution.py:527
  47.2 1.0 %collective-permute-done.11.refs_6_ = bf16[2,16,1,2,16,256]{5,4,3,2,1,0:T(8,128)(2,1)S(1)} collective-permute-done((bf16[2,16,1,2,16,256]{5,4,3,2,1,0:T(8,128)(2,1)S(1)}, bf16[2,16,1,2,16,256]{5,4,3,2,1,0:T(8,128)(2,1)S(1)}, u32[]{:S(2)}, u32[]{:S(2)}) %collective-permute-start.11) | collective-permute-done | bytes 524320 | tf_op jit(solution)/shard_map/ppermute | solution.py:559
  48.1 1.9 %edge_far.1 = (s16[25,16,128]{2,1,0:T(8,128)(2,1)S(1)}, f32[4,3,2,16,128]{4,3,2,1,0:T(8,128)S(1)}) custom-call(f32[32,2,8,128]{3,2,1,0:T(8,128)S(1)} %weights.1.weight.refs_0_, bf16[1024,256]{1,0:T(8,128)(2,1)S(1)} %copy-done.2, bf16[256,256]{1,0:T(8,128)(2,1)S(1)} %copy-done.3, bf16[512,512]{1,0:T(8,128)(2,1)S(1)} %copy-done.1, ...), custom_call_target="tpu_custom_call" | custom-call | flops 1 | bytes 1 | tf_op jit(solution)/shard_map/edge_far/pallas_call | solution.py:514
  50.0 1.6 %collective-permute-start.12 = (s16[25,16,128]{2,1,0:T(8,128)(2,1)S(1)}, s16[25,16,128]{2,1,0:T(8,128)(2,1)S(1)}, u32[]{:S(2)}, u32[]{:S(2)}) collective-permute-start(s16[25,16,128]{2,1,0:T(8,128)(2,1)S(1)} %get-tuple-element.42), channel_id=1, source_target_pairs={{0,16},{8,24},{16,0},{24,8},{1,17},{9,25},{17,1},{25,9},{2,18},{10... | collective-permute-start | bytes 307208 | tf_op jit(solution)/shard_map/edge_far/ppermute | solution.py:520
  51.7 0.7 %invert.2.weight = f32[64,2,8,128]{3,2,1,0:T(8,128)S(1)} custom-call(s32[64]{0:T(128)S(1)} %pad_add_fusion.bins, f32[360]{0:T(512)S(1)} %copy-done.5), custom_call_target="tpu_custom_call" | custom-call | flops 1 | bytes 1 | tf_op jit(solution)/shard_map/invert/pallas_call | solution.py:531
  52.5 2.1 %finish.1.refs_4_ = f32[3,3,4,8,16,128]{5,4,3,2,1,0:T(8,128)} custom-call(f32[9,16,128]{2,1,0:T(8,128)S(1)} %invert.3.inverse, f32[4,3,16,16,128]{4,3,2,1,0:T(8,128)S(1)} %get-tuple-element.34.here, s16[195,16,128]{2,1,0:T(8,128)(2,1)S(1)} %collective-permute-done.7.code.exponents, s16[195,16,128]{2,1,0:T(8,128)(2,1)S(1)} %collective-permute-done.7.code.exponents), custom_call_target="tpu_custom_call" | custom-call | flops 1 | bytes 1 | tf_op jit(solution)/shard_map/finish/pallas_call | solution.py:578
  54.6 3.2 %collective-permute-done.6.halo = bf16[4,16,2,16,128]{4,3,2,1,0:T(8,128)(2,1)S(1)} collective-permute-done((bf16[4,16,2,16,128]{4,3,2,1,0:T(8,128)(2,1)S(1)}, bf16[4,16,2,16,128]{4,3,2,1,0:T(8,128)(2,1)S(1)}, u32[]{:S(2)}, u32[]{:S(2)}) %collective-permute-start.6) | collective-permute-done | bytes 524320 | tf_op jit(solution)/shard_map/ppermute | solution.py:560
  57.8 2.6 %finish_edges.1 = f32[3,3,4,8,16,128]{5,4,3,2,1,0:T(8,128)} custom-call(f32[64,2,8,128]{3,2,1,0:T(8,128)S(1)} %invert.2.weight, f32[9,16,128]{2,1,0:T(8,128)S(1)} %invert.3.inverse, bf16[512,128]{1,0:T(8,128)(2,1)S(1)} %copy-done.4, bf16[256,256]{1,0:T(8,128)(2,1)S(1)} %copy-done.3, ...), custom_call_target="tpu_custom_call", output_to_operand_aliasing={{}: (13, {})} | custom-call | flops 1 | bytes 1 | tf_op jit(solution)/shard_map/finish_edges/pallas_call | solution.py:595
  (35 shorter events, 1.0 us)
Async XLA Ops:
  0.0 10.4 %collective-permute-start.3 = (bf16[16,3,8,16,512]{4,3,2,1,0:T(8,128)(2,1)}, bf16[16,3,8,16,512]{4,3,2,1,0:T(8,128)(2,1)S(1)}, u32[]{:S(2)}, u32[]{:S(2)}) collective-permute-start(bf16[16,3,8,16,512]{4,3,2,1,0:T(8,128)(2,1)} %own.10), channel_id=1, source_target_pairs={{0,8},{8,0},{16,24},{24,16},{1,9},{9,1},{17,25},{25,17},{2,10},{10... | collective-permute-start | bytes 18874376 | tf_op jit(solution)/shard_map/ppermute | solution.py:522
  0.0 2.8 %copy-start = (bf16[16,3,8,16,512]{4,3,2,1,0:T(8,128)(2,1)S(1)}, bf16[16,3,8,16,512]{4,3,2,1,0:T(8,128)(2,1)}, u32[]{:S(2)}) copy-start(bf16[16,3,8,16,512]{4,3,2,1,0:T(8,128)(2,1)} %own.10) | copy-start | bytes 18874372
  3.1 21.7 %collective-permute-start.4 = (bf16[16,6,16,128]{3,2,1,0:T(8,128)(2,1)S(1)}, bf16[16,6,16,128]{3,2,1,0:T(8,128)(2,1)S(1)}, u32[]{:S(2)}, u32[]{:S(2)}) collective-permute-start(bf16[16,6,16,128]{3,2,1,0:T(8,128)(2,1)S(1)} %get-tuple-element.25), channel_id=1, source_target_pairs={{0,16},{8,24},{16,0},{24,8},{1,17},{9,25},{17,1},{25,9},{2,18},{10... | collective-permute-start | bytes 1179656 | tf_op jit(solution)/shard_map/pack/ppermute | solution.py:544
  4.7 9.3 %slice-start = ((s8[6291456]{0:T(1024)(128)(4,1)}), s8[4194304]{0:T(1024)(128)(4,1)S(1)}, s32[]{:S(2)}) async-start(s8[6291456]{0:T(1024)(128)(4,1)} %bitcast), calls=%async_computation | async-start | bytes 8388608
  4.7 7.5 %copy-start.6 = (s32[16]{0:T(128)S(1)}, s32[16]{0:T(128)}, u32[]{:S(2)}) copy-start(s32[16]{0:T(128)} %param.8) | copy-start | bytes 196
  4.7 8.7 %copy-start.5 = (f32[360]{0:T(512)S(1)}, f32[360]{0:T(512)}, u32[]{:S(2)}) copy-start(f32[360]{0:T(512)} %constant.10.clone.table) | copy-start | bytes 4324
  4.7 9.3 %slice-start.1 = ((s8[6291456]{0:T(1024)(128)(4,1)}), s8[2097152]{0:T(1024)(128)(4,1)S(1)}, s32[]{:S(2)}) async-start(s8[6291456]{0:T(1024)(128)(4,1)} %bitcast), calls=%async_computation.1 | async-start | bytes 4194304
  4.7 9.3 %copy-start.1 = (bf16[512,512]{1,0:T(8,128)(2,1)S(1)}, bf16[512,512]{1,0:T(8,128)(2,1)}, u32[]{:S(2)}) copy-start(bf16[512,512]{1,0:T(8,128)(2,1)} %constant.14.clone.all_z.refs_3_) | copy-start | bytes 1572868
  4.7 9.3 %copy-start.2 = (bf16[1024,256]{1,0:T(8,128)(2,1)S(1)}, bf16[1024,256]{1,0:T(8,128)(2,1)}, u32[]{:S(2)}) copy-start(bf16[1024,256]{1,0:T(8,128)(2,1)} %constant.11.clone.along_x.refs_1_) | copy-start | bytes 1572868
  4.7 9.3 %copy-start.3 = (bf16[256,256]{1,0:T(8,128)(2,1)S(1)}, bf16[256,256]{1,0:T(8,128)(2,1)}, u32[]{:S(2)}) copy-start(bf16[256,256]{1,0:T(8,128)(2,1)} %constant.13.clone.along_y.refs_2_) | copy-start | bytes 393220
  4.8 20.1 %collective-permute-start.5 = (bf16[16,6,16,128]{3,2,1,0:T(8,128)(2,1)S(1)}, bf16[16,6,16,128]{3,2,1,0:T(8,128)(2,1)S(1)}, u32[]{:S(2)}, u32[]{:S(2)}) collective-permute-start(bf16[16,6,16,128]{3,2,1,0:T(8,128)(2,1)S(1)} %get-tuple-element.26), channel_id=1, source_target_pairs={{0,24},{8,16},{16,8},{24,0},{1,25},{9,17},{17,9},{25,1},{2,26},{10... | collective-permute-start | bytes 1179656 | tf_op jit(solution)/shard_map/pack/ppermute | solution.py:545
  5.2 21.4 %collective-permute-start.8 = (bf16[16,2,2,16,256]{4,3,2,1,0:T(8,128)(2,1)S(1)}, bf16[16,2,2,16,256]{4,3,2,1,0:T(8,128)(2,1)S(1)}, u32[]{:S(2)}, u32[]{:S(2)}) collective-permute-start(bf16[16,2,2,16,256]{4,3,2,1,0:T(8,128)(2,1)S(1)} %pack.4), channel_id=1, source_target_pairs={{0,1},{1,0},{2,3},{3,2},{4,5},{5,4},{6,7},{7,6},{8,9},{9,8},{10,11... | collective-permute-start | bytes 1572872 | tf_op jit(solution)/shard_map/pack/ppermute | solution.py:525
  10.6 19.9 %collective-permute-start.9 = (bf16[16,2,2,16,256]{4,3,2,1,0:T(8,128)(2,1)S(1)}, bf16[16,2,2,16,256]{4,3,2,1,0:T(8,128)(2,1)S(1)}, u32[]{:S(2)}, u32[]{:S(2)}) collective-permute-start(bf16[16,2,2,16,256]{4,3,2,1,0:T(8,128)(2,1)S(1)} %get-tuple-element.28), channel_id=1, source_target_pairs={{0,1},{1,0},{2,3},{3,2},{4,5},{5,4},{6,7},{7,6},{8,9},{9,8},{10,11... | collective-permute-start | bytes 1572872 | tf_op jit(solution)/shard_map/pack/ppermute | solution.py:549
  12.2 1.1 %collective-permute-start = (s32[16]{0:T(128)S(1)}, s32[16]{0:T(128)S(1)}, u32[]{:S(2)}, u32[]{:S(2)}) collective-permute-start(s32[16]{0:T(128)S(1)} %copy-done.6), channel_id=1, source_target_pairs={{0,8},{8,0},{16,24},{24,16},{1,9},{9,1},{17,25},{25,17},{2,10},{10... | collective-permute-start | bytes 200 | tf_op jit(solution)/shard_map/ppermute | solution.py:526
  25.0 20.7 %collective-permute-start.7 = (s16[195,16,128]{2,1,0:T(8,128)(2,1)S(1)}, s16[195,16,128]{2,1,0:T(8,128)(2,1)S(1)}, u32[]{:S(2)}, u32[]{:S(2)}) collective-permute-start(s16[195,16,128]{2,1,0:T(8,128)(2,1)S(1)} %get-tuple-element.35), channel_id=1, source_target_pairs={{0,16},{8,24},{16,0},{24,8},{1,17},{9,25},{17,1},{25,9},{2,18},{10... | collective-permute-start | bytes 2396168 | tf_op jit(solution)/shard_map/ppermute | solution.py:520
  30.5 17.6 %collective-permute-start.11 = (bf16[2,16,1,2,16,256]{5,4,3,2,1,0:T(8,128)(2,1)S(1)}, bf16[2,16,1,2,16,256]{5,4,3,2,1,0:T(8,128)(2,1)S(1)}, u32[]{:S(2)}, u32[]{:S(2)}) collective-permute-start(bf16[2,16,1,2,16,256]{5,4,3,2,1,0:T(8,128)(2,1)S(1)} %get-tuple-element.40), channel_id=1, source_target_pairs={{1,2},{3,4},{5,6},{2,1},{4,3},{6,5},{9,10},{11,12},{13,14},{10,9},... | collective-permute-start | bytes 1572872 | tf_op jit(solution)/shard_map/ppermute | solution.py:559
  33.8 24.0 %collective-permute-start.6 = (bf16[4,16,2,16,128]{4,3,2,1,0:T(8,128)(2,1)S(1)}, bf16[4,16,2,16,128]{4,3,2,1,0:T(8,128)(2,1)S(1)}, u32[]{:S(2)}, u32[]{:S(2)}) collective-permute-start(bf16[4,16,2,16,128]{4,3,2,1,0:T(8,128)(2,1)S(1)} %pack.7), channel_id=1, source_target_pairs={{1,2},{3,4},{5,6},{2,1},{4,3},{6,5},{9,10},{11,12},{13,14},{10,9},... | collective-permute-start | bytes 1572872 | tf_op jit(solution)/shard_map/ppermute | solution.py:560
  40.7 17.1 %collective-permute-start.10 = (s16[50,16,128]{2,1,0:T(8,128)(2,1)S(1)}, s16[50,16,128]{2,1,0:T(8,128)(2,1)S(1)}, u32[]{:S(2)}, u32[]{:S(2)}) collective-permute-start(s16[50,16,128]{2,1,0:T(8,128)(2,1)S(1)} %get-tuple-element.38), channel_id=1, source_target_pairs={{0,16},{8,24},{16,0},{24,8},{1,17},{9,25},{17,1},{25,9},{2,18},{10... | collective-permute-start | bytes 614408 | tf_op jit(solution)/shard_map/edge_near/ppermute | solution.py:520
  42.3 9.4 %collective-permute-start.2 = (s32[16]{0:T(128)S(1)}, s32[16]{0:T(128)S(1)}, u32[]{:S(2)}, u32[]{:S(2)}) collective-permute-start(s32[16]{0:T(128)S(1)} %copy-done.6), channel_id=1, source_target_pairs={{0,24},{8,16},{16,8},{24,0},{1,25},{9,17},{17,9},{25,1},{2,26},{10... | collective-permute-start | bytes 200 | tf_op jit(solution)/shard_map/ppermute | solution.py:527
  45.7 6.0 %collective-permute-start.1 = (s32[16]{0:T(128)S(1)}, s32[16]{0:T(128)S(1)}, u32[]{:S(2)}, u32[]{:S(2)}) collective-permute-start(s32[16]{0:T(128)S(1)} %copy-done.6), channel_id=1, source_target_pairs={{0,16},{8,24},{16,0},{24,8},{1,17},{9,25},{17,1},{25,9},{2,18},{10... | collective-permute-start | bytes 200 | tf_op jit(solution)/shard_map/ppermute | solution.py:527
  50.0 7.8 %collective-permute-start.12 = (s16[25,16,128]{2,1,0:T(8,128)(2,1)S(1)}, s16[25,16,128]{2,1,0:T(8,128)(2,1)S(1)}, u32[]{:S(2)}, u32[]{:S(2)}) collective-permute-start(s16[25,16,128]{2,1,0:T(8,128)(2,1)S(1)} %get-tuple-element.42), channel_id=1, source_target_pairs={{0,16},{8,24},{16,0},{24,8},{1,17},{9,25},{17,1},{25,9},{2,18},{10... | collective-permute-start | bytes 307208 | tf_op jit(solution)/shard_map/edge_far/ppermute | solution.py:520
  52.5 5.4 %copy-start.4 = (bf16[512,128]{1,0:T(8,128)(2,1)S(1)}, bf16[512,128]{1,0:T(8,128)(2,1)}, u32[]{:S(2)}) copy-start(bf16[512,128]{1,0:T(8,128)(2,1)} %constant.12.clone.along_x) | copy-start | bytes 393220

commit v4 on v3

--- a/solution.py
+++ b/solution.py
@@ -553,11 +553,11 @@
 
     with jax.named_scope("pack"):
         (far_v,) = pack(
-            pack_far_kernel, (velocity, after(other, inside_parts[0]), across, diagonal), [(4, snaps, 2, rows, width)], 4
+            pack_far_kernel, (velocity, after(other, inside_parts[0], halo_own), across, diagonal), [(4, snaps, 2, rows, width)], 4
         )
     inside = exchange((after(inside_parts[0], far_v), inside_parts[1]))
-    halo_w = lax.ppermute(after(far_w, halo_other, halo_own, inside_parts[0]), "slab", far_pairs)
-    halo_v = lax.ppermute(far_v, "slab", far_pairs)
+    halo_w = lax.ppermute(after(far_w, inside_parts[0]), "slab", far_pairs)
+    halo_v = lax.ppermute(after(far_v, halo_other), "slab", far_pairs)
 
     with jax.named_scope("edge_near"):
         near = exchange(edge_sums(pair_weights, (1, 2), True, (halo_own, halo_other), lambda halos, g: halos[g]))

time: 60.8 us -> 58.2 us (0.957)
  starting transfers between devices: 18.2 us -> 16.6 us
  waiting for transfers between devices: 16.4 us -> 14.9 us
    ppermute x3, waiting for transfers between devices: 3.38 us -> 7.74 us  [exchange(): return (here, lax.ppermute(code, 'snap', chip_pairs))]
    ppermute x1, waiting for transfers between devices: 3.93 us -> 0.01 us  [local(): halo_other = lax.ppermute(near_other, 'slab', near_pairs)]
    ppermute x2, waiting for transfers between devices: 4.21 us -> 1.97 us  [the longest x1 1.96 us: local(): halo_v = lax.ppermute(after(far_v, halo_other), 'slab', far_pairs)]
    ppermute x3, starting transfers between devices: 4.75 us -> 2.74 us  [exchange(): return (here, lax.ppermute(code, 'snap', chip_pairs))]
  transfers between devices with their start and end apart: 13 -> 13, of which waited for: 6 -> 5; matrix products, arithmetic and copies ran while one was open for 0% -> 0% of each run, Pallas kernels for 33% -> 35%
where the time goes in v4:
time: 58.2 us; the launch traced here: 57.5 us
  Pallas kernels  22.6 us (39%)
  starting transfers between devices  16.6 us (29%)
  waiting for transfers between devices  14.9 us (26%)
  local copies, waits for them, and re-layouts  2.83 us (5%)
    pallas_call x1, Pallas kernels, inside_sums(): pl.pallas_call(inside_kernel, scratch_shapes=[*scratch, field, field, fie...  10.8 us
    ppermute x3, waiting for transfers between devices, exchange(): return (here, lax.ppermute(code, 'snap', chip_pairs))  7.74 us
    pallas_call x2, Pallas kernels, edge_sums(): pl.pallas_call(body, scratch_shapes=[*scratch, field, field], **call, **p...  5.13 us
    ppermute x1, starting transfers between devices, local(): halo_v = lax.ppermute(after(far_v, halo_other), 'slab', far_pairs)  4.59 us
    ppermute x1, waiting for transfers between devices, local(): other = lax.ppermute(velocity, 'snap', core_pairs)  3.96 us
    unnamed x18, local copies, waits for them, and re-layouts  2.83 us
    ppermute x3, starting transfers between devices, exchange(): return (here, lax.ppermute(code, 'snap', chip_pairs))  2.74 us
    pallas_call x1, Pallas kernels, local(): pl.pallas_call(finish_edges_kernel, out_shape=out_shape, in_specs=[vmem()...  2.63 us
  transfers between devices with their start and end apart: 13, of which 5 were waited for; matrix products, arithmetic and copies ran while one was open for 0% of the time, Pallas kernels for 35%

profile of v4, /device:TPU:16, one launch (start us, length us, event | category | flops | bytes accessed | tf_op | source)
XLA Modules:
  0.0 57.5 jit_solution(2061017589398010206)
XLA Ops:
  0.0 2.8 %copy-done = bf16[16,3,8,16,512]{4,3,2,1,0:T(8,128)(2,1)S(1)} copy-done((bf16[16,3,8,16,512]{4,3,2,1,0:T(8,128)(2,1)S(1)}, bf16[16,3,8,16,512]{4,3,2,1,0:T(8,128)(2,1)}, u32[]{:S(2)}) %copy-start) | copy-done | bytes 6291480
  2.9 1.6 %collective-permute-start.6 = (bf16[16,2,2,16,256]{4,3,2,1,0:T(8,128)(2,1)S(1)}, bf16[16,2,2,16,256]{4,3,2,1,0:T(8,128)(2,1)S(1)}, u32[]{:S(2)}, u32[]{:S(2)}) collective-permute-start(bf16[16,2,2,16,256]{4,3,2,1,0:T(8,128)(2,1)S(1)} %pack.4), channel_id=1, source_target_pairs={{0,1},{1,0},{2,3},{3,2},{4,5},{5,4},{6,7},{7,6},{8,9},{9,8},{10,11... | collective-permute-start | bytes 1572872 | tf_op jit(solution)/shard_map/pack/ppermute | solution.py:525
  4.5 0.2 pack.5
  4.7 1.6 %collective-permute-start.4 = (bf16[16,6,16,128]{3,2,1,0:T(8,128)(2,1)S(1)}, bf16[16,6,16,128]{3,2,1,0:T(8,128)(2,1)S(1)}, u32[]{:S(2)}, u32[]{:S(2)}) collective-permute-start(bf16[16,6,16,128]{3,2,1,0:T(8,128)(2,1)S(1)} %get-tuple-element.26), channel_id=1, source_target_pairs={{0,16},{8,24},{16,0},{24,8},{1,17},{9,25},{17,1},{25,9},{2,18},{10... | collective-permute-start | bytes 1179656 | tf_op jit(solution)/shard_map/pack/ppermute | solution.py:544
  6.4 4.0 %collective-permute-done.3.other.refs_5_ = bf16[16,3,8,16,512]{4,3,2,1,0:T(8,128)(2,1)S(1)} collective-permute-done((bf16[16,3,8,16,512]{4,3,2,1,0:T(8,128)(2,1)}, bf16[16,3,8,16,512]{4,3,2,1,0:T(8,128)(2,1)S(1)}, u32[]{:S(2)}, u32[]{:S(2)}) %collective-permute-start.3) | collective-permute-done | bytes 6291488 | tf_op jit(solution)/shard_map/ppermute | solution.py:522
  10.4 0.3 pack.6
  10.6 1.6 %collective-permute-start.7 = (bf16[16,2,2,16,256]{4,3,2,1,0:T(8,128)(2,1)S(1)}, bf16[16,2,2,16,256]{4,3,2,1,0:T(8,128)(2,1)S(1)}, u32[]{:S(2)}, u32[]{:S(2)}) collective-permute-start(bf16[16,2,2,16,256]{4,3,2,1,0:T(8,128)(2,1)S(1)} %get-tuple-element.29), channel_id=1, source_target_pairs={{0,1},{1,0},{2,3},{3,2},{4,5},{5,4},{6,7},{7,6},{8,9},{9,8},{10,11... | collective-permute-start | bytes 1572872 | tf_op jit(solution)/shard_map/pack/ppermute | solution.py:549
  12.2 1.1 %collective-permute-done = s32[16]{0:T(128)S(1)} collective-permute-done((s32[16]{0:T(128)S(1)}, s32[16]{0:T(128)S(1)}, u32[]{:S(2)}, u32[]{:S(2)}) %collective-permute-start) | collective-permute-done | bytes 96 | tf_op jit(solution)/shard_map/ppermute | solution.py:526
  13.4 0.6 %weights.1.weight.refs_0_ = f32[32,2,8,128]{3,2,1,0:T(8,128)S(1)} custom-call(s32[32]{0:T(128)S(1)} %pad_add_fusion.1.bins, f32[360]{0:T(512)S(1)} %copy-done.5), custom_call_target="tpu_custom_call" | custom-call | flops 1 | bytes 1 | tf_op jit(solution)/shard_map/weights/pallas_call | solution.py:531
  14.1 10.8 %inside.1 = (s16[195,16,128]{2,1,0:T(8,128)(2,1)S(1)}, f32[4,3,16,16,128]{4,3,2,1,0:T(8,128)S(1)}) custom-call(f32[32,2,8,128]{3,2,1,0:T(8,128)S(1)} %weights.1.weight.refs_0_, bf16[1024,256]{1,0:T(8,128)(2,1)S(1)} %copy-done.2, bf16[256,256]{1,0:T(8,128)(2,1)S(1)} %copy-done.3, bf16[512,512]{1,0:T(8,128)(2,1)S(1)} %copy-done.1, ...), custom_call_target="tpu_custom_call" | custom-call | flops 1 | bytes 1 | tf_op jit(solution)/shard_map/inside/pallas_call | solution.py:503
  25.0 1.6 %collective-permute-start.9 = (s16[195,16,128]{2,1,0:T(8,128)(2,1)S(1)}, s16[195,16,128]{2,1,0:T(8,128)(2,1)S(1)}, u32[]{:S(2)}, u32[]{:S(2)}) collective-permute-start(s16[195,16,128]{2,1,0:T(8,128)(2,1)S(1)} %get-tuple-element.37), channel_id=1, source_target_pairs={{0,16},{8,24},{16,0},{24,8},{1,17},{9,25},{17,1},{25,9},{2,18},{10... | collective-permute-start | bytes 2396168 | tf_op jit(solution)/shard_map/ppermute | solution.py:520
  26.6 2.3 %collective-permute-start.11 = (bf16[2,16,1,2,16,256]{5,4,3,2,1,0:T(8,128)(2,1)S(1)}, bf16[2,16,1,2,16,256]{5,4,3,2,1,0:T(8,128)(2,1)S(1)}, u32[]{:S(2)}, u32[]{:S(2)}) collective-permute-start(bf16[2,16,1,2,16,256]{5,4,3,2,1,0:T(8,128)(2,1)S(1)} %get-tuple-element.42), channel_id=1, source_target_pairs={{1,2},{3,4},{5,6},{2,1},{4,3},{6,5},{9,10},{11,12},{13,14},{10,9},... | collective-permute-start | bytes 1572872 | tf_op jit(solution)/shard_map/ppermute | solution.py:559
  28.9 4.6 %collective-permute-start.8 = (bf16[4,16,2,16,128]{4,3,2,1,0:T(8,128)(2,1)S(1)}, bf16[4,16,2,16,128]{4,3,2,1,0:T(8,128)(2,1)S(1)}, u32[]{:S(2)}, u32[]{:S(2)}) collective-permute-start(bf16[4,16,2,16,128]{4,3,2,1,0:T(8,128)(2,1)S(1)} %pack.7), channel_id=1, source_target_pairs={{1,2},{3,4},{5,6},{2,1},{4,3},{6,5},{9,10},{11,12},{13,14},{10,9},... | collective-permute-start | bytes 1572872 | tf_op jit(solution)/shard_map/ppermute | solution.py:560
  33.5 3.3 %edge_near.1 = (s16[50,16,128]{2,1,0:T(8,128)(2,1)S(1)}, f32[4,3,4,16,128]{4,3,2,1,0:T(8,128)S(1)}) custom-call(f32[32,2,8,128]{3,2,1,0:T(8,128)S(1)} %weights.1.weight.refs_0_, bf16[1024,256]{1,0:T(8,128)(2,1)S(1)} %copy-done.2, bf16[256,256]{1,0:T(8,128)(2,1)S(1)} %copy-done.3, bf16[512,512]{1,0:T(8,128)(2,1)S(1)} %copy-done.1, ...), custom_call_target="tpu_custom_call" | custom-call | flops 1 | bytes 1 | tf_op jit(solution)/shard_map/edge_near/pallas_call | solution.py:514
  36.8 0.6 collective-permute-start.10
  37.3 0.6 %collective-permute-start.2 = (s32[16]{0:T(128)S(1)}, s32[16]{0:T(128)S(1)}, u32[]{:S(2)}, u32[]{:S(2)}) collective-permute-start(s32[16]{0:T(128)S(1)} %copy-done.6), channel_id=1, source_target_pairs={{0,24},{8,16},{16,8},{24,0},{1,25},{9,17},{17,9},{25,1},{2,26},{10... | collective-permute-start | bytes 200 | tf_op jit(solution)/shard_map/ppermute | solution.py:527
  37.9 7.7 %collective-permute-done.9.code.exponents = s16[195,16,128]{2,1,0:T(8,128)(2,1)S(1)} collective-permute-done((s16[195,16,128]{2,1,0:T(8,128)(2,1)S(1)}, s16[195,16,128]{2,1,0:T(8,128)(2,1)S(1)}, u32[]{:S(2)}, u32[]{:S(2)}) %collective-permute-start.9) | collective-permute-done | bytes 798752 | tf_op jit(solution)/shard_map/ppermute | solution.py:520
  45.7 1.5 %collective-permute-start.1 = (s32[16]{0:T(128)S(1)}, s32[16]{0:T(128)S(1)}, u32[]{:S(2)}, u32[]{:S(2)}) collective-permute-start(s32[16]{0:T(128)S(1)} %copy-done.6), channel_id=1, source_target_pairs={{0,16},{8,24},{16,0},{24,8},{1,17},{9,25},{17,1},{25,9},{2,18},{10... | collective-permute-start | bytes 200 | tf_op jit(solution)/shard_map/ppermute | solution.py:527
  47.2 1.9 %edge_far.1 = (s16[25,16,128]{2,1,0:T(8,128)(2,1)S(1)}, f32[4,3,2,16,128]{4,3,2,1,0:T(8,128)S(1)}) custom-call(f32[32,2,8,128]{3,2,1,0:T(8,128)S(1)} %weights.1.weight.refs_0_, bf16[1024,256]{1,0:T(8,128)(2,1)S(1)} %copy-done.2, bf16[256,256]{1,0:T(8,128)(2,1)S(1)} %copy-done.3, bf16[512,512]{1,0:T(8,128)(2,1)S(1)} %copy-done.1, ...), custom_call_target="tpu_custom_call" | custom-call | flops 1 | bytes 1 | tf_op jit(solution)/shard_map/edge_far/pallas_call | solution.py:514
  49.1 0.6 %collective-permute-start.12 = (s16[25,16,128]{2,1,0:T(8,128)(2,1)S(1)}, s16[25,16,128]{2,1,0:T(8,128)(2,1)S(1)}, u32[]{:S(2)}, u32[]{:S(2)}) collective-permute-start(s16[25,16,128]{2,1,0:T(8,128)(2,1)S(1)} %get-tuple-element.44), channel_id=1, source_target_pairs={{0,16},{8,24},{16,0},{24,8},{1,17},{9,25},{17,1},{25,9},{2,18},{10... | collective-permute-start | bytes 307208 | tf_op jit(solution)/shard_map/edge_far/ppermute | solution.py:520
  49.8 0.7 %invert.2.weight = f32[64,2,8,128]{3,2,1,0:T(8,128)S(1)} custom-call(s32[64]{0:T(128)S(1)} %pad_add_fusion.bins, f32[360]{0:T(512)S(1)} %copy-done.5), custom_call_target="tpu_custom_call" | custom-call | flops 1 | bytes 1 | tf_op jit(solution)/shard_map/invert/pallas_call | solution.py:531
  50.6 2.1 %finish.1.refs_4_ = f32[3,3,4,8,16,128]{5,4,3,2,1,0:T(8,128)} custom-call(f32[9,16,128]{2,1,0:T(8,128)S(1)} %invert.3.inverse, f32[4,3,16,16,128]{4,3,2,1,0:T(8,128)S(1)} %get-tuple-element.36.here, s16[195,16,128]{2,1,0:T(8,128)(2,1)S(1)} %collective-permute-done.9.code.exponents, s16[195,16,128]{2,1,0:T(8,128)(2,1)S(1)} %collective-permute-done.9.code.exponents), custom_call_target="tpu_custom_call" | custom-call | flops 1 | bytes 1 | tf_op jit(solution)/shard_map/finish/pallas_call | solution.py:578
  52.7 2.0 %collective-permute-done.8.halo = bf16[4,16,2,16,128]{4,3,2,1,0:T(8,128)(2,1)S(1)} collective-permute-done((bf16[4,16,2,16,128]{4,3,2,1,0:T(8,128)(2,1)S(1)}, bf16[4,16,2,16,128]{4,3,2,1,0:T(8,128)(2,1)S(1)}, u32[]{:S(2)}, u32[]{:S(2)}) %collective-permute-start.8) | collective-permute-done | bytes 524320 | tf_op jit(solution)/shard_map/ppermute | solution.py:560
  54.7 2.6 %finish_edges.1 = f32[3,3,4,8,16,128]{5,4,3,2,1,0:T(8,128)} custom-call(f32[64,2,8,128]{3,2,1,0:T(8,128)S(1)} %invert.2.weight, f32[9,16,128]{2,1,0:T(8,128)S(1)} %invert.3.inverse, bf16[512,128]{1,0:T(8,128)(2,1)S(1)} %copy-done.4, bf16[256,256]{1,0:T(8,128)(2,1)S(1)} %copy-done.3, ...), custom_call_target="tpu_custom_call", output_to_operand_aliasing={{}: (13, {})} | custom-call | flops 1 | bytes 1 | tf_op jit(solution)/shard_map/finish_edges/pallas_call | solution.py:595
  (35 shorter events, 0.7 us)
Async XLA Ops:
  0.0 10.4 %collective-permute-start.3 = (bf16[16,3,8,16,512]{4,3,2,1,0:T(8,128)(2,1)}, bf16[16,3,8,16,512]{4,3,2,1,0:T(8,128)(2,1)S(1)}, u32[]{:S(2)}, u32[]{:S(2)}) collective-permute-start(bf16[16,3,8,16,512]{4,3,2,1,0:T(8,128)(2,1)} %own.10), channel_id=1, source_target_pairs={{0,8},{8,0},{16,24},{24,16},{1,9},{9,1},{17,25},{25,17},{2,10},{10... | collective-permute-start | bytes 18874376 | tf_op jit(solution)/shard_map/ppermute | solution.py:522
  0.0 2.8 %copy-start = (bf16[16,3,8,16,512]{4,3,2,1,0:T(8,128)(2,1)S(1)}, bf16[16,3,8,16,512]{4,3,2,1,0:T(8,128)(2,1)}, u32[]{:S(2)}) copy-start(bf16[16,3,8,16,512]{4,3,2,1,0:T(8,128)(2,1)} %own.10) | copy-start | bytes 18874372
  2.9 21.9 %collective-permute-start.6 = (bf16[16,2,2,16,256]{4,3,2,1,0:T(8,128)(2,1)S(1)}, bf16[16,2,2,16,256]{4,3,2,1,0:T(8,128)(2,1)S(1)}, u32[]{:S(2)}, u32[]{:S(2)}) collective-permute-start(bf16[16,2,2,16,256]{4,3,2,1,0:T(8,128)(2,1)S(1)} %pack.4), channel_id=1, source_target_pairs={{0,1},{1,0},{2,3},{3,2},{4,5},{5,4},{6,7},{7,6},{8,9},{9,8},{10,11... | collective-permute-start | bytes 1572872 | tf_op jit(solution)/shard_map/pack/ppermute | solution.py:525
  4.7 20.2 %collective-permute-start.4 = (bf16[16,6,16,128]{3,2,1,0:T(8,128)(2,1)S(1)}, bf16[16,6,16,128]{3,2,1,0:T(8,128)(2,1)S(1)}, u32[]{:S(2)}, u32[]{:S(2)}) collective-permute-start(bf16[16,6,16,128]{3,2,1,0:T(8,128)(2,1)S(1)} %get-tuple-element.26), channel_id=1, source_target_pairs={{0,16},{8,24},{16,0},{24,8},{1,17},{9,25},{17,1},{25,9},{2,18},{10... | collective-permute-start | bytes 1179656 | tf_op jit(solution)/shard_map/pack/ppermute | solution.py:544
  6.2 7.8 %slice-start = ((s8[6291456]{0:T(1024)(128)(4,1)}), s8[4194304]{0:T(1024)(128)(4,1)S(1)}, s32[]{:S(2)}) async-start(s8[6291456]{0:T(1024)(128)(4,1)} %bitcast), calls=%async_computation | async-start | bytes 8388608
  6.2 5.9 %copy-start.6 = (s32[16]{0:T(128)S(1)}, s32[16]{0:T(128)}, u32[]{:S(2)}) copy-start(s32[16]{0:T(128)} %param.8) | copy-start | bytes 196
  6.2 7.1 %copy-start.5 = (f32[360]{0:T(512)S(1)}, f32[360]{0:T(512)}, u32[]{:S(2)}) copy-start(f32[360]{0:T(512)} %constant.10.clone.table) | copy-start | bytes 4324
  6.2 7.8 %slice-start.1 = ((s8[6291456]{0:T(1024)(128)(4,1)}), s8[2097152]{0:T(1024)(128)(4,1)S(1)}, s32[]{:S(2)}) async-start(s8[6291456]{0:T(1024)(128)(4,1)} %bitcast), calls=%async_computation.1 | async-start | bytes 4194304
  6.3 7.8 %copy-start.1 = (bf16[512,512]{1,0:T(8,128)(2,1)S(1)}, bf16[512,512]{1,0:T(8,128)(2,1)}, u32[]{:S(2)}) copy-start(bf16[512,512]{1,0:T(8,128)(2,1)} %constant.14.clone.all_z.refs_3_) | copy-start | bytes 1572868
  6.3 7.8 %copy-start.2 = (bf16[1024,256]{1,0:T(8,128)(2,1)S(1)}, bf16[1024,256]{1,0:T(8,128)(2,1)}, u32[]{:S(2)}) copy-start(bf16[1024,256]{1,0:T(8,128)(2,1)} %constant.11.clone.along_x.refs_1_) | copy-start | bytes 1572868
  6.3 7.8 %copy-start.3 = (bf16[256,256]{1,0:T(8,128)(2,1)S(1)}, bf16[256,256]{1,0:T(8,128)(2,1)}, u32[]{:S(2)}) copy-start(bf16[256,256]{1,0:T(8,128)(2,1)} %constant.13.clone.along_y.refs_2_) | copy-start | bytes 393220
  6.3 18.6 %collective-permute-start.5 = (bf16[16,6,16,128]{3,2,1,0:T(8,128)(2,1)S(1)}, bf16[16,6,16,128]{3,2,1,0:T(8,128)(2,1)S(1)}, u32[]{:S(2)}, u32[]{:S(2)}) collective-permute-start(bf16[16,6,16,128]{3,2,1,0:T(8,128)(2,1)S(1)} %get-tuple-element.27), channel_id=1, source_target_pairs={{0,24},{8,16},{16,8},{24,0},{1,25},{9,17},{17,9},{25,1},{2,26},{10... | collective-permute-start | bytes 1179656 | tf_op jit(solution)/shard_map/pack/ppermute | solution.py:545
  10.6 18.3 %collective-permute-start.7 = (bf16[16,2,2,16,256]{4,3,2,1,0:T(8,128)(2,1)S(1)}, bf16[16,2,2,16,256]{4,3,2,1,0:T(8,128)(2,1)S(1)}, u32[]{:S(2)}, u32[]{:S(2)}) collective-permute-start(bf16[16,2,2,16,256]{4,3,2,1,0:T(8,128)(2,1)S(1)} %get-tuple-element.29), channel_id=1, source_target_pairs={{0,1},{1,0},{2,3},{3,2},{4,5},{5,4},{6,7},{7,6},{8,9},{9,8},{10,11... | collective-permute-start | bytes 1572872 | tf_op jit(solution)/shard_map/pack/ppermute | solution.py:549
  12.2 1.1 %collective-permute-start = (s32[16]{0:T(128)S(1)}, s32[16]{0:T(128)S(1)}, u32[]{:S(2)}, u32[]{:S(2)}) collective-permute-start(s32[16]{0:T(128)S(1)} %copy-done.6), channel_id=1, source_target_pairs={{0,8},{8,0},{16,24},{24,16},{1,9},{9,1},{17,25},{25,17},{2,10},{10... | collective-permute-start | bytes 200 | tf_op jit(solution)/shard_map/ppermute | solution.py:526
  25.0 20.7 %collective-permute-start.9 = (s16[195,16,128]{2,1,0:T(8,128)(2,1)S(1)}, s16[195,16,128]{2,1,0:T(8,128)(2,1)S(1)}, u32[]{:S(2)}, u32[]{:S(2)}) collective-permute-start(s16[195,16,128]{2,1,0:T(8,128)(2,1)S(1)} %get-tuple-element.37), channel_id=1, source_target_pairs={{0,16},{8,24},{16,0},{24,8},{1,17},{9,25},{17,1},{25,9},{2,18},{10... | collective-permute-start | bytes 2396168 | tf_op jit(solution)/shard_map/ppermute | solution.py:520
  26.6 20.6 %collective-permute-start.11 = (bf16[2,16,1,2,16,256]{5,4,3,2,1,0:T(8,128)(2,1)S(1)}, bf16[2,16,1,2,16,256]{5,4,3,2,1,0:T(8,128)(2,1)S(1)}, u32[]{:S(2)}, u32[]{:S(2)}) collective-permute-start(bf16[2,16,1,2,16,256]{5,4,3,2,1,0:T(8,128)(2,1)S(1)} %get-tuple-element.42), channel_id=1, source_target_pairs={{1,2},{3,4},{5,6},{2,1},{4,3},{6,5},{9,10},{11,12},{13,14},{10,9},... | collective-permute-start | bytes 1572872 | tf_op jit(solution)/shard_map/ppermute | solution.py:559
  28.9 25.7 %collective-permute-start.8 = (bf16[4,16,2,16,128]{4,3,2,1,0:T(8,128)(2,1)S(1)}, bf16[4,16,2,16,128]{4,3,2,1,0:T(8,128)(2,1)S(1)}, u32[]{:S(2)}, u32[]{:S(2)}) collective-permute-start(bf16[4,16,2,16,128]{4,3,2,1,0:T(8,128)(2,1)S(1)} %pack.7), channel_id=1, source_target_pairs={{1,2},{3,4},{5,6},{2,1},{4,3},{6,5},{9,10},{11,12},{13,14},{10,9},... | collective-permute-start | bytes 1572872 | tf_op jit(solution)/shard_map/ppermute | solution.py:560
  36.8 17.9 %collective-permute-start.10 = (s16[50,16,128]{2,1,0:T(8,128)(2,1)S(1)}, s16[50,16,128]{2,1,0:T(8,128)(2,1)S(1)}, u32[]{:S(2)}, u32[]{:S(2)}) collective-permute-start(s16[50,16,128]{2,1,0:T(8,128)(2,1)S(1)} %get-tuple-element.40), channel_id=1, source_target_pairs={{0,16},{8,24},{16,0},{24,8},{1,17},{9,25},{17,1},{25,9},{2,18},{10... | collective-permute-start | bytes 614408 | tf_op jit(solution)/shard_map/edge_near/ppermute | solution.py:520
  37.3 12.3 %collective-permute-start.2 = (s32[16]{0:T(128)S(1)}, s32[16]{0:T(128)S(1)}, u32[]{:S(2)}, u32[]{:S(2)}) collective-permute-start(s32[16]{0:T(128)S(1)} %copy-done.6), channel_id=1, source_target_pairs={{0,24},{8,16},{16,8},{24,0},{1,25},{9,17},{17,9},{25,1},{2,26},{10... | collective-permute-start | bytes 200 | tf_op jit(solution)/shard_map/ppermute | solution.py:527
  45.7 4.1 %collective-permute-start.1 = (s32[16]{0:T(128)S(1)}, s32[16]{0:T(128)S(1)}, u32[]{:S(2)}, u32[]{:S(2)}) collective-permute-start(s32[16]{0:T(128)S(1)} %copy-done.6), channel_id=1, source_target_pairs={{0,16},{8,24},{16,0},{24,8},{1,17},{9,25},{17,1},{25,9},{2,18},{10... | collective-permute-start | bytes 200 | tf_op jit(solution)/shard_map/ppermute | solution.py:527
  49.1 5.6 %collective-permute-start.12 = (s16[25,16,128]{2,1,0:T(8,128)(2,1)S(1)}, s16[25,16,128]{2,1,0:T(8,128)(2,1)S(1)}, u32[]{:S(2)}, u32[]{:S(2)}) collective-permute-start(s16[25,16,128]{2,1,0:T(8,128)(2,1)S(1)} %get-tuple-element.44), channel_id=1, source_target_pairs={{0,16},{8,24},{16,0},{24,8},{1,17},{9,25},{17,1},{25,9},{2,18},{10... | collective-permute-start | bytes 307208 | tf_op jit(solution)/shard_map/edge_far/ppermute | solution.py:520
  50.6 4.1 %copy-start.4 = (bf16[512,128]{1,0:T(8,128)(2,1)S(1)}, bf16[512,128]{1,0:T(8,128)(2,1)}, u32[]{:S(2)}) copy-start(bf16[512,128]{1,0:T(8,128)(2,1)} %constant.12.clone.along_x) | copy-start | bytes 393220

commit v5 on v4

--- a/solution.py
+++ b/solution.py
@@ -30,15 +30,26 @@
     return np.stack([np.cos(centers), np.sin(centers)], axis=1).astype(np.float32)
 
 
-def weights_kernel(bins, table, weight):
+def weights_kernel(bins, table, weight, spread):
     for s in range(bins.shape[0]):
         weight[s, 0] = jnp.full(weight.shape[2:], table[bins[s] * 2], jnp.float32)
         weight[s, 1] = jnp.full(weight.shape[2:], table[bins[s] * 2 + 1], jnp.float32)
-
-
-def invert_kernel(weight, inverse):
+        spread[pl.ds(s, 1), :] = jnp.full((1, spread.shape[1]), bins[s], jnp.int32).astype(jnp.float32)
+
+
+def invert_kernel(table, pair_weight, code, weight, inverse, received, bins, sem):
+    count = pair_weight.shape[0]
+    received[...] = code[code.shape[0] - count // code.shape[1] :].astype(jnp.int32).reshape(received.shape)
+    copy = pltpu.make_async_copy(received, bins, sem)
+    copy.start()
+    weight[:count] = pair_weight[...]
+    copy.wait()
     g01 = g02 = g11 = g12 = g22 = jnp.zeros(weight.shape[2:], jnp.float32)
     for s in range(weight.shape[0]):
+        if s >= count:
+            row = bins[s - count, 0] * 2
+            weight[s, 0] = jnp.full(weight.shape[2:], table[row], jnp.float32)
+            weight[s, 1] = jnp.full(weight.shape[2:], table[row + 1], jnp.float32)
         cosine, sine = weight[s, 0], weight[s, 1]
         g01, g02 = g01 + cosine, g02 + sine
         g11, g12, g22 = g11 + cosine * cosine, g12 + cosine * sine, g22 + sine * sine
@@ -132,7 +143,7 @@
             done += 1
 
 
-def encode(sums, exponents, code, groups):
+def encode(sums, exponents, code, groups, bins=None):
     cells, rows = sums.shape[2:4]
     exponents[...] = jnp.zeros(exponents.shape, jnp.float32)
     for n in range(ORDERS * 3):
@@ -143,6 +154,8 @@
             rounded = jnp.round(value * (jnp.exp2(-exponent) * LEVELS))
             code[n * cells + start : n * cells + stop] = rounded.astype(jnp.int32).astype(jnp.int16)
             exponents[pl.ds(n * len(groups) + g, 1), :] = exponent
+    if bins is not None:
+        exponents[exponents.shape[0] - bins.shape[0] :] = bins[...]
     last = exponents[...].reshape(exponents.shape[0] // rows, rows, exponents.shape[1])
     code[ORDERS * 3 * cells :] = last.astype(jnp.int32).astype(jnp.int16)
 
@@ -208,7 +221,7 @@
     return jnp.concatenate([flat(load(block)) for block in spot.pair()], axis=1)
 
 
-def inside_kernel(weight, along_x, along_y, all_z, own, other, code, here, there, exponents, *fields):
+def inside_kernel(bins, weight, along_x, along_y, all_z, own, other, code, here, there, exponents, *fields):
     planes, rows = own.shape[2:4]
     steps = planes // 2
     spot = Spot(planes)
@@ -248,7 +261,7 @@
         )
         weave(summed(2, planes + step), streamwise(fields[0], jnp.minimum(2 * step + 2, planes - 1)))
 
-    encode(there, exponents, code, [(g * steps, g * steps + steps) for g in range(4)])
+    encode(there, exponents, code, [(g * steps, g * steps + steps) for g in range(4)], bins)
 
 
 def edge_kernel(components, near, n_halos, halo_of, weight, along_x, along_y, all_z, own, other, *refs):
@@ -302,31 +315,32 @@
         store(i, inverse[3 * i] * sums[0] + inverse[3 * i + 1] * sums[1] + inverse[3 * i + 2] * sums[2])
 
 
-def finish_kernel(inverse, here, code, exponents, out, scales):
+def finish_kernel(inverse, here, code, exponents, near_here, near_code, near_exponents, out, scales, near_scales):
     planes = out.shape[3]
     half = planes // 2
+    edge = pl.ds(Spot(planes).near.edge, 2)
 
     @pl.when(pl.program_id(0) == 0)
     def _():
         decode_scales(exponents[...], scales)
-
-    rows = scales.shape[0] // ORDERS
-    own = scales.at[pl.ds(pl.program_id(0) * rows, rows)]
-    for group in range(4):
-        cells = group * half, group * half + half
-
-        def store(i, value, group=group):
-            if group < 2:
-                out[i, 0, 0, group * half : group * half + half] = value
-            else:
-                out[i, group - 1, 0, 2 : planes - 2] = value
-
-        solve(inverse, here.at[0], code, own, cells, group, store)
-
-
-def finish_edges_kernel(weight, inverse, along_x, along_y, own, other, across, diagonal, halo, *refs):
-    near_here, near_code, far_here, far_code, _, out, near_out, far_out = refs[:8]
-    near_scales, far_scales, *fields, out_sems = refs[8:]
+        decode_scales(near_exponents[...], near_scales)
+
+    inner = slice(2, planes - 2)
+    targets = [(0, slice(0, half)), (0, slice(half, planes)), (1, inner), (2, inner), (2, edge), (1, edge)]
+    for n, (component, at) in enumerate(targets):
+        def store(i, value, component=component, at=at):
+            out[i, component, 0, at] = value
+
+        if n < 4:
+            own = scales.at[pl.ds(pl.program_id(0) * 12, 12)]
+            solve(inverse, here.at[0], code, own, (n * half, n * half + half), n, store)
+        else:
+            own = near_scales.at[pl.ds(pl.program_id(0) * 6, 6)]
+            solve(inverse, near_here.at[0], near_code, own, (2 * n - 8, 2 * n - 6), n - 4, store)
+
+
+def finish_far_kernel(weight, inverse, along_x, along_y, own, other, across, diagonal, halo, *refs):
+    far_here, far_code, _, out, far_out, far_scales, *fields, out_sem = refs
     rows = own.shape[3]
     spot = Spot(own.shape[2])
     side, lane_here = spot.far, spot.lanes(spot.here)
@@ -345,13 +359,6 @@
         return fill_z(fields[p], along_x, along_y, u, around)
 
     def solve_order(k):
-        for c in range(2):
-            def store_near(i, value, c=c):
-                near_out[i, c, k] = value
-
-            cells, scales = (2 - 2 * c, 4 - 2 * c), near_scales.at[pl.ds(6 * k, 6)]
-            solve(inverse, near_here.at[k], near_code.at[pl.ds(12 * k, 12)], scales, cells, 1 - c, store_near)
-
         def store_far(i, value):
             far_out[i, 0, k] = value
 
@@ -370,23 +377,14 @@
 
         power_sums(fields[p], weight, 0, half, rows, store)
 
-    decode_scales(near_code[ORDERS * 12 :], near_scales)
     decode_scales(far_code[ORDERS * 6 :], far_scales)
     weave([lambda k=k: solve_order(k) for k in range(ORDERS)], fill(0))
-    near_copy, far_copy = make_copies(
-        [
-            (near_out, out.at[:, pl.ds(1, 2), :, pl.ds(spot.near.edge, 2)]),
-            (far_out, out.at[:, pl.ds(1, 2), :, pl.ds(spot.far.edge, 2)]),
-        ],
-        out_sems,
-    )
-    near_copy.start()
     weave([lambda half=half: sum_half(0, half) for half in range(rows // 8)], fill(1))
     for half in range(rows // 8):
         sum_half(1, half)
-    far_copy.start()
-    near_copy.wait()
-    far_copy.wait()
+    copy = pltpu.make_async_copy(far_out, out.at[:, pl.ds(1, 2), :, pl.ds(side.edge, 2)], out_sem)
+    copy.start()
+    copy.wait()
 
 
 def pack_near_kernel(own, near, sems):
@@ -470,14 +468,14 @@
     chip_pairs = [(i, (i + 2) % n_snap) for i in range(n_snap)]
     diagonal_pairs = [(i, ((i + 2) % n_snap) ^ 1) for i in range(n_snap)]
 
-    def pack(kernel, arrays, shapes, copies):
+    def pack(kernel, arrays, shapes, copies, megabytes=8):
         return pl.pallas_call(
             kernel,
             in_specs=[hbm()] * len(arrays),
             out_specs=[vmem()] * len(shapes),
             out_shape=[jax.ShapeDtypeStruct(shape, kind) for shape in shapes],
             scratch_shapes=[pltpu.SemaphoreType.DMA((copies,))],
-            **params(8),
+            **params(megabytes),
         )(*arrays)
 
     near_shape, far_shape = (snaps, 2, 2, rows, pair), (2, snaps, 1, 2, rows, pair)
@@ -488,9 +486,9 @@
     along_z = jnp.asarray(band(lanes).T, jnp.bfloat16)
     field = pltpu.VMEM((2 * size, pair), jnp.float32)
 
-    def sums(cells, groups):
+    def sums(cells, groups, extra=0):
         shape = (ORDERS, 3, cells, rows, width)
-        last = -(-ORDERS * 3 * groups // rows)
+        last = -(-(ORDERS * 3 * groups + extra) // rows)
         return {
             "out_shape": [
                 jax.ShapeDtypeStruct((ORDERS * 3 * cells + last, rows, width), jnp.int16),
@@ -499,10 +497,12 @@
         }, [pltpu.VMEM(shape, jnp.float32), pltpu.VMEM((last * rows, width), jnp.float32)]
 
     def inside_sums(weights):
-        call, scratch = sums(2 * planes, 4)
+        call, scratch = sums(2 * planes, 4, 2 * snaps)
         return pl.pallas_call(
-            inside_kernel, scratch_shapes=[*scratch, field, field, field, field], **call, **params(26)
-        )(weights, along_x, along_y, along_z, velocity, other)
+            inside_kernel,
+            scratch_shapes=[*scratch, field, field, field, field],
+            **call, **params(26),
+        )(spread_bins, weights, along_x, along_y, along_z, velocity, other)
 
     def edge_sums(weights, components, near, halos, halo_of):
         count = len(components)
@@ -521,22 +521,20 @@
 
     other = lax.ppermute(velocity, "snap", core_pairs)
     with jax.named_scope("pack"):
-        (near_own,) = pack(pack_near_kernel, (velocity,), [near_shape], 2)
+        (near_own,) = pack(pack_near_kernel, (velocity,), [near_shape], 2, 51)
         halo_own = lax.ppermute(near_own, "slab", near_pairs)
     pair_bins = jnp.concatenate([phase_bins, lax.ppermute(phase_bins, "snap", core_pairs)])
-    chip_bins = [lax.ppermute(phase_bins, "snap", pairs) for pairs in (chip_pairs, diagonal_pairs)]
-    all_bins = jnp.concatenate([pair_bins, *chip_bins])
-
-    def spread(bins):
-        return pl.pallas_call(
+
+    with jax.named_scope("weights"):
+        pair_weights, spread_bins = pl.pallas_call(
             weights_kernel,
             in_specs=[smem(), smem()],
-            out_shape=jax.ShapeDtypeStruct((bins.shape[0], 2, 8, 128), jnp.float32),
+            out_shape=[
+                jax.ShapeDtypeStruct((2 * snaps, 2, 8, 128), jnp.float32),
+                jax.ShapeDtypeStruct((2 * snaps, width), jnp.float32),
+            ],
             **params(8),
-        )(bins, table)
-
-    with jax.named_scope("weights"):
-        pair_weights = spread(pair_bins)
+        )(pair_bins, table)
     with jax.named_scope("pack"):
         for_across, for_diagonal = pack(
             pack_across_kernel, (after(velocity, near_own),), [(snaps, 6, rows, width)] * 2, 4
@@ -562,18 +560,37 @@
     with jax.named_scope("edge_near"):
         near = exchange(edge_sums(pair_weights, (1, 2), True, (halo_own, halo_other), lambda halos, g: halos[g]))
     with jax.named_scope("edge_far"):
-        ready = after(pair_weights, inside[1])
+        ready = pair_weights
         far_y = exchange(edge_sums(ready, (2,), False, (halo_w,), lambda halos, g: halos[0].at[g]))
 
     with jax.named_scope("invert"):
-        weights = spread(after(all_bins, inside_parts[0]))
-        inverse = pl.pallas_call(
-            invert_kernel, out_shape=jax.ShapeDtypeStruct((9, rows, width), jnp.float32), **params(8)
-        )(weights)
+        weights, inverse = pl.pallas_call(
+            invert_kernel,
+            in_specs=[smem(), vmem(), vmem()],
+            out_shape=[
+                jax.ShapeDtypeStruct((4 * snaps, 2, 8, 128), jnp.float32),
+                jax.ShapeDtypeStruct((9, rows, width), jnp.float32),
+            ],
+            scratch_shapes=[
+                pltpu.VMEM((2 * snaps, width), jnp.int32),
+                pltpu.SMEM((2 * snaps, width), jnp.int32),
+                pltpu.SemaphoreType.DMA,
+            ],
+            **params(8),
+        )(table, pair_weights, inside[1])
 
     out_shape = jax.ShapeDtypeStruct((3, 3, ORDERS, planes, rows, width), jnp.float32)
 
-    last = 3
+    lasts = 3, 2
+
+    def one_order(parts, last):
+        cells = parts[0].shape[2]
+        return [
+            pl.BlockSpec((1, 3, cells, rows, width), lambda p: (p, 0, 0, 0, 0)),
+            pl.BlockSpec((3 * cells, rows, width), lambda p: (p, 0, 0)),
+            pl.BlockSpec((last, rows, width), lambda p: (ORDERS * 3 * cells // last, 0, 0)),
+        ]
+
     with jax.named_scope("finish"):
         out = pl.pallas_call(
             finish_kernel,
@@ -581,35 +598,32 @@
             grid=(ORDERS,),
             in_specs=[
                 pl.BlockSpec((9, rows, width), lambda p: (0, 0, 0)),
-                pl.BlockSpec((1, 3, 2 * planes, rows, width), lambda p: (p, 0, 0, 0, 0)),
-                pl.BlockSpec((6 * planes, rows, width), lambda p: (p, 0, 0)),
-                pl.BlockSpec((last, rows, width), lambda p: (ORDERS * 6 * planes // last, 0, 0)),
+                *one_order(inside, lasts[0]), *one_order(near, lasts[1]),
             ],
             out_specs=pl.BlockSpec((3, 3, 1, planes, rows, width), lambda p: (0, 0, p, 0, 0, 0)),
-            scratch_shapes=[pltpu.VMEM((last * rows, width), jnp.float32)],
+            scratch_shapes=[pltpu.VMEM((last * rows, width), jnp.float32) for last in lasts],
             **params(16),
-        )(inverse, *inside, inside[1])
-
-    with jax.named_scope("finish_edges"):
+        )(inverse, *inside, inside[1], *near, near[1])
+
+    with jax.named_scope("finish_far"):
         edges = pltpu.VMEM((3, 2, ORDERS, 2, rows, width), jnp.float32)
         return pl.pallas_call(
-            finish_edges_kernel,
+            finish_far_kernel,
             out_shape=out_shape,
-            in_specs=[vmem()] * 13 + [hbm()],
+            in_specs=[vmem()] * 11 + [hbm()],
             out_specs=hbm(),
             scratch_shapes=[
-                edges, edges,
-                pltpu.VMEM((2 * rows, width), jnp.float32),
+                edges,
                 pltpu.VMEM((rows, width), jnp.float32),
                 pltpu.VMEM((4 * size, width), jnp.float32),
                 pltpu.VMEM((4 * size, width), jnp.float32),
-                pltpu.SemaphoreType.DMA((2,)),
+                pltpu.SemaphoreType.DMA,
             ],
-            input_output_aliases={13: 0},
+            input_output_aliases={11: 0},
             **params(26),
         )(
             weights, inverse, along_x_half, along_y, velocity, other, across, diagonal,
-            after(halo_v, out), *near, *far_y, out,
+            after(halo_v, out), *far_y, out,
         )
 
 

time: 58.2 us -> 57.2 us (0.983)
  waiting for transfers between devices: 14.9 us -> 18 us
  local copies, waits for them, and re-layouts: 2.83 us -> 0.18 us
  starting transfers between devices: 16.6 us -> 14.3 us
  Pallas kernels: 22.6 us -> 24.3 us
    ppermute x1, waiting for transfers between devices: 0.01 us -> 6.91 us  [local(): halo_w = lax.ppermute(after(far_w, inside_parts[0]), 'slab', far_pairs)]
    ppermute x3, waiting for transfers between devices: 7.74 us -> 2.19 us  [exchange(): return (here, lax.ppermute(code, 'snap', chip_pairs))]
    unnamed x18 -> x14, local copies, waits for them, and re-layouts: 2.83 us -> 0.18 us
    ppermute x2 -> x0, starting transfers between devices: 2.1 us -> none  [local(): lax.ppermute(phase_bins, 'snap', pairs)]
    ppermute x1, waiting for transfers between devices: 3.96 us -> 5.52 us  [local(): other = lax.ppermute(velocity, 'snap', core_pairs)]
    pallas_call x4, Pallas kernels: 0.67 us -> 1.8 us  [pack(): pl.pallas_call(kernel, in_specs=[hbm()] * len(arrays), out_specs=[vmem()]...]
    pallas_call x4 -> x3, Pallas kernels: 3.97 us -> 4.45 us  [the longest x1 2.38 us: local(): pl.pallas_call(finish_far_kernel, out_shape=out_shape, in_specs=[vmem()]...]
  transfers between devices with their start and end apart: 13 -> 11, of which waited for: 5 -> 5; matrix products, arithmetic and copies ran while one was open for 0% -> 0% of each run, Pallas kernels for 35% -> 38%
where the time goes in v5:
time: 57.2 us; the launch traced here: 57 us
  Pallas kernels  24.3 us (42%)
  waiting for transfers between devices  18 us (31%)
  starting transfers between devices  14.3 us (25%)
    pallas_call x1, Pallas kernels, inside_sums(): pl.pallas_call(inside_kernel, scratch_shapes=[*scratch, field, field, fie...  10.8 us
    ppermute x1, waiting for transfers between devices, local(): halo_w = lax.ppermute(after(far_w, inside_parts[0]), 'slab', far_pairs)  6.91 us
    ppermute x1, waiting for transfers between devices, local(): other = lax.ppermute(velocity, 'snap', core_pairs)  5.52 us
    pallas_call x2, Pallas kernels, edge_sums(): pl.pallas_call(body, scratch_shapes=[*scratch, field, field], **call, **p...  5.12 us
    ppermute x1, starting transfers between devices, local(): halo_v = lax.ppermute(after(far_v, halo_other), 'slab', far_pairs)  4.41 us
    ppermute x3, starting transfers between devices, exchange(): return (here, lax.ppermute(code, 'snap', chip_pairs))  2.78 us
    pallas_call x1, Pallas kernels, local(): pl.pallas_call(finish_far_kernel, out_shape=out_shape, in_specs=[vmem()]...  2.38 us
    ppermute x1, starting transfers between devices, local(): halo_w = lax.ppermute(after(far_w, inside_parts[0]), 'slab', far_pairs)  2.32 us
  transfers between devices with their start and end apart: 11, of which 5 were waited for; matrix products, arithmetic and copies ran while one was open for 0% of the time, Pallas kernels for 38%

profile of v5, /device:TPU:16, one launch (start us, length us, event | category | flops | bytes accessed | tf_op | source)
XLA Modules:
  0.0 57.0 jit_solution(8676624349923100885)
XLA Ops:
  0.0 1.2 %pack.4 = bf16[16,2,2,16,256]{4,3,2,1,0:T(8,128)(2,1)S(1)} custom-call(bf16[16,3,8,16,512]{4,3,2,1,0:T(8,128)(2,1)} %own.10), custom_call_target="tpu_custom_call" | custom-call | flops 1 | bytes 1 | tf_op jit(solution)/shard_map/pack/pallas_call | solution.py:472
  1.2 1.6 %collective-permute-start.2 = (bf16[16,2,2,16,256]{4,3,2,1,0:T(8,128)(2,1)S(1)}, bf16[16,2,2,16,256]{4,3,2,1,0:T(8,128)(2,1)S(1)}, u32[]{:S(2)}, u32[]{:S(2)}) collective-permute-start(bf16[16,2,2,16,256]{4,3,2,1,0:T(8,128)(2,1)S(1)} %pack.4), channel_id=1, source_target_pairs={{0,1},{1,0},{2,3},{3,2},{4,5},{5,4},{6,7},{7,6},{8,9},{9,8},{10,11... | collective-permute-start | bytes 1572872 | tf_op jit(solution)/shard_map/pack/ppermute | solution.py:525
  2.8 0.2 copy-done
  3.0 0.2 pack.5
  3.1 1.6 %collective-permute-start.3 = (bf16[16,6,16,128]{3,2,1,0:T(8,128)(2,1)S(1)}, bf16[16,6,16,128]{3,2,1,0:T(8,128)(2,1)S(1)}, u32[]{:S(2)}, u32[]{:S(2)}) collective-permute-start(bf16[16,6,16,128]{3,2,1,0:T(8,128)(2,1)S(1)} %get-tuple-element.30), channel_id=1, source_target_pairs={{0,16},{8,24},{16,0},{24,8},{1,17},{9,25},{17,1},{25,9},{2,18},{10... | collective-permute-start | bytes 1179656 | tf_op jit(solution)/shard_map/pack/ppermute | solution.py:542
  4.9 5.5 %collective-permute-done.1.other.refs_5_ = bf16[16,3,8,16,512]{4,3,2,1,0:T(8,128)(2,1)S(1)} collective-permute-done((bf16[16,3,8,16,512]{4,3,2,1,0:T(8,128)(2,1)}, bf16[16,3,8,16,512]{4,3,2,1,0:T(8,128)(2,1)S(1)}, u32[]{:S(2)}, u32[]{:S(2)}) %collective-permute-start.1) | collective-permute-done | bytes 6291488 | tf_op jit(solution)/shard_map/ppermute | solution.py:522
  10.4 0.3 pack.6
  10.6 1.6 %collective-permute-start.6 = (bf16[16,2,2,16,256]{4,3,2,1,0:T(8,128)(2,1)S(1)}, bf16[16,2,2,16,256]{4,3,2,1,0:T(8,128)(2,1)S(1)}, u32[]{:S(2)}, u32[]{:S(2)}) collective-permute-start(bf16[16,2,2,16,256]{4,3,2,1,0:T(8,128)(2,1)S(1)} %get-tuple-element.33), channel_id=1, source_target_pairs={{0,1},{1,0},{2,3},{3,2},{4,5},{5,4},{6,7},{7,6},{8,9},{9,8},{10,11... | collective-permute-start | bytes 1572872 | tf_op jit(solution)/shard_map/pack/ppermute | solution.py:547
  12.2 1.1 %collective-permute-done = s32[16]{0:T(128)S(1)} collective-permute-done((s32[16]{0:T(128)S(1)}, s32[16]{0:T(128)S(1)}, u32[]{:S(2)}, u32[]{:S(2)}) %collective-permute-start) | collective-permute-done | bytes 96 | tf_op jit(solution)/shard_map/ppermute | solution.py:526
  13.4 0.6 %weights.1 = (f32[32,2,8,128]{3,2,1,0:T(8,128)S(1)}, f32[32,128]{1,0:T(8,128)S(1)}) custom-call(s32[32]{0:T(128)S(1)} %pad_add_fusion.bins, f32[360]{0:T(512)S(1)} %copy-done.5), custom_call_target="tpu_custom_call" | custom-call | flops 1 | bytes 1 | tf_op jit(solution)/shard_map/weights/pallas_call | solution.py:529
  14.0 10.8 %inside.1 = (s16[197,16,128]{2,1,0:T(8,128)(2,1)S(1)}, f32[4,3,16,16,128]{4,3,2,1,0:T(8,128)S(1)}) custom-call(f32[32,128]{1,0:T(8,128)S(1)} %get-tuple-element.28.bins, f32[32,2,8,128]{3,2,1,0:T(8,128)S(1)} %get-tuple-element.35.weight.pair_weight.refs_0_, bf16[1024,256]{1,0:T(8,128)(2,1)S(1)} %copy-done.2, bf16[256,256]{1,0:T(8,128)(2,1)S(1)} %copy-done.3, ...), custom_call_target="tpu_custom_call" | custom-call | flops 1 | bytes 1 | tf_op jit(solution)/shard_map/inside/pallas_call | solution.py:501
  25.0 1.6 %collective-permute-start.5 = (s16[197,16,128]{2,1,0:T(8,128)(2,1)S(1)}, s16[197,16,128]{2,1,0:T(8,128)(2,1)S(1)}, u32[]{:S(2)}, u32[]{:S(2)}) collective-permute-start(s16[197,16,128]{2,1,0:T(8,128)(2,1)S(1)} %get-tuple-element.38), channel_id=1, source_target_pairs={{0,16},{8,24},{16,0},{24,8},{1,17},{9,25},{17,1},{25,9},{2,18},{10... | collective-permute-start | bytes 2420744 | tf_op jit(solution)/shard_map/ppermute | solution.py:520
  26.5 2.3 %collective-permute-start.9 = (bf16[2,16,1,2,16,256]{5,4,3,2,1,0:T(8,128)(2,1)S(1)}, bf16[2,16,1,2,16,256]{5,4,3,2,1,0:T(8,128)(2,1)S(1)}, u32[]{:S(2)}, u32[]{:S(2)}) collective-permute-start(bf16[2,16,1,2,16,256]{5,4,3,2,1,0:T(8,128)(2,1)S(1)} %get-tuple-element.46), channel_id=1, source_target_pairs={{1,2},{3,4},{5,6},{2,1},{4,3},{6,5},{9,10},{11,12},{13,14},{10,9},... | collective-permute-start | bytes 1572872 | tf_op jit(solution)/shard_map/ppermute | solution.py:557
  28.9 4.4 %collective-permute-start.7 = (bf16[4,16,2,16,128]{4,3,2,1,0:T(8,128)(2,1)S(1)}, bf16[4,16,2,16,128]{4,3,2,1,0:T(8,128)(2,1)S(1)}, u32[]{:S(2)}, u32[]{:S(2)}) collective-permute-start(bf16[4,16,2,16,128]{4,3,2,1,0:T(8,128)(2,1)S(1)} %pack.7), channel_id=1, source_target_pairs={{1,2},{3,4},{5,6},{2,1},{4,3},{6,5},{9,10},{11,12},{13,14},{10,9},... | collective-permute-start | bytes 1572872 | tf_op jit(solution)/shard_map/ppermute | solution.py:558
  33.3 3.3 %edge_near.1 = (s16[50,16,128]{2,1,0:T(8,128)(2,1)S(1)}, f32[4,3,4,16,128]{4,3,2,1,0:T(8,128)S(1)}) custom-call(f32[32,2,8,128]{3,2,1,0:T(8,128)S(1)} %get-tuple-element.35.weight.pair_weight.refs_0_, bf16[1024,256]{1,0:T(8,128)(2,1)S(1)} %copy-done.2, bf16[256,256]{1,0:T(8,128)(2,1)S(1)} %copy-done.3, bf16[512,512]{1,0:T(8,128)(2,1)S(1)} %copy-done.1, ...), custom_call_target="tpu_custom_call" | custom-call | flops 1 | bytes 1 | tf_op jit(solution)/shard_map/edge_near/pallas_call | solution.py:514
  36.6 0.6 %collective-permute-start.8 = (s16[50,16,128]{2,1,0:T(8,128)(2,1)S(1)}, s16[50,16,128]{2,1,0:T(8,128)(2,1)S(1)}, u32[]{:S(2)}, u32[]{:S(2)}) collective-permute-start(s16[50,16,128]{2,1,0:T(8,128)(2,1)S(1)} %get-tuple-element.44), channel_id=1, source_target_pairs={{0,16},{8,24},{16,0},{24,8},{1,17},{9,25},{17,1},{25,9},{2,18},{10... | collective-permute-start | bytes 614408 | tf_op jit(solution)/shard_map/edge_near/ppermute | solution.py:520
  37.2 6.9 %collective-permute-done.9.refs_6_ = bf16[2,16,1,2,16,256]{5,4,3,2,1,0:T(8,128)(2,1)S(1)} collective-permute-done((bf16[2,16,1,2,16,256]{5,4,3,2,1,0:T(8,128)(2,1)S(1)}, bf16[2,16,1,2,16,256]{5,4,3,2,1,0:T(8,128)(2,1)S(1)}, u32[]{:S(2)}, u32[]{:S(2)}) %collective-permute-start.9) | collective-permute-done | bytes 524320 | tf_op jit(solution)/shard_map/ppermute | solution.py:557
  44.1 1.9 %edge_far.1 = (s16[25,16,128]{2,1,0:T(8,128)(2,1)S(1)}, f32[4,3,2,16,128]{4,3,2,1,0:T(8,128)S(1)}) custom-call(f32[32,2,8,128]{3,2,1,0:T(8,128)S(1)} %get-tuple-element.35.weight.pair_weight.refs_0_, bf16[1024,256]{1,0:T(8,128)(2,1)S(1)} %copy-done.2, bf16[256,256]{1,0:T(8,128)(2,1)S(1)} %copy-done.3, bf16[512,512]{1,0:T(8,128)(2,1)S(1)} %copy-done.1, ...), custom_call_target="tpu_custom_call" | custom-call | flops 1 | bytes 1 | tf_op jit(solution)/shard_map/edge_far/pallas_call | solution.py:514
  45.9 0.6 %collective-permute-start.10 = (s16[25,16,128]{2,1,0:T(8,128)(2,1)S(1)}, s16[25,16,128]{2,1,0:T(8,128)(2,1)S(1)}, u32[]{:S(2)}, u32[]{:S(2)}) collective-permute-start(s16[25,16,128]{2,1,0:T(8,128)(2,1)S(1)} %get-tuple-element.48), channel_id=1, source_target_pairs={{0,16},{8,24},{16,0},{24,8},{1,17},{9,25},{17,1},{25,9},{2,18},{10... | collective-permute-start | bytes 307208 | tf_op jit(solution)/shard_map/edge_far/ppermute | solution.py:520
  46.6 1.5 %invert.1 = (f32[64,2,8,128]{3,2,1,0:T(8,128)S(1)}, f32[9,16,128]{2,1,0:T(8,128)S(1)}) custom-call(f32[360]{0:T(512)S(1)} %copy-done.5, f32[32,2,8,128]{3,2,1,0:T(8,128)S(1)} %get-tuple-element.35.weight.pair_weight.refs_0_, s16[197,16,128]{2,1,0:T(8,128)(2,1)S(1)} %collective-permute-done.5.code.exponents), custom_call_target="tpu_custom_call" | custom-call | flops 1 | bytes 1 | tf_op jit(solution)/shard_map/invert/pallas_call | solution.py:567
  48.0 2.2 %collective-permute-done.8.near_code.near_exponents = s16[50,16,128]{2,1,0:T(8,128)(2,1)S(1)} collective-permute-done((s16[50,16,128]{2,1,0:T(8,128)(2,1)S(1)}, s16[50,16,128]{2,1,0:T(8,128)(2,1)S(1)}, u32[]{:S(2)}, u32[]{:S(2)}) %collective-permute-start.8) | collective-permute-done | bytes 204832 | tf_op jit(solution)/shard_map/edge_near/ppermute | solution.py:520
  50.2 2.1 %finish.1.refs_2_ = f32[3,3,4,8,16,128]{5,4,3,2,1,0:T(8,128)} custom-call(f32[9,16,128]{2,1,0:T(8,128)S(1)} %get-tuple-element.40.inverse, f32[4,3,16,16,128]{4,3,2,1,0:T(8,128)S(1)} %get-tuple-element.42.here, s16[197,16,128]{2,1,0:T(8,128)(2,1)S(1)} %collective-permute-done.5.code.exponents, ...), custom_call_target="tpu_custom_call" | custom-call | flops 1 | bytes 1 | tf_op jit(solution)/shard_map/finish/pallas_call | solution.py:595
  52.4 2.3 %collective-permute-done.7.halo = bf16[4,16,2,16,128]{4,3,2,1,0:T(8,128)(2,1)S(1)} collective-permute-done((bf16[4,16,2,16,128]{4,3,2,1,0:T(8,128)(2,1)S(1)}, bf16[4,16,2,16,128]{4,3,2,1,0:T(8,128)(2,1)S(1)}, u32[]{:S(2)}, u32[]{:S(2)}) %collective-permute-start.7) | collective-permute-done | bytes 524320 | tf_op jit(solution)/shard_map/ppermute | solution.py:558
  54.6 2.4 %finish_far.1 = f32[3,3,4,8,16,128]{5,4,3,2,1,0:T(8,128)} custom-call(f32[64,2,8,128]{3,2,1,0:T(8,128)S(1)} %get-tuple-element.39.weight, f32[9,16,128]{2,1,0:T(8,128)S(1)} %get-tuple-element.40.inverse, bf16[512,128]{1,0:T(8,128)(2,1)S(1)} %copy-done.4, bf16[256,256]{1,0:T(8,128)(2,1)S(1)} %copy-done.3, ...), custom_call_target="tpu_custom_call", output_to_operand_aliasing={{}: (11, {})} | custom-call | flops 1 | bytes 1 | tf_op jit(solution)/shard_map/finish_far/pallas_call | solution.py:610
  (24 shorter events, 0.3 us)
Async XLA Ops:
  0.0 3.0 %copy-start = (bf16[16,3,8,16,512]{4,3,2,1,0:T(8,128)(2,1)S(1)}, bf16[16,3,8,16,512]{4,3,2,1,0:T(8,128)(2,1)}, u32[]{:S(2)}) copy-start(bf16[16,3,8,16,512]{4,3,2,1,0:T(8,128)(2,1)} %own.10) | copy-start | bytes 18874372
  0.0 10.4 %collective-permute-start.1 = (bf16[16,3,8,16,512]{4,3,2,1,0:T(8,128)(2,1)}, bf16[16,3,8,16,512]{4,3,2,1,0:T(8,128)(2,1)S(1)}, u32[]{:S(2)}, u32[]{:S(2)}) collective-permute-start(bf16[16,3,8,16,512]{4,3,2,1,0:T(8,128)(2,1)} %own.10), channel_id=1, source_target_pairs={{0,8},{8,0},{16,24},{24,16},{1,9},{9,1},{17,25},{25,17},{2,10},{10... | collective-permute-start | bytes 18874376 | tf_op jit(solution)/shard_map/ppermute | solution.py:522
  1.2 23.6 %collective-permute-start.2 = (bf16[16,2,2,16,256]{4,3,2,1,0:T(8,128)(2,1)S(1)}, bf16[16,2,2,16,256]{4,3,2,1,0:T(8,128)(2,1)S(1)}, u32[]{:S(2)}, u32[]{:S(2)}) collective-permute-start(bf16[16,2,2,16,256]{4,3,2,1,0:T(8,128)(2,1)S(1)} %pack.4), channel_id=1, source_target_pairs={{0,1},{1,0},{2,3},{3,2},{4,5},{5,4},{6,7},{7,6},{8,9},{9,8},{10,11... | collective-permute-start | bytes 1572872 | tf_op jit(solution)/shard_map/pack/ppermute | solution.py:525
  3.1 21.7 %collective-permute-start.3 = (bf16[16,6,16,128]{3,2,1,0:T(8,128)(2,1)S(1)}, bf16[16,6,16,128]{3,2,1,0:T(8,128)(2,1)S(1)}, u32[]{:S(2)}, u32[]{:S(2)}) collective-permute-start(bf16[16,6,16,128]{3,2,1,0:T(8,128)(2,1)S(1)} %get-tuple-element.30), channel_id=1, source_target_pairs={{0,16},{8,24},{16,0},{24,8},{1,17},{9,25},{17,1},{25,9},{2,18},{10... | collective-permute-start | bytes 1179656 | tf_op jit(solution)/shard_map/pack/ppermute | solution.py:542
  4.7 7.5 %copy-start.6 = (s32[16]{0:T(128)S(1)}, s32[16]{0:T(128)}, u32[]{:S(2)}) copy-start(s32[16]{0:T(128)} %param.8) | copy-start | bytes 196
  4.7 8.7 %copy-start.5 = (f32[360]{0:T(512)S(1)}, f32[360]{0:T(512)}, u32[]{:S(2)}) copy-start(f32[360]{0:T(512)} %constant.10.clone.table) | copy-start | bytes 4324
  4.7 9.3 %copy-start.1 = (bf16[512,512]{1,0:T(8,128)(2,1)S(1)}, bf16[512,512]{1,0:T(8,128)(2,1)}, u32[]{:S(2)}) copy-start(bf16[512,512]{1,0:T(8,128)(2,1)} %constant.14.clone.all_z.refs_3_) | copy-start | bytes 1572868
  4.7 9.3 %copy-start.2 = (bf16[1024,256]{1,0:T(8,128)(2,1)S(1)}, bf16[1024,256]{1,0:T(8,128)(2,1)}, u32[]{:S(2)}) copy-start(bf16[1024,256]{1,0:T(8,128)(2,1)} %constant.11.clone.along_x.refs_1_) | copy-start | bytes 1572868
  4.7 9.3 %copy-start.3 = (bf16[256,256]{1,0:T(8,128)(2,1)S(1)}, bf16[256,256]{1,0:T(8,128)(2,1)}, u32[]{:S(2)}) copy-start(bf16[256,256]{1,0:T(8,128)(2,1)} %constant.13.clone.along_y.refs_2_) | copy-start | bytes 393220
  4.8 20.1 %collective-permute-start.4 = (bf16[16,6,16,128]{3,2,1,0:T(8,128)(2,1)S(1)}, bf16[16,6,16,128]{3,2,1,0:T(8,128)(2,1)S(1)}, u32[]{:S(2)}, u32[]{:S(2)}) collective-permute-start(bf16[16,6,16,128]{3,2,1,0:T(8,128)(2,1)S(1)} %get-tuple-element.31), channel_id=1, source_target_pairs={{0,24},{8,16},{16,8},{24,0},{1,25},{9,17},{17,9},{25,1},{2,26},{10... | collective-permute-start | bytes 1179656 | tf_op jit(solution)/shard_map/pack/ppermute | solution.py:543
  10.6 18.2 %collective-permute-start.6 = (bf16[16,2,2,16,256]{4,3,2,1,0:T(8,128)(2,1)S(1)}, bf16[16,2,2,16,256]{4,3,2,1,0:T(8,128)(2,1)S(1)}, u32[]{:S(2)}, u32[]{:S(2)}) collective-permute-start(bf16[16,2,2,16,256]{4,3,2,1,0:T(8,128)(2,1)S(1)} %get-tuple-element.33), channel_id=1, source_target_pairs={{0,1},{1,0},{2,3},{3,2},{4,5},{5,4},{6,7},{7,6},{8,9},{9,8},{10,11... | collective-permute-start | bytes 1572872 | tf_op jit(solution)/shard_map/pack/ppermute | solution.py:547
  12.2 1.1 %collective-permute-start = (s32[16]{0:T(128)S(1)}, s32[16]{0:T(128)S(1)}, u32[]{:S(2)}, u32[]{:S(2)}) collective-permute-start(s32[16]{0:T(128)S(1)} %copy-done.6), channel_id=1, source_target_pairs={{0,8},{8,0},{16,24},{24,16},{1,9},{9,1},{17,25},{25,17},{2,10},{10... | collective-permute-start | bytes 200 | tf_op jit(solution)/shard_map/ppermute | solution.py:526
  25.0 21.6 %collective-permute-start.5 = (s16[197,16,128]{2,1,0:T(8,128)(2,1)S(1)}, s16[197,16,128]{2,1,0:T(8,128)(2,1)S(1)}, u32[]{:S(2)}, u32[]{:S(2)}) collective-permute-start(s16[197,16,128]{2,1,0:T(8,128)(2,1)S(1)} %get-tuple-element.38), channel_id=1, source_target_pairs={{0,16},{8,24},{16,0},{24,8},{1,17},{9,25},{17,1},{25,9},{2,18},{10... | collective-permute-start | bytes 2420744 | tf_op jit(solution)/shard_map/ppermute | solution.py:520
  26.5 17.5 %collective-permute-start.9 = (bf16[2,16,1,2,16,256]{5,4,3,2,1,0:T(8,128)(2,1)S(1)}, bf16[2,16,1,2,16,256]{5,4,3,2,1,0:T(8,128)(2,1)S(1)}, u32[]{:S(2)}, u32[]{:S(2)}) collective-permute-start(bf16[2,16,1,2,16,256]{5,4,3,2,1,0:T(8,128)(2,1)S(1)} %get-tuple-element.46), channel_id=1, source_target_pairs={{1,2},{3,4},{5,6},{2,1},{4,3},{6,5},{9,10},{11,12},{13,14},{10,9},... | collective-permute-start | bytes 1572872 | tf_op jit(solution)/shard_map/ppermute | solution.py:557
  28.9 25.7 %collective-permute-start.7 = (bf16[4,16,2,16,128]{4,3,2,1,0:T(8,128)(2,1)S(1)}, bf16[4,16,2,16,128]{4,3,2,1,0:T(8,128)(2,1)S(1)}, u32[]{:S(2)}, u32[]{:S(2)}) collective-permute-start(bf16[4,16,2,16,128]{4,3,2,1,0:T(8,128)(2,1)S(1)} %pack.7), channel_id=1, source_target_pairs={{1,2},{3,4},{5,6},{2,1},{4,3},{6,5},{9,10},{11,12},{13,14},{10,9},... | collective-permute-start | bytes 1572872 | tf_op jit(solution)/shard_map/ppermute | solution.py:558
  36.6 13.7 %collective-permute-start.8 = (s16[50,16,128]{2,1,0:T(8,128)(2,1)S(1)}, s16[50,16,128]{2,1,0:T(8,128)(2,1)S(1)}, u32[]{:S(2)}, u32[]{:S(2)}) collective-permute-start(s16[50,16,128]{2,1,0:T(8,128)(2,1)S(1)} %get-tuple-element.44), channel_id=1, source_target_pairs={{0,16},{8,24},{16,0},{24,8},{1,17},{9,25},{17,1},{25,9},{2,18},{10... | collective-permute-start | bytes 614408 | tf_op jit(solution)/shard_map/edge_near/ppermute | solution.py:520
  45.9 8.7 %collective-permute-start.10 = (s16[25,16,128]{2,1,0:T(8,128)(2,1)S(1)}, s16[25,16,128]{2,1,0:T(8,128)(2,1)S(1)}, u32[]{:S(2)}, u32[]{:S(2)}) collective-permute-start(s16[25,16,128]{2,1,0:T(8,128)(2,1)S(1)} %get-tuple-element.48), channel_id=1, source_target_pairs={{0,16},{8,24},{16,0},{24,8},{1,17},{9,25},{17,1},{25,9},{2,18},{10... | collective-permute-start | bytes 307208 | tf_op jit(solution)/shard_map/edge_far/ppermute | solution.py:520
  50.2 4.4 %copy-start.4 = (bf16[512,128]{1,0:T(8,128)(2,1)S(1)}, bf16[512,128]{1,0:T(8,128)(2,1)}, u32[]{:S(2)}) copy-start(bf16[512,128]{1,0:T(8,128)(2,1)} %constant.12.clone.along_x) | copy-start | bytes 393220

commit v6 on v5

--- a/solution.py
+++ b/solution.py
@@ -542,7 +542,7 @@
         across = lax.ppermute(for_across, "snap", chip_pairs)
         diagonal = lax.ppermute(for_diagonal, "snap", diagonal_pairs)
         near_other, far_w = pack(
-            pack_other_kernel, (velocity, after(other, for_across, for_diagonal)), [near_shape, far_shape], 6
+            pack_other_kernel, (velocity, after(other, for_across, for_diagonal, pair_weights)), [near_shape, far_shape], 6
         )
         halo_other = lax.ppermute(near_other, "slab", near_pairs)
 

time: 57.2 us -> 55.5 us (0.970)
  waiting for transfers between devices: 18 us -> 15.8 us
    ppermute x1, waiting for transfers between devices: 5.52 us -> 0.01 us  [local(): other = lax.ppermute(velocity, 'snap', core_pairs)]
    ppermute x1, waiting for transfers between devices: 1.12 us -> 4.76 us  [local(): lax.ppermute(phase_bins, 'snap', core_pairs)]
  transfers between devices with their start and end apart: 11 -> 11, of which waited for: 5 -> 4; matrix products, arithmetic and copies ran while one was open for 0% -> 0% of each run, Pallas kernels for 38% -> 40%
where the time goes in v6:
time: 55.5 us; the launch traced here: 55.4 us
  Pallas kernels  24.3 us (44%)
  waiting for transfers between devices  15.8 us (28%)
  starting transfers between devices  14.8 us (27%)
    pallas_call x1, Pallas kernels, inside_sums(): pl.pallas_call(inside_kernel, scratch_shapes=[*scratch, field, field, fie...  10.8 us
    ppermute x1, waiting for transfers between devices, local(): halo_w = lax.ppermute(after(far_w, inside_parts[0]), 'slab', far_pairs)  6.95 us
    pallas_call x2, Pallas kernels, edge_sums(): pl.pallas_call(body, scratch_shapes=[*scratch, field, field], **call, **p...  5.12 us
    ppermute x1, waiting for transfers between devices, local(): lax.ppermute(phase_bins, 'snap', core_pairs)  4.76 us
    ppermute x1, starting transfers between devices, local(): halo_v = lax.ppermute(after(far_v, halo_other), 'slab', far_pairs)  4.12 us
    ppermute x3, starting transfers between devices, exchange(): return (here, lax.ppermute(code, 'snap', chip_pairs))  2.78 us
    ppermute x1, starting transfers between devices, local(): halo_w = lax.ppermute(after(far_w, inside_parts[0]), 'slab', far_pairs)  2.6 us
    pallas_call x1, Pallas kernels, local(): pl.pallas_call(finish_far_kernel, out_shape=out_shape, in_specs=[vmem()]...  2.37 us
  transfers between devices with their start and end apart: 11, of which 4 were waited for; matrix products, arithmetic and copies ran while one was open for 0% of the time, Pallas kernels for 40%

profile of v6, /device:TPU:16, one launch (start us, length us, event | category | flops | bytes accessed | tf_op | source)
XLA Modules:
  0.0 55.4 jit_solution(16047769198831465564)
XLA Ops:
  0.0 1.2 %pack.4 = bf16[16,2,2,16,256]{4,3,2,1,0:T(8,128)(2,1)S(1)} custom-call(bf16[16,3,8,16,512]{4,3,2,1,0:T(8,128)(2,1)} %own.10), custom_call_target="tpu_custom_call" | custom-call | flops 1 | bytes 1 | tf_op jit(solution)/shard_map/pack/pallas_call | solution.py:472
  1.3 1.6 %collective-permute-start.2 = (bf16[16,2,2,16,256]{4,3,2,1,0:T(8,128)(2,1)S(1)}, bf16[16,2,2,16,256]{4,3,2,1,0:T(8,128)(2,1)S(1)}, u32[]{:S(2)}, u32[]{:S(2)}) collective-permute-start(bf16[16,2,2,16,256]{4,3,2,1,0:T(8,128)(2,1)S(1)} %pack.4), channel_id=1, source_target_pairs={{0,1},{1,0},{2,3},{3,2},{4,5},{5,4},{6,7},{7,6},{8,9},{9,8},{10,11... | collective-permute-start | bytes 1572872 | tf_op jit(solution)/shard_map/pack/ppermute | solution.py:525
  2.8 0.1 copy-done
  3.0 0.2 pack.5
  3.1 1.6 %collective-permute-start.3 = (bf16[16,6,16,128]{3,2,1,0:T(8,128)(2,1)S(1)}, bf16[16,6,16,128]{3,2,1,0:T(8,128)(2,1)S(1)}, u32[]{:S(2)}, u32[]{:S(2)}) collective-permute-start(bf16[16,6,16,128]{3,2,1,0:T(8,128)(2,1)S(1)} %get-tuple-element.30), channel_id=1, source_target_pairs={{0,16},{8,24},{16,0},{24,8},{1,17},{9,25},{17,1},{25,9},{2,18},{10... | collective-permute-start | bytes 1179656 | tf_op jit(solution)/shard_map/pack/ppermute | solution.py:542
  4.8 0.6 %collective-permute-start = (s32[16]{0:T(128)S(1)}, s32[16]{0:T(128)S(1)}, u32[]{:S(2)}, u32[]{:S(2)}) collective-permute-start(s32[16]{0:T(128)S(1)} %copy-done.6), channel_id=1, source_target_pairs={{0,8},{8,0},{16,24},{24,16},{1,9},{9,1},{17,25},{25,17},{2,10},{10... | collective-permute-start | bytes 200 | tf_op jit(solution)/shard_map/ppermute | solution.py:526
  5.4 4.8 %collective-permute-done = s32[16]{0:T(128)S(1)} collective-permute-done((s32[16]{0:T(128)S(1)}, s32[16]{0:T(128)S(1)}, u32[]{:S(2)}, u32[]{:S(2)}) %collective-permute-start) | collective-permute-done | bytes 96 | tf_op jit(solution)/shard_map/ppermute | solution.py:526
  10.2 0.6 %weights.1 = (f32[32,2,8,128]{3,2,1,0:T(8,128)S(1)}, f32[32,128]{1,0:T(8,128)S(1)}) custom-call(s32[32]{0:T(128)S(1)} %pad_add_fusion.bins, f32[360]{0:T(512)S(1)} %copy-done.5), custom_call_target="tpu_custom_call" | custom-call | flops 1 | bytes 1 | tf_op jit(solution)/shard_map/weights/pallas_call | solution.py:529
  10.9 0.3 pack.6
  11.1 1.6 %collective-permute-start.6 = (bf16[16,2,2,16,256]{4,3,2,1,0:T(8,128)(2,1)S(1)}, bf16[16,2,2,16,256]{4,3,2,1,0:T(8,128)(2,1)S(1)}, u32[]{:S(2)}, u32[]{:S(2)}) collective-permute-start(bf16[16,2,2,16,256]{4,3,2,1,0:T(8,128)(2,1)S(1)} %get-tuple-element.33), channel_id=1, source_target_pairs={{0,1},{1,0},{2,3},{3,2},{4,5},{5,4},{6,7},{7,6},{8,9},{9,8},{10,11... | collective-permute-start | bytes 1572872 | tf_op jit(solution)/shard_map/pack/ppermute | solution.py:547
  12.7 10.8 %inside.1 = (s16[197,16,128]{2,1,0:T(8,128)(2,1)S(1)}, f32[4,3,16,16,128]{4,3,2,1,0:T(8,128)S(1)}) custom-call(f32[32,128]{1,0:T(8,128)S(1)} %get-tuple-element.28.bins, f32[32,2,8,128]{3,2,1,0:T(8,128)S(1)} %get-tuple-element.35.weight.pair_weight.refs_0_, bf16[1024,256]{1,0:T(8,128)(2,1)S(1)} %copy-done.2, bf16[256,256]{1,0:T(8,128)(2,1)S(1)} %copy-done.3, ...), custom_call_target="tpu_custom_call" | custom-call | flops 1 | bytes 1 | tf_op jit(solution)/shard_map/inside/pallas_call | solution.py:501
  23.6 1.6 %collective-permute-start.5 = (s16[197,16,128]{2,1,0:T(8,128)(2,1)S(1)}, s16[197,16,128]{2,1,0:T(8,128)(2,1)S(1)}, u32[]{:S(2)}, u32[]{:S(2)}) collective-permute-start(s16[197,16,128]{2,1,0:T(8,128)(2,1)S(1)} %get-tuple-element.38), channel_id=1, source_target_pairs={{0,16},{8,24},{16,0},{24,8},{1,17},{9,25},{17,1},{25,9},{2,18},{10... | collective-permute-start | bytes 2420744 | tf_op jit(solution)/shard_map/ppermute | solution.py:520
  25.2 2.6 %collective-permute-start.9 = (bf16[2,16,1,2,16,256]{5,4,3,2,1,0:T(8,128)(2,1)S(1)}, bf16[2,16,1,2,16,256]{5,4,3,2,1,0:T(8,128)(2,1)S(1)}, u32[]{:S(2)}, u32[]{:S(2)}) collective-permute-start(bf16[2,16,1,2,16,256]{5,4,3,2,1,0:T(8,128)(2,1)S(1)} %get-tuple-element.46), channel_id=1, source_target_pairs={{1,2},{3,4},{5,6},{2,1},{4,3},{6,5},{9,10},{11,12},{13,14},{10,9},... | collective-permute-start | bytes 1572872 | tf_op jit(solution)/shard_map/ppermute | solution.py:557
  27.8 4.1 %collective-permute-start.7 = (bf16[4,16,2,16,128]{4,3,2,1,0:T(8,128)(2,1)S(1)}, bf16[4,16,2,16,128]{4,3,2,1,0:T(8,128)(2,1)S(1)}, u32[]{:S(2)}, u32[]{:S(2)}) collective-permute-start(bf16[4,16,2,16,128]{4,3,2,1,0:T(8,128)(2,1)S(1)} %pack.7), channel_id=1, source_target_pairs={{1,2},{3,4},{5,6},{2,1},{4,3},{6,5},{9,10},{11,12},{13,14},{10,9},... | collective-permute-start | bytes 1572872 | tf_op jit(solution)/shard_map/ppermute | solution.py:558
  32.0 3.3 %edge_near.1 = (s16[50,16,128]{2,1,0:T(8,128)(2,1)S(1)}, f32[4,3,4,16,128]{4,3,2,1,0:T(8,128)S(1)}) custom-call(f32[32,2,8,128]{3,2,1,0:T(8,128)S(1)} %get-tuple-element.35.weight.pair_weight.refs_0_, bf16[1024,256]{1,0:T(8,128)(2,1)S(1)} %copy-done.2, bf16[256,256]{1,0:T(8,128)(2,1)S(1)} %copy-done.3, bf16[512,512]{1,0:T(8,128)(2,1)S(1)} %copy-done.1, ...), custom_call_target="tpu_custom_call" | custom-call | flops 1 | bytes 1 | tf_op jit(solution)/shard_map/edge_near/pallas_call | solution.py:514
  35.2 0.6 %collective-permute-start.8 = (s16[50,16,128]{2,1,0:T(8,128)(2,1)S(1)}, s16[50,16,128]{2,1,0:T(8,128)(2,1)S(1)}, u32[]{:S(2)}, u32[]{:S(2)}) collective-permute-start(s16[50,16,128]{2,1,0:T(8,128)(2,1)S(1)} %get-tuple-element.44), channel_id=1, source_target_pairs={{0,16},{8,24},{16,0},{24,8},{1,17},{9,25},{17,1},{25,9},{2,18},{10... | collective-permute-start | bytes 614408 | tf_op jit(solution)/shard_map/edge_near/ppermute | solution.py:520
  35.8 7.0 %collective-permute-done.9.refs_6_ = bf16[2,16,1,2,16,256]{5,4,3,2,1,0:T(8,128)(2,1)S(1)} collective-permute-done((bf16[2,16,1,2,16,256]{5,4,3,2,1,0:T(8,128)(2,1)S(1)}, bf16[2,16,1,2,16,256]{5,4,3,2,1,0:T(8,128)(2,1)S(1)}, u32[]{:S(2)}, u32[]{:S(2)}) %collective-permute-start.9) | collective-permute-done | bytes 524320 | tf_op jit(solution)/shard_map/ppermute | solution.py:557
  42.8 1.9 %edge_far.1 = (s16[25,16,128]{2,1,0:T(8,128)(2,1)S(1)}, f32[4,3,2,16,128]{4,3,2,1,0:T(8,128)S(1)}) custom-call(f32[32,2,8,128]{3,2,1,0:T(8,128)S(1)} %get-tuple-element.35.weight.pair_weight.refs_0_, bf16[1024,256]{1,0:T(8,128)(2,1)S(1)} %copy-done.2, bf16[256,256]{1,0:T(8,128)(2,1)S(1)} %copy-done.3, bf16[512,512]{1,0:T(8,128)(2,1)S(1)} %copy-done.1, ...), custom_call_target="tpu_custom_call" | custom-call | flops 1 | bytes 1 | tf_op jit(solution)/shard_map/edge_far/pallas_call | solution.py:514
  44.6 0.6 %collective-permute-start.10 = (s16[25,16,128]{2,1,0:T(8,128)(2,1)S(1)}, s16[25,16,128]{2,1,0:T(8,128)(2,1)S(1)}, u32[]{:S(2)}, u32[]{:S(2)}) collective-permute-start(s16[25,16,128]{2,1,0:T(8,128)(2,1)S(1)} %get-tuple-element.48), channel_id=1, source_target_pairs={{0,16},{8,24},{16,0},{24,8},{1,17},{9,25},{17,1},{25,9},{2,18},{10... | collective-permute-start | bytes 307208 | tf_op jit(solution)/shard_map/edge_far/ppermute | solution.py:520
  45.3 1.5 %invert.1 = (f32[64,2,8,128]{3,2,1,0:T(8,128)S(1)}, f32[9,16,128]{2,1,0:T(8,128)S(1)}) custom-call(f32[360]{0:T(512)S(1)} %copy-done.5, f32[32,2,8,128]{3,2,1,0:T(8,128)S(1)} %get-tuple-element.35.weight.pair_weight.refs_0_, s16[197,16,128]{2,1,0:T(8,128)(2,1)S(1)} %collective-permute-done.5.code.exponents), custom_call_target="tpu_custom_call" | custom-call | flops 1 | bytes 1 | tf_op jit(solution)/shard_map/invert/pallas_call | solution.py:567
  46.7 2.2 %collective-permute-done.8.near_code.near_exponents = s16[50,16,128]{2,1,0:T(8,128)(2,1)S(1)} collective-permute-done((s16[50,16,128]{2,1,0:T(8,128)(2,1)S(1)}, s16[50,16,128]{2,1,0:T(8,128)(2,1)S(1)}, u32[]{:S(2)}, u32[]{:S(2)}) %collective-permute-start.8) | collective-permute-done | bytes 204832 | tf_op jit(solution)/shard_map/edge_near/ppermute | solution.py:520
  48.9 2.1 %finish.1.refs_2_ = f32[3,3,4,8,16,128]{5,4,3,2,1,0:T(8,128)} custom-call(f32[9,16,128]{2,1,0:T(8,128)S(1)} %get-tuple-element.40.inverse, f32[4,3,16,16,128]{4,3,2,1,0:T(8,128)S(1)} %get-tuple-element.42.here, s16[197,16,128]{2,1,0:T(8,128)(2,1)S(1)} %collective-permute-done.5.code.exponents, ...), custom_call_target="tpu_custom_call" | custom-call | flops 1 | bytes 1 | tf_op jit(solution)/shard_map/finish/pallas_call | solution.py:595
  51.1 1.9 %collective-permute-done.7.halo = bf16[4,16,2,16,128]{4,3,2,1,0:T(8,128)(2,1)S(1)} collective-permute-done((bf16[4,16,2,16,128]{4,3,2,1,0:T(8,128)(2,1)S(1)}, bf16[4,16,2,16,128]{4,3,2,1,0:T(8,128)(2,1)S(1)}, u32[]{:S(2)}, u32[]{:S(2)}) %collective-permute-start.7) | collective-permute-done | bytes 524320 | tf_op jit(solution)/shard_map/ppermute | solution.py:558
  53.0 2.4 %finish_far.1 = f32[3,3,4,8,16,128]{5,4,3,2,1,0:T(8,128)} custom-call(f32[64,2,8,128]{3,2,1,0:T(8,128)S(1)} %get-tuple-element.39.weight, f32[9,16,128]{2,1,0:T(8,128)S(1)} %get-tuple-element.40.inverse, bf16[512,128]{1,0:T(8,128)(2,1)S(1)} %copy-done.4, bf16[256,256]{1,0:T(8,128)(2,1)S(1)} %copy-done.3, ...), custom_call_target="tpu_custom_call", output_to_operand_aliasing={{}: (11, {})} | custom-call | flops 1 | bytes 1 | tf_op jit(solution)/shard_map/finish_far/pallas_call | solution.py:610
  (24 shorter events, 0.3 us)
Async XLA Ops:
  0.0 3.0 %copy-start = (bf16[16,3,8,16,512]{4,3,2,1,0:T(8,128)(2,1)S(1)}, bf16[16,3,8,16,512]{4,3,2,1,0:T(8,128)(2,1)}, u32[]{:S(2)}) copy-start(bf16[16,3,8,16,512]{4,3,2,1,0:T(8,128)(2,1)} %own.10) | copy-start | bytes 18874372
  0.0 10.8 %collective-permute-start.1 = (bf16[16,3,8,16,512]{4,3,2,1,0:T(8,128)(2,1)}, bf16[16,3,8,16,512]{4,3,2,1,0:T(8,128)(2,1)S(1)}, u32[]{:S(2)}, u32[]{:S(2)}) collective-permute-start(bf16[16,3,8,16,512]{4,3,2,1,0:T(8,128)(2,1)} %own.10), channel_id=1, source_target_pairs={{0,8},{8,0},{16,24},{24,16},{1,9},{9,1},{17,25},{25,17},{2,10},{10... | collective-permute-start | bytes 18874376 | tf_op jit(solution)/shard_map/ppermute | solution.py:522
  1.2 3.5 %copy-start.6 = (s32[16]{0:T(128)S(1)}, s32[16]{0:T(128)}, u32[]{:S(2)}) copy-start(s32[16]{0:T(128)} %param.8) | copy-start | bytes 196
  1.3 8.9 %copy-start.5 = (f32[360]{0:T(512)S(1)}, f32[360]{0:T(512)}, u32[]{:S(2)}) copy-start(f32[360]{0:T(512)} %constant.10.clone.table) | copy-start | bytes 4324
  1.3 22.2 %collective-permute-start.2 = (bf16[16,2,2,16,256]{4,3,2,1,0:T(8,128)(2,1)S(1)}, bf16[16,2,2,16,256]{4,3,2,1,0:T(8,128)(2,1)S(1)}, u32[]{:S(2)}, u32[]{:S(2)}) collective-permute-start(bf16[16,2,2,16,256]{4,3,2,1,0:T(8,128)(2,1)S(1)} %pack.4), channel_id=1, source_target_pairs={{0,1},{1,0},{2,3},{3,2},{4,5},{5,4},{6,7},{7,6},{8,9},{9,8},{10,11... | collective-permute-start | bytes 1572872 | tf_op jit(solution)/shard_map/pack/ppermute | solution.py:525
  3.1 20.3 %collective-permute-start.3 = (bf16[16,6,16,128]{3,2,1,0:T(8,128)(2,1)S(1)}, bf16[16,6,16,128]{3,2,1,0:T(8,128)(2,1)S(1)}, u32[]{:S(2)}, u32[]{:S(2)}) collective-permute-start(bf16[16,6,16,128]{3,2,1,0:T(8,128)(2,1)S(1)} %get-tuple-element.30), channel_id=1, source_target_pairs={{0,16},{8,24},{16,0},{24,8},{1,17},{9,25},{17,1},{25,9},{2,18},{10... | collective-permute-start | bytes 1179656 | tf_op jit(solution)/shard_map/pack/ppermute | solution.py:542
  4.7 18.8 %collective-permute-start.4 = (bf16[16,6,16,128]{3,2,1,0:T(8,128)(2,1)S(1)}, bf16[16,6,16,128]{3,2,1,0:T(8,128)(2,1)S(1)}, u32[]{:S(2)}, u32[]{:S(2)}) collective-permute-start(bf16[16,6,16,128]{3,2,1,0:T(8,128)(2,1)S(1)} %get-tuple-element.31), channel_id=1, source_target_pairs={{0,24},{8,16},{16,8},{24,0},{1,25},{9,17},{17,9},{25,1},{2,26},{10... | collective-permute-start | bytes 1179656 | tf_op jit(solution)/shard_map/pack/ppermute | solution.py:543
  4.8 5.3 %collective-permute-start = (s32[16]{0:T(128)S(1)}, s32[16]{0:T(128)S(1)}, u32[]{:S(2)}, u32[]{:S(2)}) collective-permute-start(s32[16]{0:T(128)S(1)} %copy-done.6), channel_id=1, source_target_pairs={{0,8},{8,0},{16,24},{24,16},{1,9},{9,1},{17,25},{25,17},{2,10},{10... | collective-permute-start | bytes 200 | tf_op jit(solution)/shard_map/ppermute | solution.py:526
  10.8 1.9 %copy-start.1 = (bf16[512,512]{1,0:T(8,128)(2,1)S(1)}, bf16[512,512]{1,0:T(8,128)(2,1)}, u32[]{:S(2)}) copy-start(bf16[512,512]{1,0:T(8,128)(2,1)} %constant.14.clone.all_z.refs_3_) | copy-start | bytes 1572868
  10.8 1.9 %copy-start.2 = (bf16[1024,256]{1,0:T(8,128)(2,1)S(1)}, bf16[1024,256]{1,0:T(8,128)(2,1)}, u32[]{:S(2)}) copy-start(bf16[1024,256]{1,0:T(8,128)(2,1)} %constant.11.clone.along_x.refs_1_) | copy-start | bytes 1572868
  10.9 1.9 %copy-start.3 = (bf16[256,256]{1,0:T(8,128)(2,1)S(1)}, bf16[256,256]{1,0:T(8,128)(2,1)}, u32[]{:S(2)}) copy-start(bf16[256,256]{1,0:T(8,128)(2,1)} %constant.13.clone.along_y.refs_2_) | copy-start | bytes 393220
  11.1 16.7 %collective-permute-start.6 = (bf16[16,2,2,16,256]{4,3,2,1,0:T(8,128)(2,1)S(1)}, bf16[16,2,2,16,256]{4,3,2,1,0:T(8,128)(2,1)S(1)}, u32[]{:S(2)}, u32[]{:S(2)}) collective-permute-start(bf16[16,2,2,16,256]{4,3,2,1,0:T(8,128)(2,1)S(1)} %get-tuple-element.33), channel_id=1, source_target_pairs={{0,1},{1,0},{2,3},{3,2},{4,5},{5,4},{6,7},{7,6},{8,9},{9,8},{10,11... | collective-permute-start | bytes 1572872 | tf_op jit(solution)/shard_map/pack/ppermute | solution.py:547
  23.6 21.6 %collective-permute-start.5 = (s16[197,16,128]{2,1,0:T(8,128)(2,1)S(1)}, s16[197,16,128]{2,1,0:T(8,128)(2,1)S(1)}, u32[]{:S(2)}, u32[]{:S(2)}) collective-permute-start(s16[197,16,128]{2,1,0:T(8,128)(2,1)S(1)} %get-tuple-element.38), channel_id=1, source_target_pairs={{0,16},{8,24},{16,0},{24,8},{1,17},{9,25},{17,1},{25,9},{2,18},{10... | collective-permute-start | bytes 2420744 | tf_op jit(solution)/shard_map/ppermute | solution.py:520
  25.2 17.6 %collective-permute-start.9 = (bf16[2,16,1,2,16,256]{5,4,3,2,1,0:T(8,128)(2,1)S(1)}, bf16[2,16,1,2,16,256]{5,4,3,2,1,0:T(8,128)(2,1)S(1)}, u32[]{:S(2)}, u32[]{:S(2)}) collective-permute-start(bf16[2,16,1,2,16,256]{5,4,3,2,1,0:T(8,128)(2,1)S(1)} %get-tuple-element.46), channel_id=1, source_target_pairs={{1,2},{3,4},{5,6},{2,1},{4,3},{6,5},{9,10},{11,12},{13,14},{10,9},... | collective-permute-start | bytes 1572872 | tf_op jit(solution)/shard_map/ppermute | solution.py:557
  27.8 25.1 %collective-permute-start.7 = (bf16[4,16,2,16,128]{4,3,2,1,0:T(8,128)(2,1)S(1)}, bf16[4,16,2,16,128]{4,3,2,1,0:T(8,128)(2,1)S(1)}, u32[]{:S(2)}, u32[]{:S(2)}) collective-permute-start(bf16[4,16,2,16,128]{4,3,2,1,0:T(8,128)(2,1)S(1)} %pack.7), channel_id=1, source_target_pairs={{1,2},{3,4},{5,6},{2,1},{4,3},{6,5},{9,10},{11,12},{13,14},{10,9},... | collective-permute-start | bytes 1572872 | tf_op jit(solution)/shard_map/ppermute | solution.py:558
  35.2 13.7 %collective-permute-start.8 = (s16[50,16,128]{2,1,0:T(8,128)(2,1)S(1)}, s16[50,16,128]{2,1,0:T(8,128)(2,1)S(1)}, u32[]{:S(2)}, u32[]{:S(2)}) collective-permute-start(s16[50,16,128]{2,1,0:T(8,128)(2,1)S(1)} %get-tuple-element.44), channel_id=1, source_target_pairs={{0,16},{8,24},{16,0},{24,8},{1,17},{9,25},{17,1},{25,9},{2,18},{10... | collective-permute-start | bytes 614408 | tf_op jit(solution)/shard_map/edge_near/ppermute | solution.py:520
  44.6 8.3 %collective-permute-start.10 = (s16[25,16,128]{2,1,0:T(8,128)(2,1)S(1)}, s16[25,16,128]{2,1,0:T(8,128)(2,1)S(1)}, u32[]{:S(2)}, u32[]{:S(2)}) collective-permute-start(s16[25,16,128]{2,1,0:T(8,128)(2,1)S(1)} %get-tuple-element.48), channel_id=1, source_target_pairs={{0,16},{8,24},{16,0},{24,8},{1,17},{9,25},{17,1},{25,9},{2,18},{10... | collective-permute-start | bytes 307208 | tf_op jit(solution)/shard_map/edge_far/ppermute | solution.py:520
  48.9 4.1 %copy-start.4 = (bf16[512,128]{1,0:T(8,128)(2,1)S(1)}, bf16[512,128]{1,0:T(8,128)(2,1)}, u32[]{:S(2)}) copy-start(bf16[512,128]{1,0:T(8,128)(2,1)} %constant.12.clone.along_x) | copy-start | bytes 393220

commit v7 on v6

--- a/solution.py
+++ b/solution.py
@@ -23,6 +23,17 @@
 
 def four_planes(width):
     return np.concatenate([factor * np.eye(width, dtype=np.float32) for _, factor in TAPS])
+
+
+def halo_planes(width):
+    factors = dict(TAPS)
+    eye = np.eye(width, dtype=np.float32)
+    return np.stack(
+        [
+            np.stack([np.concatenate([factors.get(4 * high + i - p - 2, 0.0) * eye for i in range(2)]) for p in range(2)])
+            for high in range(2)
+        ]
+    )
 
 
 def phase_table():
@@ -339,24 +350,39 @@
             solve(inverse, near_here.at[0], near_code, own, (2 * n - 8, 2 * n - 6), n - 4, store)
 
 
-def finish_far_kernel(weight, inverse, along_x, along_y, own, other, across, diagonal, halo, *refs):
-    far_here, far_code, _, out, far_out, far_scales, *fields, out_sem = refs
-    rows = own.shape[3]
+def far_field_kernel(along_x, along_y, own, other, across, diagonal, base):
     spot = Spot(own.shape[2])
     side, lane_here = spot.far, spot.lanes(spot.here)
     sources = (own, other, across, diagonal)
 
-    def fill(p):
-        def u(g):
+    for p in range(2):
+        def u(g, p=p):
             return flat(sources[g][:, 0, side.edge + p, :, lane_here] if g < 2 else sources[g][:, 4 + p])
 
         def own_plane(g, i):
             return flat(sources[g][:, 1, side.own + i, :, lane_here] if g < 2 else sources[g][:, i])
 
-        def around(g):
-            return side.around(p, lambda i: own_plane(g, i), lambda i: flat(halo[g, :, i]))
-
-        return fill_z(fields[p], along_x, along_y, u, around)
+        def around(g, p=p):
+            nothing = jnp.zeros((along_y.shape[0], along_x.shape[1]), own.dtype)
+            return side.around(p, lambda i: own_plane(g, i), lambda i: nothing)
+
+        run(fill_z(base.at[p], along_x, along_y, u, around))
+
+
+def finish_far_kernel(weight, inverse, along_halo, base, halo, *refs):
+    far_here, far_code, _, out, far_out, far_scales, *fields, out_sem = refs
+    parts, snaps, _, rows, _ = halo.shape
+    size = snaps * rows
+    side = Spot(out.shape[3]).far
+    high = side.halo_at // 4
+
+    def fill(p):
+        def chunk(g):
+            planes = jnp.concatenate([flat(halo[g, :, i]) for i in range(2)], axis=1)
+            at = pl.ds(g * size, size)
+            fields[p][at, :] = base[p, at, :] + product(planes, along_halo[high, p])
+
+        return [lambda g=g: chunk(g) for g in range(parts)]
 
     def solve_order(k):
         def store_far(i, value):
@@ -605,12 +631,19 @@
             **params(16),
         )(inverse, *inside, inside[1], *near, near[1])
 
+    with jax.named_scope("far_field"):
+        base = pl.pallas_call(
+            far_field_kernel,
+            out_shape=jax.ShapeDtypeStruct((2, 4 * size, width), jnp.float32),
+            **params(26),
+        )(after(along_x_half, near[0]), along_y, velocity, other, across, diagonal)
+
     with jax.named_scope("finish_far"):
         edges = pltpu.VMEM((3, 2, ORDERS, 2, rows, width), jnp.float32)
         return pl.pallas_call(
             finish_far_kernel,
             out_shape=out_shape,
-            in_specs=[vmem()] * 11 + [hbm()],
+            in_specs=[vmem()] * 7 + [hbm()],
             out_specs=hbm(),
             scratch_shapes=[
                 edges,
@@ -619,11 +652,10 @@
                 pltpu.VMEM((4 * size, width), jnp.float32),
                 pltpu.SemaphoreType.DMA,
             ],
-            input_output_aliases={11: 0},
+            input_output_aliases={7: 0},
             **params(26),
         )(
-            weights, inverse, along_x_half, along_y, velocity, other, across, diagonal,
-            after(halo_v, out), *far_y, out,
+            weights, inverse, jnp.asarray(halo_planes(width), jnp.bfloat16), base, after(halo_v, out), *far_y, out
         )
 
 

time: 55.5 us -> 55.3 us (level)
  waiting for transfers between devices: 15.8 us -> 14.6 us
  Pallas kernels: 24.3 us -> 24.9 us
    ppermute x3, waiting for transfers between devices: 2.18 us -> 1.2 us  [exchange(): return (here, lax.ppermute(code, 'snap', chip_pairs))]
    pallas_call x0 -> x1, Pallas kernels: none -> 0.97 us  [local(): pl.pallas_call(far_field_kernel, out_shape=jax.ShapeDtypeStruct((2, 4 * s...]
  transfers between devices with their start and end apart: 11 -> 11, of which waited for: 4 -> 4; matrix products, arithmetic and copies ran while one was open for 0% -> 0% of each run, Pallas kernels for 40% -> 41%
where the time goes in v7:
time: 55.3 us; the launch traced here: 55.2 us
  Pallas kernels  24.9 us (45%)
  starting transfers between devices  15 us (27%)
  waiting for transfers between devices  14.6 us (26%)
    pallas_call x1, Pallas kernels, inside_sums(): pl.pallas_call(inside_kernel, scratch_shapes=[*scratch, field, field, fie...  10.8 us
    ppermute x1, waiting for transfers between devices, local(): halo_w = lax.ppermute(after(far_w, inside_parts[0]), 'slab', far_pairs)  6.76 us
    pallas_call x2, Pallas kernels, edge_sums(): pl.pallas_call(body, scratch_shapes=[*scratch, field, field], **call, **p...  5.11 us
    ppermute x1, waiting for transfers between devices, local(): lax.ppermute(phase_bins, 'snap', core_pairs)  4.76 us
    ppermute x1, starting transfers between devices, local(): halo_v = lax.ppermute(after(far_v, halo_other), 'slab', far_pairs)  4.31 us
    ppermute x3, starting transfers between devices, exchange(): return (here, lax.ppermute(code, 'snap', chip_pairs))  2.79 us
    ppermute x1, starting transfers between devices, local(): halo_w = lax.ppermute(after(far_w, inside_parts[0]), 'slab', far_pairs)  2.6 us
    pallas_call x1, Pallas kernels, local(): pl.pallas_call(finish_kernel, out_shape=out_shape, grid=(ORDERS,), in_spe...  2.15 us
  transfers between devices with their start and end apart: 11, of which 4 were waited for; matrix products, arithmetic and copies ran while one was open for 0% of the time, Pallas kernels for 41%

profile of v7, /device:TPU:16, one launch (start us, length us, event | category | flops | bytes accessed | tf_op | source)
XLA Modules:
  0.0 55.2 jit_solution(17247948192658431101)
XLA Ops:
  0.0 1.2 %pack.4 = bf16[16,2,2,16,256]{4,3,2,1,0:T(8,128)(2,1)S(1)} custom-call(bf16[16,3,8,16,512]{4,3,2,1,0:T(8,128)(2,1)} %refs_4_.3), custom_call_target="tpu_custom_call" | custom-call | flops 1 | bytes 1 | tf_op jit(solution)/shard_map/pack/pallas_call | solution.py:498
  1.3 1.6 %collective-permute-start.2 = (bf16[16,2,2,16,256]{4,3,2,1,0:T(8,128)(2,1)S(1)}, bf16[16,2,2,16,256]{4,3,2,1,0:T(8,128)(2,1)S(1)}, u32[]{:S(2)}, u32[]{:S(2)}) collective-permute-start(bf16[16,2,2,16,256]{4,3,2,1,0:T(8,128)(2,1)S(1)} %pack.4), channel_id=1, source_target_pairs={{0,1},{1,0},{2,3},{3,2},{4,5},{5,4},{6,7},{7,6},{8,9},{9,8},{10,11... | collective-permute-start | bytes 1572872 | tf_op jit(solution)/shard_map/pack/ppermute | solution.py:551
  3.0 0.2 pack.5
  3.1 1.6 %collective-permute-start.3 = (bf16[16,6,16,128]{3,2,1,0:T(8,128)(2,1)S(1)}, bf16[16,6,16,128]{3,2,1,0:T(8,128)(2,1)S(1)}, u32[]{:S(2)}, u32[]{:S(2)}) collective-permute-start(bf16[16,6,16,128]{3,2,1,0:T(8,128)(2,1)S(1)} %get-tuple-element.31), channel_id=1, source_target_pairs={{0,16},{8,24},{16,0},{24,8},{1,17},{9,25},{17,1},{25,9},{2,18},{10... | collective-permute-start | bytes 1179656 | tf_op jit(solution)/shard_map/pack/ppermute | solution.py:568
  4.8 0.6 %collective-permute-start = (s32[16]{0:T(128)S(1)}, s32[16]{0:T(128)S(1)}, u32[]{:S(2)}, u32[]{:S(2)}) collective-permute-start(s32[16]{0:T(128)S(1)} %copy-done.7), channel_id=1, source_target_pairs={{0,8},{8,0},{16,24},{24,16},{1,9},{9,1},{17,25},{25,17},{2,10},{10... | collective-permute-start | bytes 200 | tf_op jit(solution)/shard_map/ppermute | solution.py:552
  5.4 4.8 %collective-permute-done = s32[16]{0:T(128)S(1)} collective-permute-done((s32[16]{0:T(128)S(1)}, s32[16]{0:T(128)S(1)}, u32[]{:S(2)}, u32[]{:S(2)}) %collective-permute-start) | collective-permute-done | bytes 96 | tf_op jit(solution)/shard_map/ppermute | solution.py:552
  10.2 0.6 %weights.1 = (f32[32,2,8,128]{3,2,1,0:T(8,128)S(1)}, f32[32,128]{1,0:T(8,128)S(1)}) custom-call(s32[32]{0:T(128)S(1)} %pad_add_fusion.bins, f32[360]{0:T(512)S(1)} %copy-done.6), custom_call_target="tpu_custom_call" | custom-call | flops 1 | bytes 1 | tf_op jit(solution)/shard_map/weights/pallas_call | solution.py:555
  10.9 0.3 pack.6
  11.1 1.6 %collective-permute-start.6 = (bf16[16,2,2,16,256]{4,3,2,1,0:T(8,128)(2,1)S(1)}, bf16[16,2,2,16,256]{4,3,2,1,0:T(8,128)(2,1)S(1)}, u32[]{:S(2)}, u32[]{:S(2)}) collective-permute-start(bf16[16,2,2,16,256]{4,3,2,1,0:T(8,128)(2,1)S(1)} %get-tuple-element.34), channel_id=1, source_target_pairs={{0,1},{1,0},{2,3},{3,2},{4,5},{5,4},{6,7},{7,6},{8,9},{9,8},{10,11... | collective-permute-start | bytes 1572872 | tf_op jit(solution)/shard_map/pack/ppermute | solution.py:573
  12.7 10.8 %inside.1 = (s16[197,16,128]{2,1,0:T(8,128)(2,1)S(1)}, f32[4,3,16,16,128]{4,3,2,1,0:T(8,128)S(1)}) custom-call(f32[32,128]{1,0:T(8,128)S(1)} %get-tuple-element.29.bins, f32[32,2,8,128]{3,2,1,0:T(8,128)S(1)} %get-tuple-element.36.weight.pair_weight.refs_0_, bf16[1024,256]{1,0:T(8,128)(2,1)S(1)} %copy-done.2, bf16[256,256]{1,0:T(8,128)(2,1)S(1)} %copy-done.3, ...), custom_call_target="tpu_custom_call" | custom-call | flops 1 | bytes 1 | tf_op jit(solution)/shard_map/inside/pallas_call | solution.py:527
  23.6 1.6 %collective-permute-start.5 = (s16[197,16,128]{2,1,0:T(8,128)(2,1)S(1)}, s16[197,16,128]{2,1,0:T(8,128)(2,1)S(1)}, u32[]{:S(2)}, u32[]{:S(2)}) collective-permute-start(s16[197,16,128]{2,1,0:T(8,128)(2,1)S(1)} %get-tuple-element.39), channel_id=1, source_target_pairs={{0,16},{8,24},{16,0},{24,8},{1,17},{9,25},{17,1},{25,9},{2,18},{10... | collective-permute-start | bytes 2420744 | tf_op jit(solution)/shard_map/ppermute | solution.py:546
  25.2 2.6 %collective-permute-start.9 = (bf16[2,16,1,2,16,256]{5,4,3,2,1,0:T(8,128)(2,1)S(1)}, bf16[2,16,1,2,16,256]{5,4,3,2,1,0:T(8,128)(2,1)S(1)}, u32[]{:S(2)}, u32[]{:S(2)}) collective-permute-start(bf16[2,16,1,2,16,256]{5,4,3,2,1,0:T(8,128)(2,1)S(1)} %get-tuple-element.48), channel_id=1, source_target_pairs={{1,2},{3,4},{5,6},{2,1},{4,3},{6,5},{9,10},{11,12},{13,14},{10,9},... | collective-permute-start | bytes 1572872 | tf_op jit(solution)/shard_map/ppermute | solution.py:583
  27.8 4.3 %collective-permute-start.7 = (bf16[4,16,2,16,128]{4,3,2,1,0:T(8,128)(2,1)S(1)}, bf16[4,16,2,16,128]{4,3,2,1,0:T(8,128)(2,1)S(1)}, u32[]{:S(2)}, u32[]{:S(2)}) collective-permute-start(bf16[4,16,2,16,128]{4,3,2,1,0:T(8,128)(2,1)S(1)} %pack.7), channel_id=1, source_target_pairs={{1,2},{3,4},{5,6},{2,1},{4,3},{6,5},{9,10},{11,12},{13,14},{10,9},... | collective-permute-start | bytes 1572872 | tf_op jit(solution)/shard_map/ppermute | solution.py:584
  32.1 3.2 %edge_near.1 = (s16[50,16,128]{2,1,0:T(8,128)(2,1)S(1)}, f32[4,3,4,16,128]{4,3,2,1,0:T(8,128)S(1)}) custom-call(f32[32,2,8,128]{3,2,1,0:T(8,128)S(1)} %get-tuple-element.36.weight.pair_weight.refs_0_, bf16[1024,256]{1,0:T(8,128)(2,1)S(1)} %copy-done.2, bf16[256,256]{1,0:T(8,128)(2,1)S(1)} %copy-done.3, bf16[512,512]{1,0:T(8,128)(2,1)S(1)} %copy-done.1, ...), custom_call_target="tpu_custom_call" | custom-call | flops 1 | bytes 1 | tf_op jit(solution)/shard_map/edge_near/pallas_call | solution.py:540
  35.4 0.6 %collective-permute-start.8 = (s16[50,16,128]{2,1,0:T(8,128)(2,1)S(1)}, s16[50,16,128]{2,1,0:T(8,128)(2,1)S(1)}, u32[]{:S(2)}, u32[]{:S(2)}) collective-permute-start(s16[50,16,128]{2,1,0:T(8,128)(2,1)S(1)} %get-tuple-element.46), channel_id=1, source_target_pairs={{0,16},{8,24},{16,0},{24,8},{1,17},{9,25},{17,1},{25,9},{2,18},{10... | collective-permute-start | bytes 614408 | tf_op jit(solution)/shard_map/edge_near/ppermute | solution.py:546
  36.0 6.8 %collective-permute-done.9.refs_6_ = bf16[2,16,1,2,16,256]{5,4,3,2,1,0:T(8,128)(2,1)S(1)} collective-permute-done((bf16[2,16,1,2,16,256]{5,4,3,2,1,0:T(8,128)(2,1)S(1)}, bf16[2,16,1,2,16,256]{5,4,3,2,1,0:T(8,128)(2,1)S(1)}, u32[]{:S(2)}, u32[]{:S(2)}) %collective-permute-start.9) | collective-permute-done | bytes 524320 | tf_op jit(solution)/shard_map/ppermute | solution.py:583
  42.8 1.9 %edge_far.1 = (s16[25,16,128]{2,1,0:T(8,128)(2,1)S(1)}, f32[4,3,2,16,128]{4,3,2,1,0:T(8,128)S(1)}) custom-call(f32[32,2,8,128]{3,2,1,0:T(8,128)S(1)} %get-tuple-element.36.weight.pair_weight.refs_0_, bf16[1024,256]{1,0:T(8,128)(2,1)S(1)} %copy-done.2, bf16[256,256]{1,0:T(8,128)(2,1)S(1)} %copy-done.3, bf16[512,512]{1,0:T(8,128)(2,1)S(1)} %copy-done.1, ...), custom_call_target="tpu_custom_call" | custom-call | flops 1 | bytes 1 | tf_op jit(solution)/shard_map/edge_far/pallas_call | solution.py:540
  44.6 0.6 %collective-permute-start.10 = (s16[25,16,128]{2,1,0:T(8,128)(2,1)S(1)}, s16[25,16,128]{2,1,0:T(8,128)(2,1)S(1)}, u32[]{:S(2)}, u32[]{:S(2)}) collective-permute-start(s16[25,16,128]{2,1,0:T(8,128)(2,1)S(1)} %get-tuple-element.50), channel_id=1, source_target_pairs={{0,16},{8,24},{16,0},{24,8},{1,17},{9,25},{17,1},{25,9},{2,18},{10... | collective-permute-start | bytes 307208 | tf_op jit(solution)/shard_map/edge_far/ppermute | solution.py:546
  45.3 1.0 %far_field.1.base = f32[2,1024,128]{2,1,0:T(8,128)S(1)} custom-call(bf16[512,128]{1,0:T(8,128)(2,1)S(1)} %copy-done.5, bf16[256,256]{1,0:T(8,128)(2,1)S(1)} %copy-done.3, bf16[16,3,8,16,512]{4,3,2,1,0:T(8,128)(2,1)S(1)} %copy-done, bf16[16,3,8,16,512]{4,3,2,1,0:T(8,128)(2,1)S(1)} %collective-permute-done.1.other.refs_5_, ...), custom_call_target="tpu_custom_call" | custom-call | flops 1 | bytes 1 | tf_op jit(solution)/shard_map/far_field/pallas_call | solution.py:635
  46.2 1.5 %invert.1 = (f32[64,2,8,128]{3,2,1,0:T(8,128)S(1)}, f32[9,16,128]{2,1,0:T(8,128)S(1)}) custom-call(f32[360]{0:T(512)S(1)} %copy-done.6, f32[32,2,8,128]{3,2,1,0:T(8,128)S(1)} %get-tuple-element.36.weight.pair_weight.refs_0_, s16[197,16,128]{2,1,0:T(8,128)(2,1)S(1)} %collective-permute-done.5.code.exponents), custom_call_target="tpu_custom_call" | custom-call | flops 1 | bytes 1 | tf_op jit(solution)/shard_map/invert/pallas_call | solution.py:593
  47.7 1.2 %collective-permute-done.8.near_code.near_exponents = s16[50,16,128]{2,1,0:T(8,128)(2,1)S(1)} collective-permute-done((s16[50,16,128]{2,1,0:T(8,128)(2,1)S(1)}, s16[50,16,128]{2,1,0:T(8,128)(2,1)S(1)}, u32[]{:S(2)}, u32[]{:S(2)}) %collective-permute-start.8) | collective-permute-done | bytes 204832 | tf_op jit(solution)/shard_map/edge_near/ppermute | solution.py:546
  48.9 2.1 %finish.1.refs_2_ = f32[3,3,4,8,16,128]{5,4,3,2,1,0:T(8,128)} custom-call(f32[9,16,128]{2,1,0:T(8,128)S(1)} %get-tuple-element.41.inverse, f32[4,3,16,16,128]{4,3,2,1,0:T(8,128)S(1)} %get-tuple-element.45.here, s16[197,16,128]{2,1,0:T(8,128)(2,1)S(1)} %collective-permute-done.5.code.exponents, ...), custom_call_target="tpu_custom_call" | custom-call | flops 1 | bytes 1 | tf_op jit(solution)/shard_map/finish/pallas_call | solution.py:621
  51.1 1.9 %collective-permute-done.7.halo = bf16[4,16,2,16,128]{4,3,2,1,0:T(8,128)(2,1)S(1)} collective-permute-done((bf16[4,16,2,16,128]{4,3,2,1,0:T(8,128)(2,1)S(1)}, bf16[4,16,2,16,128]{4,3,2,1,0:T(8,128)(2,1)S(1)}, u32[]{:S(2)}, u32[]{:S(2)}) %collective-permute-start.7) | collective-permute-done | bytes 524320 | tf_op jit(solution)/shard_map/ppermute | solution.py:584
  53.0 2.0 %finish_far.1 = f32[3,3,4,8,16,128]{5,4,3,2,1,0:T(8,128)} custom-call(f32[64,2,8,128]{3,2,1,0:T(8,128)S(1)} %get-tuple-element.40.weight, f32[9,16,128]{2,1,0:T(8,128)S(1)} %get-tuple-element.41.inverse, bf16[2,2,256,128]{3,2,1,0:T(8,128)(2,1)S(1)} %copy-done.4, f32[2,1024,128]{2,1,0:T(8,128)S(1)} %far_field.1.base, ...), custom_call_target="tpu_custom_call", output_to_operand_aliasing={{}: (7, {})} | custom-call | flops 1 | bytes 1 | tf_op jit(solution)/shard_map/finish_far/pallas_call | solution.py:643
  (27 shorter events, 0.5 us)
Async XLA Ops:
  0.0 3.0 %copy-start = (bf16[16,3,8,16,512]{4,3,2,1,0:T(8,128)(2,1)S(1)}, bf16[16,3,8,16,512]{4,3,2,1,0:T(8,128)(2,1)}, u32[]{:S(2)}) copy-start(bf16[16,3,8,16,512]{4,3,2,1,0:T(8,128)(2,1)} %refs_4_.3) | copy-start | bytes 18874372
  0.0 10.8 %collective-permute-start.1 = (bf16[16,3,8,16,512]{4,3,2,1,0:T(8,128)(2,1)}, bf16[16,3,8,16,512]{4,3,2,1,0:T(8,128)(2,1)S(1)}, u32[]{:S(2)}, u32[]{:S(2)}) collective-permute-start(bf16[16,3,8,16,512]{4,3,2,1,0:T(8,128)(2,1)} %refs_4_.3), channel_id=1, source_target_pairs={{0,8},{8,0},{16,24},{24,16},{1,9},{9,1},{17,25},{25,17},{2,10},{10... | collective-permute-start | bytes 18874376 | tf_op jit(solution)/shard_map/ppermute | solution.py:548
  1.2 3.5 %copy-start.7 = (s32[16]{0:T(128)S(1)}, s32[16]{0:T(128)}, u32[]{:S(2)}) copy-start(s32[16]{0:T(128)} %param.9) | copy-start | bytes 196
  1.3 8.9 %copy-start.6 = (f32[360]{0:T(512)S(1)}, f32[360]{0:T(512)}, u32[]{:S(2)}) copy-start(f32[360]{0:T(512)} %constant.12.clone.table) | copy-start | bytes 4324
  1.3 22.2 %collective-permute-start.2 = (bf16[16,2,2,16,256]{4,3,2,1,0:T(8,128)(2,1)S(1)}, bf16[16,2,2,16,256]{4,3,2,1,0:T(8,128)(2,1)S(1)}, u32[]{:S(2)}, u32[]{:S(2)}) collective-permute-start(bf16[16,2,2,16,256]{4,3,2,1,0:T(8,128)(2,1)S(1)} %pack.4), channel_id=1, source_target_pairs={{0,1},{1,0},{2,3},{3,2},{4,5},{5,4},{6,7},{7,6},{8,9},{9,8},{10,11... | collective-permute-start | bytes 1572872 | tf_op jit(solution)/shard_map/pack/ppermute | solution.py:551
  3.1 20.3 %collective-permute-start.3 = (bf16[16,6,16,128]{3,2,1,0:T(8,128)(2,1)S(1)}, bf16[16,6,16,128]{3,2,1,0:T(8,128)(2,1)S(1)}, u32[]{:S(2)}, u32[]{:S(2)}) collective-permute-start(bf16[16,6,16,128]{3,2,1,0:T(8,128)(2,1)S(1)} %get-tuple-element.31), channel_id=1, source_target_pairs={{0,16},{8,24},{16,0},{24,8},{1,17},{9,25},{17,1},{25,9},{2,18},{10... | collective-permute-start | bytes 1179656 | tf_op jit(solution)/shard_map/pack/ppermute | solution.py:568
  4.7 18.8 %collective-permute-start.4 = (bf16[16,6,16,128]{3,2,1,0:T(8,128)(2,1)S(1)}, bf16[16,6,16,128]{3,2,1,0:T(8,128)(2,1)S(1)}, u32[]{:S(2)}, u32[]{:S(2)}) collective-permute-start(bf16[16,6,16,128]{3,2,1,0:T(8,128)(2,1)S(1)} %get-tuple-element.32), channel_id=1, source_target_pairs={{0,24},{8,16},{16,8},{24,0},{1,25},{9,17},{17,9},{25,1},{2,26},{10... | collective-permute-start | bytes 1179656 | tf_op jit(solution)/shard_map/pack/ppermute | solution.py:569
  4.8 5.3 %collective-permute-start = (s32[16]{0:T(128)S(1)}, s32[16]{0:T(128)S(1)}, u32[]{:S(2)}, u32[]{:S(2)}) collective-permute-start(s32[16]{0:T(128)S(1)} %copy-done.7), channel_id=1, source_target_pairs={{0,8},{8,0},{16,24},{24,16},{1,9},{9,1},{17,25},{25,17},{2,10},{10... | collective-permute-start | bytes 200 | tf_op jit(solution)/shard_map/ppermute | solution.py:552
  10.8 1.9 %copy-start.1 = (bf16[512,512]{1,0:T(8,128)(2,1)S(1)}, bf16[512,512]{1,0:T(8,128)(2,1)}, u32[]{:S(2)}) copy-start(bf16[512,512]{1,0:T(8,128)(2,1)} %constant.16.clone.all_z.refs_3_) | copy-start | bytes 1572868
  10.8 1.9 %copy-start.2 = (bf16[1024,256]{1,0:T(8,128)(2,1)S(1)}, bf16[1024,256]{1,0:T(8,128)(2,1)}, u32[]{:S(2)}) copy-start(bf16[1024,256]{1,0:T(8,128)(2,1)} %constant.13.clone.along_x.refs_1_) | copy-start | bytes 1572868
  10.9 1.9 %copy-start.3 = (bf16[256,256]{1,0:T(8,128)(2,1)S(1)}, bf16[256,256]{1,0:T(8,128)(2,1)}, u32[]{:S(2)}) copy-start(bf16[256,256]{1,0:T(8,128)(2,1)} %constant.15.clone.along_y.refs_2_) | copy-start | bytes 393220
  11.1 16.7 %collective-permute-start.6 = (bf16[16,2,2,16,256]{4,3,2,1,0:T(8,128)(2,1)S(1)}, bf16[16,2,2,16,256]{4,3,2,1,0:T(8,128)(2,1)S(1)}, u32[]{:S(2)}, u32[]{:S(2)}) collective-permute-start(bf16[16,2,2,16,256]{4,3,2,1,0:T(8,128)(2,1)S(1)} %get-tuple-element.34), channel_id=1, source_target_pairs={{0,1},{1,0},{2,3},{3,2},{4,5},{5,4},{6,7},{7,6},{8,9},{9,8},{10,11... | collective-permute-start | bytes 1572872 | tf_op jit(solution)/shard_map/pack/ppermute | solution.py:573
  23.6 22.6 %collective-permute-start.5 = (s16[197,16,128]{2,1,0:T(8,128)(2,1)S(1)}, s16[197,16,128]{2,1,0:T(8,128)(2,1)S(1)}, u32[]{:S(2)}, u32[]{:S(2)}) collective-permute-start(s16[197,16,128]{2,1,0:T(8,128)(2,1)S(1)} %get-tuple-element.39), channel_id=1, source_target_pairs={{0,16},{8,24},{16,0},{24,8},{1,17},{9,25},{17,1},{25,9},{2,18},{10... | collective-permute-start | bytes 2420744 | tf_op jit(solution)/shard_map/ppermute | solution.py:546
  25.2 17.6 %collective-permute-start.9 = (bf16[2,16,1,2,16,256]{5,4,3,2,1,0:T(8,128)(2,1)S(1)}, bf16[2,16,1,2,16,256]{5,4,3,2,1,0:T(8,128)(2,1)S(1)}, u32[]{:S(2)}, u32[]{:S(2)}) collective-permute-start(bf16[2,16,1,2,16,256]{5,4,3,2,1,0:T(8,128)(2,1)S(1)} %get-tuple-element.48), channel_id=1, source_target_pairs={{1,2},{3,4},{5,6},{2,1},{4,3},{6,5},{9,10},{11,12},{13,14},{10,9},... | collective-permute-start | bytes 1572872 | tf_op jit(solution)/shard_map/ppermute | solution.py:583
  27.8 25.1 %collective-permute-start.7 = (bf16[4,16,2,16,128]{4,3,2,1,0:T(8,128)(2,1)S(1)}, bf16[4,16,2,16,128]{4,3,2,1,0:T(8,128)(2,1)S(1)}, u32[]{:S(2)}, u32[]{:S(2)}) collective-permute-start(bf16[4,16,2,16,128]{4,3,2,1,0:T(8,128)(2,1)S(1)} %pack.7), channel_id=1, source_target_pairs={{1,2},{3,4},{5,6},{2,1},{4,3},{6,5},{9,10},{11,12},{13,14},{10,9},... | collective-permute-start | bytes 1572872 | tf_op jit(solution)/shard_map/ppermute | solution.py:584
  35.4 9.9 %copy-start.5 = (bf16[512,128]{1,0:T(8,128)(2,1)S(1)}, bf16[512,128]{1,0:T(8,128)(2,1)}, u32[]{:S(2)}) copy-start(bf16[512,128]{1,0:T(8,128)(2,1)} %constant.14.clone.along_x) | copy-start | bytes 393220
  35.4 13.5 %collective-permute-start.8 = (s16[50,16,128]{2,1,0:T(8,128)(2,1)S(1)}, s16[50,16,128]{2,1,0:T(8,128)(2,1)S(1)}, u32[]{:S(2)}, u32[]{:S(2)}) collective-permute-start(s16[50,16,128]{2,1,0:T(8,128)(2,1)S(1)} %get-tuple-element.46), channel_id=1, source_target_pairs={{0,16},{8,24},{16,0},{24,8},{1,17},{9,25},{17,1},{25,9},{2,18},{10... | collective-permute-start | bytes 614408 | tf_op jit(solution)/shard_map/edge_near/ppermute | solution.py:546
  44.6 8.3 %collective-permute-start.10 = (s16[25,16,128]{2,1,0:T(8,128)(2,1)S(1)}, s16[25,16,128]{2,1,0:T(8,128)(2,1)S(1)}, u32[]{:S(2)}, u32[]{:S(2)}) collective-permute-start(s16[25,16,128]{2,1,0:T(8,128)(2,1)S(1)} %get-tuple-element.50), channel_id=1, source_target_pairs={{0,16},{8,24},{16,0},{24,8},{1,17},{9,25},{17,1},{25,9},{2,18},{10... | collective-permute-start | bytes 307208 | tf_op jit(solution)/shard_map/edge_far/ppermute | solution.py:546
  48.9 4.0 %copy-start.4 = (bf16[2,2,256,128]{3,2,1,0:T(8,128)(2,1)S(1)}, bf16[2,2,256,128]{3,2,1,0:T(8,128)(2,1)}, u32[]{:S(2)}) copy-start(bf16[2,2,256,128]{3,2,1,0:T(8,128)(2,1)} %constant.17.clone.along_halo) | copy-start | bytes 786436
